TPU v7x, 32 devices: a whole 2x2x4 slice. The times are simulated.
32 devices in a mesh: groups: 2 (over y), tile: 4 (over z), win: 4 (over x, core).
Axes of the slice: x: 2, y: 2, z: 4, core: 2. Of those that a mesh axis runs over, the one named last changes fastest.
Arguments:
- phases: float32 [64, 4096, 512], P(('groups', 'win'), 'tile'), parts along dimension 0, may hold values from -3.140625 to 3.140625
- tile_blocks: int32 [4, 2], replicated, may hold values from 0 to 31, as said below
Outputs:
- correlations: float32 [8, 16, 16, 513], P(('groups', 'tile'), 'win'), parts along dimension 0
There are 2 independent parts, one for each index of `groups`. A program takes and returns all parts, laid end to end along the dimension named above; an argument that names none is the same for every part. Nothing has to cross between parts.
Inputs may be any that keep to these rules, and one draw needn't show every extreme that they name: `tile_blocks`: each row names two different channel blocks, the first smaller than the second; no two rows name the same pair.
All inputs are finite; a program needn't handle non-finite values.
Results may differ from a plain program's by a relative error of at most 0.0003.
Values sent between devices are 32-bit elements; how exact they have to be, the bound alone decides.
No kernel may reach another device: no remote copies, remote signals or barrier semaphores. Data moves between devices by JAX's collectives and lax.ppermute only.
A program may use at most 256 MiB of HBM per device.

v0:
```python
import math

import jax
import jax.numpy as jnp
from jax import lax
from jax.sharding import PartitionSpec as P

BLOCK = 16
HALF = 256


def tables_at(freq_index, bin_count, half_lags, windows):
    freq_index = freq_index[:, None]
    lag_index = jnp.arange(2 * half_lags + 1, dtype=jnp.int32)[None, :] - half_lags
    phase_turns = jnp.mod(freq_index * lag_index, 2 * bin_count).astype(jnp.float32)
    angles = phase_turns * jnp.float32(math.pi / bin_count)
    weight = jnp.where(freq_index == 0, 1.0, 2.0).astype(jnp.float32) / jnp.float32(
        math.sqrt(2.0 * windows * bin_count)
    )
    return (weight * jnp.cos(angles), -weight * jnp.sin(angles))


def cross_spectra(leading, trailing):
    cos_lead, sin_lead = (jnp.cos(leading), jnp.sin(leading))
    cos_trail, sin_trail = (jnp.cos(trailing), jnp.sin(trailing))
    highest = lax.Precision.HIGHEST
    cross_real = jnp.einsum("wfi,wfj->fij", cos_lead, cos_trail, precision=highest) + jnp.einsum(
        "wfi,wfj->fij", sin_lead, sin_trail, precision=highest
    )
    cross_imag = jnp.einsum("wfi,wfj->fij", sin_lead, cos_trail, precision=highest) - jnp.einsum(
        "wfi,wfj->fij", cos_lead, sin_trail, precision=highest
    )
    return (cross_real, cross_imag)


def to_lags(cross_real, cross_imag, cos_tab, sin_tab):
    bin_count, rows_a, rows_b = cross_real.shape
    dims = (((0,), (0,)), ((), ()))
    highest = lax.Precision.HIGHEST
    lagged = lax.dot_general(
        cross_real.reshape(bin_count, rows_a * rows_b), cos_tab, dims, precision=highest
    )
    lagged = lagged + lax.dot_general(
        cross_imag.reshape(bin_count, rows_a * rows_b), sin_tab, dims, precision=highest
    )
    return lagged.reshape(rows_a, rows_b, cos_tab.shape[1])


def on_device(phases, tile_blocks):
    tile_count = lax.axis_size("tile")
    win_count = lax.axis_size("win")
    win_local = phases.shape[0]
    bins_local = phases.shape[1]
    total_bins = bins_local * tile_count
    total_windows = win_local * win_count
    offsets = jnp.arange(BLOCK, dtype=jnp.int32)
    channels = (tile_blocks[:, :, None] * BLOCK + offsets[None, None, :]).reshape(
        tile_count * 2 * BLOCK
    )
    chosen = jnp.take(phases, channels, axis=2)
    quarter = bins_local // win_count
    received = lax.all_to_all(chosen, "tile", split_axis=2, concat_axis=1, tiled=True)
    shaped = received.reshape(win_local, tile_count, win_count, quarter, 2 * BLOCK)
    arrived = lax.all_to_all(shaped, "win", split_axis=2, concat_axis=0, tiled=True)
    arrived = arrived.reshape(total_windows, tile_count * quarter, 2 * BLOCK)
    source_index = jnp.arange(tile_count, dtype=jnp.int32)[:, None]
    inner_index = jnp.arange(quarter, dtype=jnp.int32)[None, :]
    freq_index = (
        source_index * bins_local + lax.axis_index("win") * quarter + inner_index
    ).reshape(tile_count * quarter)
    cos_tab, sin_tab = tables_at(freq_index, total_bins, HALF, total_windows)
    cross_real, cross_imag = cross_spectra(arrived[:, :, :BLOCK], arrived[:, :, BLOCK:])
    partial_lags = to_lags(cross_real, cross_imag, cos_tab, sin_tab)
    lagged = lax.psum_scatter(partial_lags, "win", scatter_dimension=0, tiled=True)
    return lagged[None]


def solution(mesh):
    placed = (P(("groups", "win"), "tile", None), P())
    return jax.shard_map(
        on_device,
        mesh=mesh,
        in_specs=placed,
        out_specs=P(("groups", "tile"), "win", None, None),
        check_vma=False,
    )
```

profile of v0, /device:TPU:0, one launch (start us, length us, event | category | flops | bytes accessed | tf_op | source)
XLA Modules:
  0.0 424.5 jit_solution(11590946940406617777)
XLA Ops:
  6.5 0.7 broadcast_multiply_fusion
  7.2 0.1 copy.14
  7.3 0.1 iota_add_fusion.1
  7.4 0.1 add.114
  7.5 0.1 add.111
  7.6 17.0 %copy.15 = f32[8,1024,512]{1,0,2:T(8,128)} copy(f32[8,1024,512]{2,1,0:T(8,128)} %param.2) | data formatting | bytes 33554432 | tf_op args[0]
  24.6 8.5 %gather_fusion = f32[128,8,1024]{2,1,0:T(8,128)} fusion(f32[8,1024,512]{1,0,2:T(8,128)} %copy.15, s32[1024]{0:T(1024)S(1)} %pad_clamp_fusion), kind=kCustom, calls=%fused_computation | custom fusion | bytes 8389120 | tf_op jit(solution)/shard_map/jit(_take)/gather | solution.py:60
  33.1 2.5 select_bitcast_fusion
  35.6 99.3 %all_to_all.30 = f32[8,1024,128]{1,0,2:T(8,128)S(1)} all-to-all(f32[8,1024,128]{1,0,2:T(8,128)S(1)} %select_bitcast_fusion), channel_id=1, replica_groups=mesh['groups'=2,'tile'=4,'win'=4] {'tile'}, dimensions={2} | all-to-all | bytes 8388608 | tf_op jit(solution)/shard_map/all_to_all | solution.py:62
  134.9 2.4 copy.16
  137.3 2.6 copy.29
  140.0 4.8 %all-to-all-start.1 = ((f32[8,4,4,256,32]{3,4,1,0,2:T(8,128)}), f32[8,4,4,256,32]{3,4,1,0,2:T(8,128)}, u32[]{:S(2)}, u32[]{:S(2)}) async-start(f32[8,4,4,256,32]{3,4,1,0,2:T(8,128)} %bitcast.33), calls=%async_computation.1 | async-start | bytes 8388608 | tf_op jit(solution)/shard_map/all_to_all | solution.py:64
  144.8 0.0 reduce-scatter.2.cloned.1.call-start
  144.9 0.1 add_bitcast_fusion
  145.0 48.1 %all-to-all-done.1 = f32[8,4,4,256,32]{3,4,1,0,2:T(8,128)} async-done(((f32[8,4,4,256,32]{3,4,1,0,2:T(8,128)}), f32[8,4,4,256,32]{3,4,1,0,2:T(8,128)}, u32[]{:S(2)}, u32[]{:S(2)}) %all-to-all-start.1) | async-done | bytes 4194336 | tf_op jit(solution)/shard_map/all_to_all | solution.py:64
  193.0 7.8 %copy.18 = f32[4,8,4,1,256,32]{4,2,5,1,0,3:T(4,128)} copy(f32[4,8,4,1,256,32]{4,5,2,1,0,3:T(8,128)} %bitcast.5) | data formatting | bytes 8388608 | tf_op jit(solution)/shard_map/all_to_all | solution.py:64
  200.8 6.0 %reshape.108 = f32[32,1024,32]{1,2,0:T(8,128)} reshape(f32[4,8,4,1,256,32]{4,2,5,1,0,3:T(4,128)} %copy.18) | data formatting | bytes 8388608 | tf_op jit(solution)/shard_map/reshape | solution.py:65
  206.8 4.0 fusion.28
  210.8 7.6 %copy.24 = f32[32,1024,16]{0,2,1:T(8,128)} copy(f32[32,1024,16]{1,2,0:T(8,128)} %get-tuple-element.10) | data formatting | bytes 4194304
  218.4 6.5 %copy.25 = f32[32,1024,16]{0,2,1:T(8,128)} copy(f32[32,1024,16]{1,2,0:T(8,128)S(1)} %get-tuple-element.9) | data formatting | bytes 4194304
  224.9 60.2 %fusion.26 = (f32[32,1024,16]{0,2,1:T(8,128)}, f32[32,1024,16]{0,2,1:T(8,128)S(1)}, f32[32,1024,16]{0,2,1:T(8,128)S(1)}, f32[32,1024,16]{0,2,1:T(8,128)}) fusion(f32[32,1024,16]{0,2,1:T(8,128)} %copy.25, f32[32,1024,16]{0,2,1:T(8,128)} %copy.24), kind=kLoop, calls=%fused_computation.42 | loop fusion | bytes 12582912 | tf_op jit(solution)/shard_map/sin | solution.py:25
  285.1 15.6 %fusion.30 = f32[1024,16,16]{2,1,0:T(8,128)} fusion(f32[32,1024,16]{0,2,1:T(8,128)S(1)} %get-tuple-element.13, f32[32,1024,16]{0,2,1:T(8,128)S(1)} %get-tuple-element.6), kind=kOutput, calls=%fused_computation.46 | convolution fusion | flops 100663296 | bytes 5242880 | tf_op jit(solution)/shard_map/wfi,wfj->fij/dot_general | solution.py:30
  300.7 17.9 %fusion.29 = f32[1024,16,16]{2,1,0:T(8,128)} fusion(f32[32,1024,16]{0,2,1:T(8,128)} %get-tuple-element.14, f32[32,1024,16]{0,2,1:T(8,128)S(1)} %get-tuple-element.6), kind=kOutput, calls=%fused_computation.45 | convolution fusion | flops 100663296 | bytes 5242880 | tf_op jit(solution)/shard_map/wfi,wfj->fij/dot_general | solution.py:27
  318.5 18.0 %convolution_subtract_fusion = f32[1024,16,16]{2,1,0:T(8,128)} fusion(f32[1024,16,16]{2,1,0:T(8,128)} %fusion.30, f32[32,1024,16]{0,2,1:T(8,128)S(1)} %copy-done.1, f32[32,1024,16]{0,2,1:T(8,128)} %get-tuple-element.5), kind=kOutput, calls=%fused_computation.8 | convolution fusion | flops 100925440 | bytes 6291456 | tf_op jit(solution)/shard_map/wfi,wfj->fij/dot_general | solution.py:30
  336.5 5.1 %copy.22 = f32[1024,16,16]{0,2,1:T(8,128)S(1)} copy(f32[1024,16,16]{2,1,0:T(8,128)} %convolution_subtract_fusion) | data formatting | bytes 2097152 | tf_op jit(solution)/shard_map/sub | solution.py:30
  341.7 20.5 %convolution_add_fusion = f32[1024,16,16]{2,1,0:T(8,128)} fusion(f32[1024,16,16]{2,1,0:T(8,128)} %fusion.29, f32[32,1024,16]{0,2,1:T(8,128)} %copy-done, f32[32,1024,16]{0,2,1:T(8,128)} %get-tuple-element.5), kind=kOutput, calls=%fused_computation.9 | convolution fusion | flops 100925440 | bytes 6291456 | tf_op jit(solution)/shard_map/wfi,wfj->fij/dot_general | solution.py:27
  362.1 5.3 %copy.21 = f32[1024,16,16]{0,2,1:T(8,128)S(1)} copy(f32[1024,16,16]{2,1,0:T(8,128)} %convolution_add_fusion) | data formatting | bytes 2097152 | tf_op jit(solution)/shard_map/add | solution.py:27
  367.5 13.8 %fusion.3 = f32[256,513]{0,1:T(8,128)S(1)} fusion(f32[1024,256]{0,1:T(8,128)S(1)} %bitcast.36, f32[1024]{0:T(1024)S(1)} %get-tuple-element.12, s32[513]{0:T(1024)S(1)} %iota_add_fusion, s32[1024]{0:T(1024)S(1)} %bitcast.39), kind=kOutput, calls=%fused_computation.13 | convolution fusion | flops 1621638144 | bytes 1584132 | tf_op jit(solution)/shard_map/dot_general | solution.py:43
  381.2 13.7 %fusion.13 = f32[256,513]{0,1:T(8,128)S(1)} fusion(f32[256,513]{0,1:T(8,128)S(1)} %fusion.3, f32[1024,256]{0,1:T(8,128)S(1)} %bitcast.37, s32[513]{0:T(1024)S(1)} %iota_add_fusion, s32[1024]{0:T(1024)S(1)} %bitcast.40, f32[1024]{0:T(1024)S(1)} %get-tuple-element.11), kind=kOutput, calls=%fused_computation.21 | convolution fusion | flops 1621769472 | bytes 2109444 | tf_op jit(solution)/shard_map/dot_general | solution.py:40
  395.0 1.1 copy.23
  396.0 0.0 reduce-scatter.2.cloned.1.call-update
  396.1 21.1 %reduce-scatter.2.cloned.1.call-done = f32[4,16,513]{2,1,0:T(8,128)} async-done(((f32[16,16,513]{2,1,0:T(8,128)}), f32[4,16,513]{2,1,0:T(8,128)}) %reduce-scatter.2.cloned.1.call-update) | async-done | bytes 131344 | tf_op jit(solution)/shard_map/reduce_scatter | solution.py:74
  (11 shorter events, 0.0 us)
Async XLA Ops:
  140.0 53.1 %all-to-all-start.1 = ((f32[8,4,4,256,32]{3,4,1,0,2:T(8,128)}), f32[8,4,4,256,32]{3,4,1,0,2:T(8,128)}, u32[]{:S(2)}, u32[]{:S(2)}) async-start(f32[8,4,4,256,32]{3,4,1,0,2:T(8,128)} %bitcast.33), calls=%async_computation.1 | async-start | bytes 8388608 | tf_op jit(solution)/shard_map/all_to_all | solution.py:64
  144.8 272.3 %reduce-scatter.2.cloned.1.call-start = ((), (), s32[]{:S(2)}) async-start(), calls=%async_computation.3 | async-start | bytes 819200 | tf_op jit(solution)/shard_map/reduce_scatter | solution.py:74
  285.1 15.6 %copy-start = (f32[32,1024,16]{0,2,1:T(8,128)}, f32[32,1024,16]{0,2,1:T(8,128)S(1)}, u32[]{:S(2)}) copy-start(f32[32,1024,16]{0,2,1:T(8,128)S(1)} %get-tuple-element.13) | copy-start | bytes 6291460
  300.7 17.9 %copy-start.1 = (f32[32,1024,16]{0,2,1:T(8,128)S(1)}, f32[32,1024,16]{0,2,1:T(8,128)}, u32[]{:S(2)}) copy-start(f32[32,1024,16]{0,2,1:T(8,128)} %get-tuple-element.14) | copy-start | bytes 6291460
Sparse Core Ops, SparseCore 0:
  396.2 20.8 reduce-scatter.1
where the time goes:
time: 431 us; the launch traced here: 424 us
  local copies, waits for them, and re-layouts  134 us (31%)
  matrix products  99.4 us (23%)
  blocking collectives  99.3 us (23%)
  waiting for transfers between devices  69.1 us (16%)
  between operations  14 us (3%)
  starting transfers between devices  4.87 us (1%)
    all_to_all x1, blocking collectives, on_device(): lax.all_to_all(chosen, 'tile', split_axis=2, concat_axis=1, tiled=True)  99.3 us
    sin x1, local copies, waits for them, and re-layouts, cross_spectra(): cos_trail, sin_trail = (jnp.cos(trailing), jnp.sin(trailing))  60.2 us
    all_to_all x1, waiting for transfers between devices, on_device(): lax.all_to_all(shaped, 'win', split_axis=2, concat_axis=0, tiled=True)  48.1 us
    unnamed x8, local copies, waits for them, and re-layouts  31.1 us
    reduce_scatter x1, waiting for transfers between devices, on_device(): lax.psum_scatter(partial_lags, 'win', scatter_dimension=0, tiled=True)  21.1 us
    dot_general x1, matrix products, cross_spectra(): jnp.einsum('wfi,wfj->fij', sin_lead, sin_trail, precision=highest)  20.5 us
    dot_general x1, matrix products, cross_spectra(): jnp.einsum('wfi,wfj->fij', cos_lead, sin_trail, precision=highest)  18 us
    dot_general x1, matrix products, cross_spectra(): jnp.einsum('wfi,wfj->fij', cos_lead, cos_trail, precision=highest)  17.9 us
  transfers between devices with their start and end apart: 2, of which 2 were waited for; matrix products, arithmetic and copies ran while one was open for 0% of the time, Pallas kernels for 0%

commit v1 on v0

--- a/solution.py
+++ b/solution.py
@@ -1,12 +1,237 @@
+import functools
 import math
 
 import jax
 import jax.numpy as jnp
+import numpy as np
 from jax import lax
+from jax.experimental import pallas as pl
+from jax.experimental.pallas import tpu as pltpu
 from jax.sharding import PartitionSpec as P
 
 BLOCK = 16
 HALF = 256
+LANES = 128
+TAB_ROWS = 272
+LAG_ROWS = 264
+SIN_FIT = (7.0710677816e-01, -2.9462767175e-02, 3.6827228729e-04, -2.1886110623e-06, 7.1958213082e-09)
+COS_FIT = (1.4142134963e+00, -1.7677635964e-01, 3.6825748950e-03, -3.0612567514e-05, 1.2790438412e-07)
+
+
+def lag_tables(total_bins, bins_local, windows):
+    bins = np.arange(total_bins, dtype=np.int64)
+    lags = np.arange(TAB_ROWS, dtype=np.int64)
+    angles = np.mod(lags[:, None] * bins[None, :], 2 * total_bins) * (math.pi / total_bins)
+    weight = np.where(bins == 0, 1.0, 2.0) / math.sqrt(2.0 * windows * total_bins)
+    out = []
+    for values in (weight * np.cos(angles), weight * np.sin(angles)):
+        values = values.astype(np.float32)
+        high = values.astype(jnp.bfloat16)
+        low = (values - high.astype(np.float32)).astype(jnp.bfloat16)
+        out.append(np.stack([high, low]))
+    table = np.stack(out)
+    table = table.reshape(2, 2, TAB_ROWS, total_bins // bins_local, bins_local)
+    return np.ascontiguousarray(np.moveaxis(table, 3, 0))
+
+
+def horner(coefs, z):
+    acc = z * coefs[-1] + coefs[-2]
+    for coef in coefs[-3::-1]:
+        acc = acc * z + coef
+    return acc
+
+
+def sin_cos(x):
+    z = x * x
+    t = x * horner(SIN_FIT, z)
+    q = horner(COS_FIT, z)
+    return t * q, 1.0 - t * t
+
+
+def lag_kernel(tiles, windows, columns_ref, slice_ref, *refs):
+    del columns_ref, slice_ref
+    cols = 2 * tiles
+    raw_refs = refs[:cols]
+    idx_ref, tab_ref, keep_ref, send_ref, plane_ref, hi_re, lo_re, hi_im, lo_im, acc_ref = refs[cols:]
+    step = pl.program_id(0)
+    chunk = raw_refs[0].shape[1]
+    per_vec = LANES // (cols * BLOCK)
+    lane = lax.broadcasted_iota(jnp.int32, (LANES, LANES), 1)
+    slots = [(w, m) for w in range(per_vec) for m in range(cols)]
+
+    @pl.when(step == 0)
+    def _():
+        acc_ref[...] = jnp.zeros_like(acc_ref)
+
+    for sub in range(chunk // LANES):
+        rows = pl.ds(sub * LANES, LANES)
+        for group in range(windows // per_vec):
+            packed = None
+            for slot, (w, m) in enumerate(slots):
+                raw = raw_refs[m][group * per_vec + w, rows, :]
+                index = jnp.broadcast_to(idx_ref[m : m + 1, :], (LANES, LANES))
+                moved = jnp.take_along_axis(raw, index, axis=1)
+                packed = moved if packed is None else jnp.where(lane >= slot * BLOCK, moved, packed)
+            sin, cos = sin_cos(packed.T)
+            both = cos + sin
+            diff = cos - sin
+            for slot, (w, m) in enumerate(slots):
+                part = slice(slot * BLOCK, (slot + 1) * BLOCK)
+                w_all = group * per_vec + w
+                if m % 2 == 0:
+                    three = (both[part], sin[part], cos[part])
+                else:
+                    three = (cos[part], diff[part], both[part])
+                for p in range(3):
+                    plane_ref[p, w_all, m * BLOCK : (m + 1) * BLOCK, :] = three[p]
+        for tile in range(tiles):
+            lead, trail = 2 * tile * BLOCK, (2 * tile + 1) * BLOCK
+            for quad in range(BLOCK // 4):
+                sums = [[None] * 3 for _ in range(4)]
+                for w in range(windows):
+                    right = [plane_ref[p, w, trail : trail + BLOCK, :] for p in range(3)]
+                    for i in range(4):
+                        row = lead + quad * 4 + i
+                        for p in range(3):
+                            left = plane_ref[p, w, row : row + 1, :]
+                            prod = left * right[p]
+                            sums[i][p] = prod if w == 0 else sums[i][p] + prod
+                for i in range(4):
+                    first = tile * BLOCK * BLOCK + (quad * 4 + i) * BLOCK
+                    where = (pl.ds(first, BLOCK), pl.ds(sub * LANES, LANES))
+                    real = sums[i][0] - sums[i][1]
+                    imag = sums[i][0] - sums[i][2]
+                    for value, hi, lo in ((real, hi_re, lo_re), (imag, hi_im, lo_im)):
+                        high = value.astype(jnp.bfloat16)
+                        hi[where] = high
+                        lo[where] = (value - high.astype(jnp.float32)).astype(jnp.bfloat16)
+
+    def product(table, spectra):
+        return lax.dot_general(
+            table, spectra, (((1,), (1,)), ((), ())), preferred_element_type=jnp.float32
+        )
+
+    pairs = BLOCK * BLOCK
+    for tile in range(tiles):
+        mine = pl.ds(tile * pairs, pairs)
+        for part, (hi, lo) in enumerate(((hi_re, lo_re), (hi_im, lo_im))):
+            tab_hi, tab_lo = tab_ref[part, 0], tab_ref[part, 1]
+            total = product(tab_hi, hi[mine, :]) + product(tab_lo, hi[mine, :])
+            total = total + product(tab_hi, lo[mine, :])
+            acc_ref[tile, part] += total
+
+    @pl.when(step == pl.num_programs(0) - 1)
+    def _():
+        half = LANES // 2
+        low_lanes = lax.broadcasted_iota(jnp.int32, (LAG_ROWS, LANES), 1) < half
+        for tile in range(tiles):
+            for core, ref in enumerate((keep_ref, send_ref)):
+                cut = (slice(0, LAG_ROWS), slice(core * LANES, (core + 1) * LANES))
+                even, odd = acc_ref[(tile, 0) + cut], acc_ref[(tile, 1) + cut]
+                ref[0, tile] = jnp.where(low_lanes, even, pltpu.roll(odd, half, 1))
+                ref[1, tile] = jnp.where(low_lanes, pltpu.roll(even, half, 1), odd)
+
+
+def partial_lags(phases, channels, table, slice_index, chunk):
+    windows, bins_local, _ = phases.shape
+    tiles = channels.shape[0]
+    cols = 2 * tiles
+    flat = channels.reshape(cols, BLOCK)
+    columns = flat[:, 0] // LANES
+    index = jnp.tile(flat % LANES, (1, LANES // BLOCK))
+    out = jax.ShapeDtypeStruct((2, tiles, LAG_ROWS, LANES), jnp.float32)
+    pairs = tiles * BLOCK * BLOCK
+    whole = pl.BlockSpec(out.shape, lambda i, c, s: (0, 0, 0, 0))
+
+    def raw_spec(m):
+        return pl.BlockSpec((windows, chunk, LANES), lambda i, c, s: (0, i, c[m]))
+
+    macs = tiles * bins_local * BLOCK * BLOCK * (windows * 4 + 6 * TAB_ROWS)
+    return pl.pallas_call(
+        functools.partial(lag_kernel, tiles, windows),
+        grid_spec=pltpu.PrefetchScalarGridSpec(
+            num_scalar_prefetch=2,
+            grid=(bins_local // chunk,),
+            in_specs=[raw_spec(m) for m in range(cols)]
+            + [
+                pl.BlockSpec((cols, LANES), lambda i, c, s: (0, 0)),
+                pl.BlockSpec((None, 2, 2, TAB_ROWS, chunk), lambda i, c, s: (s[0], 0, 0, 0, i)),
+            ],
+            out_specs=[whole, whole],
+            scratch_shapes=[pltpu.VMEM((3, windows, cols * BLOCK, LANES), jnp.float32)]
+            + [pltpu.VMEM((pairs, chunk), jnp.bfloat16)] * 4
+            + [pltpu.VMEM((tiles, 2, TAB_ROWS, BLOCK * BLOCK), jnp.float32)],
+        ),
+        out_shape=[out, out],
+        compiler_params=pltpu.CompilerParams(vmem_limit_bytes=48 * 2**20),
+        cost_estimate=pl.CostEstimate(
+            flops=2 * macs, bytes_accessed=4 * cols * windows * bins_local * LANES, transcendentals=0
+        ),
+        name="partial_lags",
+    )(columns, slice_index.reshape(1), *([phases] * cols), index, table)
+
+
+def finish_kernel(*refs):
+    out_ref = refs[-1]
+    total = refs[0][...]
+    for ref in refs[1:-1]:
+        total = total + ref[...]
+    half = LANES // 2
+    other = pltpu.roll(total, half, 1)
+    low_lanes = lax.broadcasted_iota(jnp.int32, total.shape, 1) < half
+    both = jnp.where(low_lanes, total - other, total + other)
+    rows, trailing = out_ref.shape[0], out_ref.shape[1]
+    mirror = LANES - 1 - lax.broadcasted_iota(jnp.int32, (half, LANES), 1)
+    for k in range(HALF // LANES):
+        ahead = both[k * LANES : (k + 1) * LANES, :].T[:half]
+        first = HALF + k * LANES
+        out_ref[:, :, first : first + LANES] = ahead.reshape(rows, trailing, LANES)
+        turned = both[k * LANES + 1 : (k + 1) * LANES + 1, :].T
+        behind = jnp.take_along_axis(turned[half:], mirror, axis=1)
+        first = HALF - (k + 1) * LANES
+        out_ref[:, :, first : first + LANES] = behind.reshape(rows, trailing, LANES)
+    last = turned[:half, LANES - 1 :]
+    out_ref[:, :, 2 * HALF :] = last.reshape(rows, trailing, 1)
+
+
+def finish(parts):
+    rows = BLOCK // 4
+    return pl.pallas_call(
+        finish_kernel,
+        out_shape=jax.ShapeDtypeStruct((rows, BLOCK, 2 * HALF + 1), jnp.float32),
+        name="finish",
+    )(*parts)
+
+
+def by_lags(groups, phases, tile_blocks):
+    tile_count = lax.axis_size("tile")
+    win_count = lax.axis_size("win")
+    windows, bins_local, _ = phases.shape
+    place = lax.axis_index("tile")
+    me = lax.axis_index("win")
+    chip, core = me // 2, me % 2
+    table = jnp.asarray(lag_tables(bins_local * tile_count, bins_local, windows * win_count))
+    quads = jnp.stack([2 * (chip ^ (r & 1)) + (core ^ (r >> 1)) for r in range(4)])
+    lead = (4 * quads[:, None] + jnp.arange(4, dtype=jnp.int32)[None, :]).reshape(BLOCK)
+    within = jnp.stack([lead, jnp.arange(BLOCK, dtype=jnp.int32)])
+
+    cross_core = [(w, w ^ 1) for w in range(win_count)]
+    cross_chip = [(w, w ^ 2) for w in range(win_count)]
+    parts = []
+    for group in groups:
+        blocks = jnp.stack([tile_blocks[place ^ m] for m in group])
+        channels = blocks[:, :, None] * BLOCK + within[None]
+        keep, send = partial_lags(phases, channels, table, place, 256)
+        came = lax.ppermute(send, "win", cross_core)
+        away = keep[1] + came[1]
+        mine = keep[0] + came[0]
+        mine = mine + lax.ppermute(away, "win", cross_chip)
+        for k, m in enumerate(group):
+            part = mine[k]
+            if m:
+                part = lax.ppermute(part, "tile", [(z, z ^ m) for z in range(tile_count)])
+            parts.append(part)
+    return finish(parts)[None]
 
 
 def tables_at(freq_index, bin_count, half_lags, windows):
@@ -46,7 +271,7 @@
     return lagged.reshape(rows_a, rows_b, cos_tab.shape[1])
 
 
-def on_device(phases, tile_blocks):
+def by_phases(phases, tile_blocks):
     tile_count = lax.axis_size("tile")
     win_count = lax.axis_size("win")
     win_local = phases.shape[0]
@@ -75,10 +300,28 @@
     return lagged[None]
 
 
+def on_device(groups, phases, tile_blocks):
+    tile_count = lax.axis_size("tile")
+    windows, bins_local, _ = phases.shape
+    lag_values = tile_count * BLOCK * BLOCK * (2 * HALF + 1)
+    phase_values = tile_count * 2 * BLOCK * windows * bins_local
+    fits = (
+        lax.axis_size("win") == 4
+        and tile_count & (tile_count - 1) == 0
+        and bins_local % 256 == 0
+        and windows % 8 == 0
+        and phases.shape[2] % LANES == 0
+    )
+    if fits and lag_values < phase_values:
+        return by_lags(groups, phases, tile_blocks)
+    return by_phases(phases, tile_blocks)
+
+
 def solution(mesh):
     placed = (P(("groups", "win"), "tile", None), P())
+    groups = [[m] for m in reversed(range(mesh.shape["tile"]))]
     return jax.shard_map(
-        on_device,
+        functools.partial(on_device, groups),
         mesh=mesh,
         in_specs=placed,
         out_specs=P(("groups", "tile"), "win", None, None),

time: 431 us -> 70.9 us (0.16); the launches traced: 424 us -> 70.8 us
  local copies, waits for them, and re-layouts: 134 us -> 1.54 us
  matrix products: 99.4 us -> 0 us
  blocking collectives: 99.3 us -> 0 us
  waiting for transfers between devices: 69.1 us -> 7.29 us
  Pallas kernels: 0 us -> 45 us
  between operations: 14 us -> 0.11 us
  starting transfers between devices: 4.87 us -> 14.8 us
    dot_general x6 -> x0, matrix products: 99.4 us -> none  [the longest x1 20.5 us: cross_spectra(): jnp.einsum('wfi,wfj->fij', sin_lead, sin_trail, precision=highest)]
    all_to_all x1 -> x0, blocking collectives: 99.3 us -> none  [on_device(): lax.all_to_all(chosen, 'tile', split_axis=2, concat_axis=1, tiled=True)]
    sin x1 -> x0, local copies, waits for them, and re-layouts: 60.2 us -> none  [cross_spectra(): cos_trail, sin_trail = (jnp.cos(trailing), jnp.sin(trailing))]
    all_to_all x1 -> x0, waiting for transfers between devices: 48.1 us -> none  [on_device(): lax.all_to_all(shaped, 'win', split_axis=2, concat_axis=0, tiled=True)]
    pallas_call x0 -> x5, Pallas kernels: none -> 45 us  [the longest x4 42.9 us: partial_lags(): pl.pallas_call(functools.partial(lag_kernel, tiles, windows), grid_spec=p...]
    unnamed x8 -> x6, local copies, waits for them, and re-layouts: 31.1 us -> 0.66 us
    reduce_scatter x1 -> x0, waiting for transfers between devices: 21.1 us -> none  [on_device(): lax.psum_scatter(partial_lags, 'win', scatter_dimension=0, tiled=True)]
    ppermute x0 -> x11, starting transfers between devices: none -> 14.8 us  [the longest x3 8.28 us: by_lags(): part = lax.ppermute(part, 'tile', [(z, z ^ m) for z in range(tile_count)])]
  transfers between devices with their start and end apart: 2 -> 11, of which waited for: 2 -> 4; matrix products, arithmetic and copies ran while one was open for 0% -> 2% of each run, Pallas kernels for 0% -> 45%
where the time goes in v1:
time: 70.9 us; the launch traced here: 70.8 us
  Pallas kernels  45 us (63%)
  starting transfers between devices  14.8 us (21%)
  waiting for transfers between devices  7.29 us (10%)
  other arithmetic  2.11 us (3%)
  local copies, waits for them, and re-layouts  1.54 us (2%)
    pallas_call x4, Pallas kernels, partial_lags(): pl.pallas_call(functools.partial(lag_kernel, tiles, windows), grid_spec=p...  42.9 us
    ppermute x3, starting transfers between devices, by_lags(): part = lax.ppermute(part, 'tile', [(z, z ^ m) for z in range(tile_count)])  8.28 us
    ppermute x4, starting transfers between devices, by_lags(): mine = mine + lax.ppermute(away, 'win', cross_chip)  5.25 us
    ppermute x3, waiting for transfers between devices, by_lags(): part = lax.ppermute(part, 'tile', [(z, z ^ m) for z in range(tile_count)])  4.5 us
    ppermute x4, waiting for transfers between devices, by_lags(): mine = mine + lax.ppermute(away, 'win', cross_chip)  2.79 us
    pallas_call x1, Pallas kernels, finish(): pl.pallas_call(finish_kernel, out_shape=jax.ShapeDtypeStruct((rows, BLOCK...  2.05 us
  transfers between devices with their start and end apart: 11, of which 4 were waited for; matrix products, arithmetic and copies ran while one was open for 2% of the time, Pallas kernels for 45%

profile of v1, /device:TPU:0, one launch (start us, length us, event | category | flops | bytes accessed | tf_op | source)
XLA Modules:
  0.0 70.8 jit_solution(5541822876689904063)
XLA Ops:
  0.2 0.1 add.289
  0.2 1.0 %multiply_reduce_fusion = (s32[2]{0:T(128)S(1)}, s32[2]{0:T(128)S(1)}, s32[2]{0:T(128)S(1)}, s32[2]{0:T(128)S(1)}) fusion(s32[4,2]{0,1:T(2,128)} %param.4, s32[]{:T(128)S(6)} %select_n.82, s32[]{:T(128)S(6)} %select_n.76, s32[]{:T(128)S(6)} %select_n.71, s32[]{:T(128)S(6)} %select_n.79), kind=kLoop, calls=%fused_computation.59 | loop fusion | flops 8 | bytes 80 | tf_op jit(solution)/shard_map/mul | solution.py:223
  1.3 0.1 and_select_fusion
  1.4 0.1 slice_reduce_fusion.2
  1.5 0.1 slice_reduce_fusion.3
  1.6 0.1 tile.17.refs_2_
  1.7 10.8 %partial_lags.4 = (f32[2,1,264,128]{3,2,1,0:T(8,128)S(1)}, f32[2,1,264,128]{3,2,1,0:T(8,128)S(1)}) custom-call(s32[2]{0:T(128)S(1)} %get-tuple-element.42.columns_ref, s32[1]{0:T(128)} %bitcast.4.slice_ref, f32[8,1024,512]{2,1,0:T(8,128)} %refs_1_.7, f32[8,1024,512]{2,1,0:T(8,128)} %refs_1_.7, s32[2,128]{1,0:T(2,128)S(1)} %tile.17.refs_2_, ...), custom_call_target="tpu_custom_call" | custom-call | flops 872415232 | bytes 8388608 | tf_op jit(solution)/shard_map/partial_lags/pallas_call | solution.py:150
  12.5 0.5 collective-permute-start
  13.0 0.1 slice_reduce_fusion
  13.1 0.1 slice_reduce_fusion.1
  13.3 10.7 %partial_lags.6 = (f32[2,1,264,128]{3,2,1,0:T(8,128)S(1)}, f32[2,1,264,128]{3,2,1,0:T(8,128)S(1)}) custom-call(s32[2]{0:T(128)S(1)} %get-tuple-element.40.columns_ref, s32[1]{0:T(128)} %bitcast.4.slice_ref, f32[8,1024,512]{2,1,0:T(8,128)} %refs_1_.7, f32[8,1024,512]{2,1,0:T(8,128)} %refs_1_.7, s32[2,128]{1,0:T(2,128)S(1)} %tile.41.refs_2_, ...), custom_call_target="tpu_custom_call" | custom-call | flops 872415232 | bytes 8388608 | tf_op jit(solution)/shard_map/partial_lags/pallas_call | solution.py:150
  24.1 0.1 collective-permute-start.6
  24.2 0.1 tile.19.refs_2_
  24.3 10.7 %partial_lags.5 = (f32[2,1,264,128]{3,2,1,0:T(8,128)S(1)}, f32[2,1,264,128]{3,2,1,0:T(8,128)S(1)}) custom-call(s32[2]{0:T(128)S(1)} %get-tuple-element.41.columns_ref, s32[1]{0:T(128)} %bitcast.4.slice_ref, f32[8,1024,512]{2,1,0:T(8,128)} %refs_1_.7, f32[8,1024,512]{2,1,0:T(8,128)} %refs_1_.7, s32[2,128]{1,0:T(2,128)S(1)} %tile.19.refs_2_, ...), custom_call_target="tpu_custom_call" | custom-call | flops 872415232 | bytes 8388608 | tf_op jit(solution)/shard_map/partial_lags/pallas_call | solution.py:150
  35.0 0.5 collective-permute-start.3
  35.5 0.1 tile.43.refs_2_
  35.6 10.7 %partial_lags.7 = (f32[2,1,264,128]{3,2,1,0:T(8,128)S(1)}, f32[2,1,264,128]{3,2,1,0:T(8,128)S(1)}) custom-call(s32[2]{0:T(128)S(1)} %get-tuple-element.39.columns_ref, s32[1]{0:T(128)} %bitcast.4.slice_ref, f32[8,1024,512]{2,1,0:T(8,128)} %refs_1_.7, f32[8,1024,512]{2,1,0:T(8,128)} %refs_1_.7, s32[2,128]{1,0:T(2,128)S(1)} %tile.43.refs_2_, ...), custom_call_target="tpu_custom_call" | custom-call | flops 872415232 | bytes 8388608 | tf_op jit(solution)/shard_map/partial_lags/pallas_call | solution.py:150
  46.3 0.1 collective-permute-start.9
  46.5 3.0 %collective-permute-start.1 = (f32[1,264,128]{2,1,0:T(8,128)S(1)}, f32[1,264,128]{2,1,0:T(8,128)S(1)}, u32[]{:S(2)}, u32[]{:S(2)}) collective-permute-start(f32[1,264,128]{2,1,0:T(8,128)S(1)} %fusion.12), channel_id=1, source_target_pairs={{0,2},{1,3},{2,0},{3,1},{4,6},{5,7},{6,4},{7,5},{8,10},{9,11},{10,... | collective-permute-start | bytes 405512 | tf_op jit(solution)/shard_map/ppermute | solution.py:228
  49.5 0.1 collective-permute-start.7
  49.6 2.1 %collective-permute-start.4 = (f32[1,264,128]{2,1,0:T(8,128)S(1)}, f32[1,264,128]{2,1,0:T(8,128)S(1)}, u32[]{:S(2)}, u32[]{:S(2)}) collective-permute-start(f32[1,264,128]{2,1,0:T(8,128)S(1)} %fusion.8), channel_id=1, source_target_pairs={{0,2},{1,3},{2,0},{3,1},{4,6},{5,7},{6,4},{7,5},{8,10},{9,11},{10,... | collective-permute-start | bytes 405512 | tf_op jit(solution)/shard_map/ppermute | solution.py:228
  51.7 0.1 collective-permute-start.10
  51.8 2.1 %collective-permute-done.1 = f32[1,264,128]{2,1,0:T(8,128)S(1)} collective-permute-done((f32[1,264,128]{2,1,0:T(8,128)S(1)}, f32[1,264,128]{2,1,0:T(8,128)S(1)}, u32[]{:S(2)}, u32[]{:S(2)}) %collective-permute-start.1) | collective-permute-done | bytes 135200 | tf_op jit(solution)/shard_map/ppermute | solution.py:228
  53.9 4.3 %collective-permute-start.2 = (f32[264,128]{1,0:T(8,128)S(1)}, f32[264,128]{1,0:T(8,128)S(1)}, u32[]{:S(2)}, u32[]{:S(2)}) collective-permute-start(f32[264,128]{1,0:T(8,128)S(1)} %fusion.15), channel_id=1, source_target_pairs={{0,12},{4,8},{8,4},{12,0},{1,13},{5,9},{9,5},{13,1},{2,14},{6,10},... | collective-permute-start | bytes 405512 | tf_op jit(solution)/shard_map/ppermute | solution.py:232
  58.2 0.7 %collective-permute-start.8 = (f32[264,128]{1,0:T(8,128)S(1)}, f32[264,128]{1,0:T(8,128)S(1)}, u32[]{:S(2)}, u32[]{:S(2)}) collective-permute-start(f32[264,128]{1,0:T(8,128)S(1)} %fusion.7), channel_id=1, source_target_pairs={{0,4},{4,0},{8,12},{12,8},{1,5},{5,1},{9,13},{13,9},{2,6},{6,2},{1... | collective-permute-start | bytes 405512 | tf_op jit(solution)/shard_map/ppermute | solution.py:232
  58.9 0.7 collective-permute-done.4
  59.7 3.3 %collective-permute-start.5 = (f32[264,128]{1,0:T(8,128)S(1)}, f32[264,128]{1,0:T(8,128)S(1)}, u32[]{:S(2)}, u32[]{:S(2)}) collective-permute-start(f32[264,128]{1,0:T(8,128)S(1)} %fusion.11), channel_id=1, source_target_pairs={{0,8},{4,12},{8,0},{12,4},{1,9},{5,13},{9,1},{13,5},{2,10},{6,14},... | collective-permute-start | bytes 405512 | tf_op jit(solution)/shard_map/ppermute | solution.py:232
  62.9 0.7 fusion.3.refs_3_
  63.6 1.6 %collective-permute-done.8.refs_2_ = f32[264,128]{1,0:T(8,128)S(1)} collective-permute-done((f32[264,128]{1,0:T(8,128)S(1)}, f32[264,128]{1,0:T(8,128)S(1)}, u32[]{:S(2)}, u32[]{:S(2)}) %collective-permute-start.8) | collective-permute-done | bytes 135200 | tf_op jit(solution)/shard_map/ppermute | solution.py:232
  65.2 2.9 %collective-permute-done.5.refs_1_ = f32[264,128]{1,0:T(8,128)S(1)} collective-permute-done((f32[264,128]{1,0:T(8,128)S(1)}, f32[264,128]{1,0:T(8,128)S(1)}, u32[]{:S(2)}, u32[]{:S(2)}) %collective-permute-start.5) | collective-permute-done | bytes 135200 | tf_op jit(solution)/shard_map/ppermute | solution.py:232
  68.1 0.6 copy-done.2
  68.8 2.1 %finish.1 = f32[4,16,513]{2,1,0:T(8,128)} custom-call(f32[264,128]{1,0:T(8,128)} %copy-done, f32[264,128]{1,0:T(8,128)} %copy-done.2, f32[264,128]{1,0:T(8,128)} %copy-done.1, f32[264,128]{1,0:T(8,128)} %fusion.3.refs_3_), custom_call_target="tpu_custom_call" | custom-call | tf_op jit(solution)/shard_map/finish/pallas_call | solution.py:199
  (29 shorter events, 0.4 us)
Async XLA Ops:
  12.5 34.0 %collective-permute-start = (f32[2,1,264,128]{3,2,1,0:T(8,128)S(1)}, f32[2,1,264,128]{3,2,1,0:T(8,128)S(1)}, u32[]{:S(2)}, u32[]{:S(2)}) collective-permute-start(f32[2,1,264,128]{3,2,1,0:T(8,128)S(1)} %get-tuple-element.14), channel_id=1, source_target_pairs={{0,1},{1,0},{2,3},{3,2},{4,5},{5,4},{6,7},{7,6},{8,9},{9,8},{10,11... | collective-permute-start | bytes 811016 | tf_op jit(solution)/shard_map/ppermute | solution.py:225
  24.1 25.4 %collective-permute-start.6 = (f32[2,1,264,128]{3,2,1,0:T(8,128)S(1)}, f32[2,1,264,128]{3,2,1,0:T(8,128)S(1)}, u32[]{:S(2)}, u32[]{:S(2)}) collective-permute-start(f32[2,1,264,128]{3,2,1,0:T(8,128)S(1)} %get-tuple-element.18), channel_id=1, source_target_pairs={{0,1},{1,0},{2,3},{3,2},{4,5},{5,4},{6,7},{7,6},{8,9},{9,8},{10,11... | collective-permute-start | bytes 811016 | tf_op jit(solution)/shard_map/ppermute | solution.py:225
  35.0 14.6 %collective-permute-start.3 = (f32[2,1,264,128]{3,2,1,0:T(8,128)S(1)}, f32[2,1,264,128]{3,2,1,0:T(8,128)S(1)}, u32[]{:S(2)}, u32[]{:S(2)}) collective-permute-start(f32[2,1,264,128]{3,2,1,0:T(8,128)S(1)} %get-tuple-element.16), channel_id=1, source_target_pairs={{0,1},{1,0},{2,3},{3,2},{4,5},{5,4},{6,7},{7,6},{8,9},{9,8},{10,11... | collective-permute-start | bytes 811016 | tf_op jit(solution)/shard_map/ppermute | solution.py:225
  46.3 5.3 %collective-permute-start.9 = (f32[2,1,264,128]{3,2,1,0:T(8,128)S(1)}, f32[2,1,264,128]{3,2,1,0:T(8,128)S(1)}, u32[]{:S(2)}, u32[]{:S(2)}) collective-permute-start(f32[2,1,264,128]{3,2,1,0:T(8,128)S(1)} %get-tuple-element.20), channel_id=1, source_target_pairs={{0,1},{1,0},{2,3},{3,2},{4,5},{5,4},{6,7},{7,6},{8,9},{9,8},{10,11... | collective-permute-start | bytes 811016 | tf_op jit(solution)/shard_map/ppermute | solution.py:225
  46.5 7.4 %collective-permute-start.1 = (f32[1,264,128]{2,1,0:T(8,128)S(1)}, f32[1,264,128]{2,1,0:T(8,128)S(1)}, u32[]{:S(2)}, u32[]{:S(2)}) collective-permute-start(f32[1,264,128]{2,1,0:T(8,128)S(1)} %fusion.12), channel_id=1, source_target_pairs={{0,2},{1,3},{2,0},{3,1},{4,6},{5,7},{6,4},{7,5},{8,10},{9,11},{10,... | collective-permute-start | bytes 405512 | tf_op jit(solution)/shard_map/ppermute | solution.py:228
  49.5 8.7 %collective-permute-start.7 = (f32[1,264,128]{2,1,0:T(8,128)S(1)}, f32[1,264,128]{2,1,0:T(8,128)S(1)}, u32[]{:S(2)}, u32[]{:S(2)}) collective-permute-start(f32[1,264,128]{2,1,0:T(8,128)S(1)} %fusion.4), channel_id=1, source_target_pairs={{0,2},{1,3},{2,0},{3,1},{4,6},{5,7},{6,4},{7,5},{8,10},{9,11},{10,... | collective-permute-start | bytes 405512 | tf_op jit(solution)/shard_map/ppermute | solution.py:228
  49.6 10.0 %collective-permute-start.4 = (f32[1,264,128]{2,1,0:T(8,128)S(1)}, f32[1,264,128]{2,1,0:T(8,128)S(1)}, u32[]{:S(2)}, u32[]{:S(2)}) collective-permute-start(f32[1,264,128]{2,1,0:T(8,128)S(1)} %fusion.8), channel_id=1, source_target_pairs={{0,2},{1,3},{2,0},{3,1},{4,6},{5,7},{6,4},{7,5},{8,10},{9,11},{10,... | collective-permute-start | bytes 405512 | tf_op jit(solution)/shard_map/ppermute | solution.py:228
  51.7 11.2 %collective-permute-start.10 = (f32[1,264,128]{2,1,0:T(8,128)S(1)}, f32[1,264,128]{2,1,0:T(8,128)S(1)}, u32[]{:S(2)}, u32[]{:S(2)}) collective-permute-start(f32[1,264,128]{2,1,0:T(8,128)S(1)} %fusion), channel_id=1, source_target_pairs={{0,2},{1,3},{2,0},{3,1},{4,6},{5,7},{6,4},{7,5},{8,10},{9,11},{10,... | collective-permute-start | bytes 405512 | tf_op jit(solution)/shard_map/ppermute | solution.py:228
  53.9 9.7 %collective-permute-start.2 = (f32[264,128]{1,0:T(8,128)S(1)}, f32[264,128]{1,0:T(8,128)S(1)}, u32[]{:S(2)}, u32[]{:S(2)}) collective-permute-start(f32[264,128]{1,0:T(8,128)S(1)} %fusion.15), channel_id=1, source_target_pairs={{0,12},{4,8},{8,4},{12,0},{1,13},{5,9},{9,5},{13,1},{2,14},{6,10},... | collective-permute-start | bytes 405512 | tf_op jit(solution)/shard_map/ppermute | solution.py:232
  58.2 7.0 %collective-permute-start.8 = (f32[264,128]{1,0:T(8,128)S(1)}, f32[264,128]{1,0:T(8,128)S(1)}, u32[]{:S(2)}, u32[]{:S(2)}) collective-permute-start(f32[264,128]{1,0:T(8,128)S(1)} %fusion.7), channel_id=1, source_target_pairs={{0,4},{4,0},{8,12},{12,8},{1,5},{5,1},{9,13},{13,9},{2,6},{6,2},{1... | collective-permute-start | bytes 405512 | tf_op jit(solution)/shard_map/ppermute | solution.py:232
  59.7 8.4 %collective-permute-start.5 = (f32[264,128]{1,0:T(8,128)S(1)}, f32[264,128]{1,0:T(8,128)S(1)}, u32[]{:S(2)}, u32[]{:S(2)}) collective-permute-start(f32[264,128]{1,0:T(8,128)S(1)} %fusion.11), channel_id=1, source_target_pairs={{0,8},{4,12},{8,0},{12,4},{1,9},{5,13},{9,1},{13,5},{2,10},{6,14},... | collective-permute-start | bytes 405512 | tf_op jit(solution)/shard_map/ppermute | solution.py:232
  63.6 4.5 %copy-start = (f32[264,128]{1,0:T(8,128)}, f32[264,128]{1,0:T(8,128)S(1)}, u32[]{:S(2)}) copy-start(f32[264,128]{1,0:T(8,128)S(1)} %collective-permute-done.2.refs_0_) | copy-start | bytes 405508
  65.2 2.9 %copy-start.1 = (f32[264,128]{1,0:T(8,128)}, f32[264,128]{1,0:T(8,128)S(1)}, u32[]{:S(2)}) copy-start(f32[264,128]{1,0:T(8,128)S(1)} %collective-permute-done.8.refs_2_) | copy-start | bytes 405508
  68.1 0.7 copy-start.2

commit v2 on v1

--- a/solution.py
+++ b/solution.py
@@ -48,80 +48,115 @@
     return t * q, 1.0 - t * t
 
 
-def lag_kernel(tiles, windows, columns_ref, slice_ref, *refs):
-    del columns_ref, slice_ref
+def lag_kernel(group, windows, place_ref, blocks_ref, *refs):
+    tiles = len(group)
     cols = 2 * tiles
     raw_refs = refs[:cols]
-    idx_ref, tab_ref, keep_ref, send_ref, plane_ref, hi_re, lo_re, hi_im, lo_im, acc_ref = refs[cols:]
+    tab_ref, keep_ref, send_ref = refs[cols : cols + 3]
+    planes = refs[cols + 3 : cols + 5]
+    spectra = refs[cols + 5 : cols + 7]
+    acc_ref = refs[cols + 7]
     step = pl.program_id(0)
-    chunk = raw_refs[0].shape[1]
+    last = pl.num_programs(0) - 1
+    pairs = BLOCK * BLOCK
     per_vec = LANES // (cols * BLOCK)
     lane = lax.broadcasted_iota(jnp.int32, (LANES, LANES), 1)
     slots = [(w, m) for w in range(per_vec) for m in range(cols)]
 
-    @pl.when(step == 0)
-    def _():
-        acc_ref[...] = jnp.zeros_like(acc_ref)
-
-    for sub in range(chunk // LANES):
-        rows = pl.ds(sub * LANES, LANES)
-        for group in range(windows // per_vec):
+    def lane_index(m):
+        at = lane[:8] % BLOCK
+        if m % 2 == 0:
+            chip, core = place_ref[1] // 2, place_ref[1] % 2
+            turned = ((at // 8) ^ core) * 4 + (((at // 4) % 2) ^ chip) * 8
+            at = turned + at % 4
+        block = blocks_ref[place_ref[0] ^ group[m // 2], m % 2]
+        row = at + (block % (LANES // BLOCK)) * BLOCK
+        return jnp.tile(row, (LANES // 8, 1))
+
+    def front(unit):
+        index = [lane_index(m) for m in range(cols)]
+
+        def one(group_index):
             packed = None
             for slot, (w, m) in enumerate(slots):
-                raw = raw_refs[m][group * per_vec + w, rows, :]
-                index = jnp.broadcast_to(idx_ref[m : m + 1, :], (LANES, LANES))
-                moved = jnp.take_along_axis(raw, index, axis=1)
+                rows = pl.ds(unit * LANES, LANES)
+                raw = raw_refs[m][group_index * per_vec + w, rows, :]
+                moved = jnp.take_along_axis(raw, index[m], axis=1)
                 packed = moved if packed is None else jnp.where(lane >= slot * BLOCK, moved, packed)
             sin, cos = sin_cos(packed.T)
             both = cos + sin
             diff = cos - sin
             for slot, (w, m) in enumerate(slots):
                 part = slice(slot * BLOCK, (slot + 1) * BLOCK)
-                w_all = group * per_vec + w
-                if m % 2 == 0:
-                    three = (both[part], sin[part], cos[part])
-                else:
-                    three = (cos[part], diff[part], both[part])
+                three = (both, sin, cos) if m % 2 == 0 else (cos, diff, both)
                 for p in range(3):
-                    plane_ref[p, w_all, m * BLOCK : (m + 1) * BLOCK, :] = three[p]
-        for tile in range(tiles):
+                    where = (p, group_index * per_vec + w, slice(m * BLOCK, (m + 1) * BLOCK))
+                    planes[unit][where] = three[p][part]
+
+        return [functools.partial(one, g) for g in range(windows // per_vec)]
+
+    def cross(unit):
+        def one(tile, quad):
             lead, trail = 2 * tile * BLOCK, (2 * tile + 1) * BLOCK
-            for quad in range(BLOCK // 4):
-                sums = [[None] * 3 for _ in range(4)]
-                for w in range(windows):
-                    right = [plane_ref[p, w, trail : trail + BLOCK, :] for p in range(3)]
+            sums = [[None] * 3 for _ in range(4)]
+            for w in range(windows):
+                for p in range(3):
+                    right = planes[unit][p, w, trail : trail + BLOCK, :]
                     for i in range(4):
                         row = lead + quad * 4 + i
-                        for p in range(3):
-                            left = plane_ref[p, w, row : row + 1, :]
-                            prod = left * right[p]
-                            sums[i][p] = prod if w == 0 else sums[i][p] + prod
-                for i in range(4):
-                    first = tile * BLOCK * BLOCK + (quad * 4 + i) * BLOCK
-                    where = (pl.ds(first, BLOCK), pl.ds(sub * LANES, LANES))
-                    real = sums[i][0] - sums[i][1]
-                    imag = sums[i][0] - sums[i][2]
-                    for value, hi, lo in ((real, hi_re, lo_re), (imag, hi_im, lo_im)):
-                        high = value.astype(jnp.bfloat16)
-                        hi[where] = high
-                        lo[where] = (value - high.astype(jnp.float32)).astype(jnp.bfloat16)
-
-    def product(table, spectra):
-        return lax.dot_general(
-            table, spectra, (((1,), (1,)), ((), ())), preferred_element_type=jnp.float32
-        )
-
-    pairs = BLOCK * BLOCK
-    for tile in range(tiles):
-        mine = pl.ds(tile * pairs, pairs)
-        for part, (hi, lo) in enumerate(((hi_re, lo_re), (hi_im, lo_im))):
-            tab_hi, tab_lo = tab_ref[part, 0], tab_ref[part, 1]
-            total = product(tab_hi, hi[mine, :]) + product(tab_lo, hi[mine, :])
-            total = total + product(tab_hi, lo[mine, :])
-            acc_ref[tile, part] += total
-
-    @pl.when(step == pl.num_programs(0) - 1)
+                        prod = planes[unit][p, w, row : row + 1, :] * right
+                        sums[i][p] = prod if w == 0 else sums[i][p] + prod
+            for i in range(4):
+                first = (quad * 4 + i) * BLOCK
+                for part in range(2):
+                    value = sums[i][0] - sums[i][1 + part]
+                    high = value.astype(jnp.bfloat16)
+                    low = (value - high.astype(jnp.float32)).astype(jnp.bfloat16)
+                    spectra[unit][tile, part, first : first + BLOCK, :LANES] = high
+                    spectra[unit][tile, part, first : first + BLOCK, LANES:] = low
+
+        return [functools.partial(one, t, q) for t in range(tiles) for q in range(BLOCK // 4)]
+
+    def lags(unit):
+        def product(table, values):
+            return lax.dot_general(
+                table, values, (((1,), (1,)), ((), ())), preferred_element_type=jnp.float32
+            )
+
+        def one(tile, part):
+            bins = slice(unit * LANES, (unit + 1) * LANES)
+            high, low = tab_ref[part, 0, :, bins], tab_ref[part, 1, :, bins]
+            values = spectra[unit][tile, part]
+            total = product(jnp.concatenate([high, high], axis=1), values)
+            acc_ref[tile, part] += total + product(low, values[:, :LANES])
+
+        return [functools.partial(one, t, part) for t in range(tiles) for part in range(2)]
+
+    def run(*stages):
+        pieces = []
+        for stage in stages:
+            pieces += [((k + 0.5) / len(stage), n, piece) for k, (n, piece) in enumerate(zip(range(99), stage))]
+        for _, _, piece in sorted(pieces, key=lambda entry: entry[:2]):
+            piece()
+
+    @pl.when(step == 0)
     def _():
+        acc_ref[...] = jnp.zeros_like(acc_ref)
+        spectra[1][...] = jnp.zeros_like(spectra[1])
+        run(front(0))
+
+    @pl.when((step > 0) & (step < last))
+    def _():
+        run(front(0), cross(1), lags(0))
+
+    @pl.when(step < last)
+    def _():
+        run(front(1), cross(0), lags(1))
+
+    @pl.when(step == last)
+    def _():
+        run(cross(1), lags(0))
+        run(lags(1))
         half = LANES // 2
         low_lanes = lax.broadcasted_iota(jnp.int32, (LAG_ROWS, LANES), 1) < half
         for tile in range(tiles):
@@ -132,43 +167,46 @@
                 ref[1, tile] = jnp.where(low_lanes, pltpu.roll(even, half, 1), odd)
 
 
-def partial_lags(phases, channels, table, slice_index, chunk):
+def partial_lags(group, phases, tile_blocks, table, place):
     windows, bins_local, _ = phases.shape
-    tiles = channels.shape[0]
+    tiles = len(group)
     cols = 2 * tiles
-    flat = channels.reshape(cols, BLOCK)
-    columns = flat[:, 0] // LANES
-    index = jnp.tile(flat % LANES, (1, LANES // BLOCK))
+    chunk = 2 * LANES
+    steps = bins_local // chunk
+    pairs = BLOCK * BLOCK
+    per_lane_tile = LANES // BLOCK
     out = jax.ShapeDtypeStruct((2, tiles, LAG_ROWS, LANES), jnp.float32)
-    pairs = tiles * BLOCK * BLOCK
-    whole = pl.BlockSpec(out.shape, lambda i, c, s: (0, 0, 0, 0))
+    whole = pl.BlockSpec(out.shape, lambda i, p, b: (0, 0, 0, 0))
 
     def raw_spec(m):
-        return pl.BlockSpec((windows, chunk, LANES), lambda i, c, s: (0, i, c[m]))
-
-    macs = tiles * bins_local * BLOCK * BLOCK * (windows * 4 + 6 * TAB_ROWS)
+        def where(i, p, b):
+            return 0, jnp.minimum(i, steps - 1), b[p[0] ^ group[m // 2], m % 2] // per_lane_tile
+
+        return pl.BlockSpec((windows, chunk, LANES), where)
+
+    def table_at(i, p, b):
+        return p[0], 0, 0, 0, jnp.maximum(i - 1, 0)
+
+    macs = tiles * bins_local * pairs * (windows * 4 + 6 * TAB_ROWS)
     return pl.pallas_call(
-        functools.partial(lag_kernel, tiles, windows),
+        functools.partial(lag_kernel, group, windows),
         grid_spec=pltpu.PrefetchScalarGridSpec(
             num_scalar_prefetch=2,
-            grid=(bins_local // chunk,),
+            grid=(steps + 1,),
             in_specs=[raw_spec(m) for m in range(cols)]
-            + [
-                pl.BlockSpec((cols, LANES), lambda i, c, s: (0, 0)),
-                pl.BlockSpec((None, 2, 2, TAB_ROWS, chunk), lambda i, c, s: (s[0], 0, 0, 0, i)),
-            ],
+            + [pl.BlockSpec((None, 2, 2, TAB_ROWS, chunk), table_at)],
             out_specs=[whole, whole],
-            scratch_shapes=[pltpu.VMEM((3, windows, cols * BLOCK, LANES), jnp.float32)]
-            + [pltpu.VMEM((pairs, chunk), jnp.bfloat16)] * 4
-            + [pltpu.VMEM((tiles, 2, TAB_ROWS, BLOCK * BLOCK), jnp.float32)],
+            scratch_shapes=[pltpu.VMEM((3, windows, cols * BLOCK, LANES), jnp.float32)] * 2
+            + [pltpu.VMEM((tiles, 2, pairs, 2 * LANES), jnp.bfloat16)] * 2
+            + [pltpu.VMEM((tiles, 2, TAB_ROWS, pairs), jnp.float32)],
         ),
         out_shape=[out, out],
-        compiler_params=pltpu.CompilerParams(vmem_limit_bytes=48 * 2**20),
+        compiler_params=pltpu.CompilerParams(vmem_limit_bytes=40 * 2**20),
         cost_estimate=pl.CostEstimate(
             flops=2 * macs, bytes_accessed=4 * cols * windows * bins_local * LANES, transcendentals=0
         ),
         name="partial_lags",
-    )(columns, slice_index.reshape(1), *([phases] * cols), index, table)
+    )(place, tile_blocks, *([phases] * cols), table)
 
 
 def finish_kernel(*refs):
@@ -207,21 +245,13 @@
     tile_count = lax.axis_size("tile")
     win_count = lax.axis_size("win")
     windows, bins_local, _ = phases.shape
-    place = lax.axis_index("tile")
-    me = lax.axis_index("win")
-    chip, core = me // 2, me % 2
+    place = jnp.stack([lax.axis_index("tile"), lax.axis_index("win")])
     table = jnp.asarray(lag_tables(bins_local * tile_count, bins_local, windows * win_count))
-    quads = jnp.stack([2 * (chip ^ (r & 1)) + (core ^ (r >> 1)) for r in range(4)])
-    lead = (4 * quads[:, None] + jnp.arange(4, dtype=jnp.int32)[None, :]).reshape(BLOCK)
-    within = jnp.stack([lead, jnp.arange(BLOCK, dtype=jnp.int32)])
-
     cross_core = [(w, w ^ 1) for w in range(win_count)]
     cross_chip = [(w, w ^ 2) for w in range(win_count)]
     parts = []
     for group in groups:
-        blocks = jnp.stack([tile_blocks[place ^ m] for m in group])
-        channels = blocks[:, :, None] * BLOCK + within[None]
-        keep, send = partial_lags(phases, channels, table, place, 256)
+        keep, send = partial_lags(group, phases, tile_blocks, table, place)
         came = lax.ppermute(send, "win", cross_core)
         away = keep[1] + came[1]
         mine = keep[0] + came[0]
@@ -319,7 +349,8 @@
 
 def solution(mesh):
     placed = (P(("groups", "win"), "tile", None), P())
-    groups = [[m] for m in reversed(range(mesh.shape["tile"]))]
+    order = list(reversed(range(mesh.shape["tile"])))
+    groups = [order[k : k + 2] for k in range(0, len(order), 2)]
     return jax.shard_map(
         functools.partial(on_device, groups),
         mesh=mesh,

time: 70.9 us -> 66.6 us (0.939)
  Pallas kernels: 45 us -> 31.9 us
  waiting for transfers between devices: 7.29 us -> 16.6 us
  local copies, waits for them, and re-layouts: 1.54 us -> 5.69 us
  starting transfers between devices: 14.8 us -> 11.6 us
  other arithmetic: 2.11 us -> 0.24 us
    pallas_call x4 -> x2, Pallas kernels: 42.9 us -> 29.8 us  [partial_lags(): pl.pallas_call(functools.partial(lag_kernel, group, windows), grid_spec=p...]
    ppermute x4 -> x2, waiting for transfers between devices: 2.79 us -> 8.02 us  [by_lags(): mine = mine + lax.ppermute(away, 'win', cross_chip)]
    unnamed x6 -> x9, local copies, waits for them, and re-layouts: 0.66 us -> 4.99 us
    ppermute x3, waiting for transfers between devices: 4.5 us -> 8.59 us  [by_lags(): part = lax.ppermute(part, 'tile', [(z, z ^ m) for z in range(tile_count)])]
    ppermute x3, starting transfers between devices: 8.28 us -> 6.38 us  [by_lags(): part = lax.ppermute(part, 'tile', [(z, z ^ m) for z in range(tile_count)])]
    mul x2 -> x0, other arithmetic: 1.12 us -> none  [the longest x1 1.04 us: by_lags(): channels = blocks[:, :, None] * BLOCK + within[None]]
    squeeze x4 -> x0, other arithmetic: 0.74 us -> none  [by_lags(): part = mine[k]]
    ppermute x4 -> x2, starting transfers between devices: 5.25 us -> 4.54 us  [by_lags(): mine = mine + lax.ppermute(away, 'win', cross_chip)]
  transfers between devices with their start and end apart: 11 -> 7, of which waited for: 4 -> 3; matrix products, arithmetic and copies ran while one was open for 2% -> 1% of each run, Pallas kernels for 45% -> 23%
where the time goes in v2:
time: 66.6 us; the launch traced here: 66 us
  Pallas kernels  31.9 us (48%)
  waiting for transfers between devices  16.6 us (25%)
  starting transfers between devices  11.6 us (17%)
  local copies, waits for them, and re-layouts  5.69 us (9%)
    pallas_call x2, Pallas kernels, partial_lags(): pl.pallas_call(functools.partial(lag_kernel, group, windows), grid_spec=p...  29.8 us
    ppermute x3, waiting for transfers between devices, by_lags(): part = lax.ppermute(part, 'tile', [(z, z ^ m) for z in range(tile_count)])  8.59 us
    ppermute x2, waiting for transfers between devices, by_lags(): mine = mine + lax.ppermute(away, 'win', cross_chip)  8.02 us
    ppermute x3, starting transfers between devices, by_lags(): part = lax.ppermute(part, 'tile', [(z, z ^ m) for z in range(tile_count)])  6.38 us
    unnamed x9, local copies, waits for them, and re-layouts  4.99 us
    ppermute x2, starting transfers between devices, by_lags(): mine = mine + lax.ppermute(away, 'win', cross_chip)  4.54 us
    pallas_call x1, Pallas kernels, finish(): pl.pallas_call(finish_kernel, out_shape=jax.ShapeDtypeStruct((rows, BLOCK...  2.05 us
  transfers between devices with their start and end apart: 7, of which 3 were waited for; matrix products, arithmetic and copies ran while one was open for 1% of the time, Pallas kernels for 23%

profile of v2, /device:TPU:0, one launch (start us, length us, event | category | flops | bytes accessed | tf_op | source)
XLA Modules:
  0.0 66.0 jit_solution(3397675834071058157)
XLA Ops:
  0.0 0.8 %copy.4.blocks_ref = s32[4,2]{1,0:T(4,128)S(1)} copy(s32[4,2]{0,1:T(2,128)} %param.4) | data formatting | bytes 64 | tf_op args[1]
  0.8 0.1 pad_add_fusion.place_ref
  0.8 0.0 copy-start
  0.8 3.5 %copy-done = bf16[4,2,2,272,1024]{4,3,2,1,0:T(8,128)(2,1)S(1)} copy-done((bf16[4,2,2,272,1024]{4,3,2,1,0:T(8,128)(2,1)S(1)}, bf16[4,2,2,272,1024]{4,3,2,1,0:T(8,128)(2,1)}, u32[]{:S(2)}) %copy-start) | copy-done | bytes 8912920
  4.4 14.9 %partial_lags.3 = (f32[2,2,264,128]{3,2,1,0:T(8,128)S(1)}, f32[2,2,264,128]{3,2,1,0:T(8,128)S(1)}) custom-call(s32[2]{0:T(128)S(1)} %pad_add_fusion.place_ref, s32[4,2]{1,0:T(4,128)S(1)} %copy.4.blocks_ref, f32[8,1024,512]{2,1,0:T(8,128)} %refs_3_.3, f32[8,1024,512]{2,1,0:T(8,128)} %refs_3_.3, f32[8,1024,512]{2,1,0:T(8,128)} %refs_3_.3, ...), custom_call_target="tpu_custom_call" | custom-call | flops 1744830464 | bytes 16777216 | tf_op jit(solution)/shard_map/partial_lags/pallas_call | solution.py:191
  19.3 0.5 collective-permute-start.4
  19.8 14.9 %partial_lags.2 = (f32[2,2,264,128]{3,2,1,0:T(8,128)S(1)}, f32[2,2,264,128]{3,2,1,0:T(8,128)S(1)}) custom-call(s32[2]{0:T(128)S(1)} %pad_add_fusion.place_ref, s32[4,2]{1,0:T(4,128)S(1)} %copy.4.blocks_ref, f32[8,1024,512]{2,1,0:T(8,128)} %refs_3_.3, f32[8,1024,512]{2,1,0:T(8,128)} %refs_3_.3, f32[8,1024,512]{2,1,0:T(8,128)} %refs_3_.3, ...), custom_call_target="tpu_custom_call" | custom-call | flops 1744830464 | bytes 16777216 | tf_op jit(solution)/shard_map/partial_lags/pallas_call | solution.py:191
  34.7 0.1 collective-permute-start
  34.9 0.0 collective-permute-done.4
  34.9 3.0 %collective-permute-start.5 = (f32[2,264,128]{2,1,0:T(8,128)S(1)}, f32[2,264,128]{2,1,0:T(8,128)S(1)}, u32[]{:S(2)}, u32[]{:S(2)}) collective-permute-start(f32[2,264,128]{2,1,0:T(8,128)S(1)} %fusion), channel_id=1, source_target_pairs={{0,2},{1,3},{2,0},{3,1},{4,6},{5,7},{6,4},{7,5},{8,10},{9,11},{10,... | collective-permute-start | bytes 811016 | tf_op jit(solution)/shard_map/ppermute | solution.py:258
  37.9 0.0 collective-permute-done
  37.9 1.5 %collective-permute-start.1 = (f32[2,264,128]{2,1,0:T(8,128)S(1)}, f32[2,264,128]{2,1,0:T(8,128)S(1)}, u32[]{:S(2)}, u32[]{:S(2)}) collective-permute-start(f32[2,264,128]{2,1,0:T(8,128)S(1)} %fusion.3), channel_id=1, source_target_pairs={{0,2},{1,3},{2,0},{3,1},{4,6},{5,7},{6,4},{7,5},{8,10},{9,11},{10,... | collective-permute-start | bytes 811016 | tf_op jit(solution)/shard_map/ppermute | solution.py:258
  39.5 5.7 %collective-permute-done.5 = f32[2,264,128]{2,1,0:T(8,128)S(1)} collective-permute-done((f32[2,264,128]{2,1,0:T(8,128)S(1)}, f32[2,264,128]{2,1,0:T(8,128)S(1)}, u32[]{:S(2)}, u32[]{:S(2)}) %collective-permute-start.5) | collective-permute-done | bytes 270368 | tf_op jit(solution)/shard_map/ppermute | solution.py:258
  45.2 0.1 fusion.2
  45.2 0.7 %slice_bitcast_fusion = (f32[264,128]{1,0:T(8,128)}, f32[264,128]{1,0:T(8,128)S(1)}) fusion(f32[2,264,128]{2,1,0:T(8,128)S(1)} %fusion.2), kind=kLoop, calls=%fused_computation.10 | loop fusion | bytes 540672 | tf_op jit(solution)/shard_map/squeeze | solution.py:260
  45.9 2.1 %collective-permute-start.6 = (f32[264,128]{1,0:T(8,128)S(1)}, f32[264,128]{1,0:T(8,128)S(1)}, u32[]{:S(2)}, u32[]{:S(2)}) collective-permute-start(f32[264,128]{1,0:T(8,128)S(1)} %get-tuple-element.14), channel_id=1, source_target_pairs={{0,4},{4,0},{8,12},{12,8},{1,5},{5,1},{9,13},{13,9},{2,6},{6,2},{1... | collective-permute-start | bytes 405512 | tf_op jit(solution)/shard_map/ppermute | solution.py:262
  48.0 2.3 %collective-permute-done.1 = f32[2,264,128]{2,1,0:T(8,128)S(1)} collective-permute-done((f32[2,264,128]{2,1,0:T(8,128)S(1)}, f32[2,264,128]{2,1,0:T(8,128)S(1)}, u32[]{:S(2)}, u32[]{:S(2)}) %collective-permute-start.1) | collective-permute-done | bytes 270368 | tf_op jit(solution)/shard_map/ppermute | solution.py:258
  50.4 2.9 %collective-permute-start.3 = (f32[264,128]{1,0:T(8,128)S(1)}, f32[264,128]{1,0:T(8,128)S(1)}, u32[]{:S(2)}, u32[]{:S(2)}) collective-permute-start(f32[264,128]{1,0:T(8,128)S(1)} %get-tuple-element.15), channel_id=1, source_target_pairs={{0,8},{4,12},{8,0},{12,4},{1,9},{5,13},{9,1},{13,5},{2,10},{6,14},... | collective-permute-start | bytes 405512 | tf_op jit(solution)/shard_map/ppermute | solution.py:262
  53.3 1.3 %collective-permute-start.2 = (f32[264,128]{1,0:T(8,128)S(1)}, f32[264,128]{1,0:T(8,128)S(1)}, u32[]{:S(2)}, u32[]{:S(2)}) collective-permute-start(f32[264,128]{1,0:T(8,128)S(1)} %get-tuple-element.16), channel_id=1, source_target_pairs={{0,12},{4,8},{8,4},{12,0},{1,13},{5,9},{9,5},{13,1},{2,14},{6,10},... | collective-permute-start | bytes 405512 | tf_op jit(solution)/shard_map/ppermute | solution.py:262
  54.7 0.0 collective-permute-done.6.refs_2_
  54.7 0.0 copy-start.1
  54.7 8.6 %collective-permute-done.3.refs_1_ = f32[264,128]{1,0:T(8,128)S(1)} collective-permute-done((f32[264,128]{1,0:T(8,128)S(1)}, f32[264,128]{1,0:T(8,128)S(1)}, u32[]{:S(2)}, u32[]{:S(2)}) %collective-permute-start.3) | collective-permute-done | bytes 135200 | tf_op jit(solution)/shard_map/ppermute | solution.py:262
  63.3 0.0 copy-start.2
  63.3 0.0 collective-permute-done.2.refs_0_
  63.3 0.0 copy-start.3
  63.3 0.0 copy-done.1
  63.3 0.6 copy-done.2
  63.9 0.1 copy-done.3
  64.0 2.1 %finish.1 = f32[4,16,513]{2,1,0:T(8,128)} custom-call(f32[264,128]{1,0:T(8,128)} %copy-done.3, f32[264,128]{1,0:T(8,128)} %copy-done.2, f32[264,128]{1,0:T(8,128)} %copy-done.1, f32[264,128]{1,0:T(8,128)} %get-tuple-element.13.refs_3_), custom_call_target="tpu_custom_call" | custom-call | tf_op jit(solution)/shard_map/finish/pallas_call | solution.py:237
  (4 shorter events, 0.1 us)
Async XLA Ops:
  0.8 3.5 %copy-start = (bf16[4,2,2,272,1024]{4,3,2,1,0:T(8,128)(2,1)S(1)}, bf16[4,2,2,272,1024]{4,3,2,1,0:T(8,128)(2,1)}, u32[]{:S(2)}) copy-start(bf16[4,2,2,272,1024]{4,3,2,1,0:T(8,128)(2,1)} %constant.9.clone.refs_4_) | copy-start | bytes 26738692
  19.3 15.6 %collective-permute-start.4 = (f32[2,2,264,128]{3,2,1,0:T(8,128)S(1)}, f32[2,2,264,128]{3,2,1,0:T(8,128)S(1)}, u32[]{:S(2)}, u32[]{:S(2)}) collective-permute-start(f32[2,2,264,128]{3,2,1,0:T(8,128)S(1)} %get-tuple-element.12), channel_id=1, source_target_pairs={{0,1},{1,0},{2,3},{3,2},{4,5},{5,4},{6,7},{7,6},{8,9},{9,8},{10,11... | collective-permute-start | bytes 1622024 | tf_op jit(solution)/shard_map/ppermute | solution.py:255
  34.7 3.2 %collective-permute-start = (f32[2,2,264,128]{3,2,1,0:T(8,128)S(1)}, f32[2,2,264,128]{3,2,1,0:T(8,128)S(1)}, u32[]{:S(2)}, u32[]{:S(2)}) collective-permute-start(f32[2,2,264,128]{3,2,1,0:T(8,128)S(1)} %get-tuple-element.10), channel_id=1, source_target_pairs={{0,1},{1,0},{2,3},{3,2},{4,5},{5,4},{6,7},{7,6},{8,9},{9,8},{10,11... | collective-permute-start | bytes 1622024 | tf_op jit(solution)/shard_map/ppermute | solution.py:255
  34.9 10.3 %collective-permute-start.5 = (f32[2,264,128]{2,1,0:T(8,128)S(1)}, f32[2,264,128]{2,1,0:T(8,128)S(1)}, u32[]{:S(2)}, u32[]{:S(2)}) collective-permute-start(f32[2,264,128]{2,1,0:T(8,128)S(1)} %fusion), channel_id=1, source_target_pairs={{0,2},{1,3},{2,0},{3,1},{4,6},{5,7},{6,4},{7,5},{8,10},{9,11},{10,... | collective-permute-start | bytes 811016 | tf_op jit(solution)/shard_map/ppermute | solution.py:258
  37.9 12.4 %collective-permute-start.1 = (f32[2,264,128]{2,1,0:T(8,128)S(1)}, f32[2,264,128]{2,1,0:T(8,128)S(1)}, u32[]{:S(2)}, u32[]{:S(2)}) collective-permute-start(f32[2,264,128]{2,1,0:T(8,128)S(1)} %fusion.3), channel_id=1, source_target_pairs={{0,2},{1,3},{2,0},{3,1},{4,6},{5,7},{6,4},{7,5},{8,10},{9,11},{10,... | collective-permute-start | bytes 811016 | tf_op jit(solution)/shard_map/ppermute | solution.py:258
  45.9 8.8 %collective-permute-start.6 = (f32[264,128]{1,0:T(8,128)S(1)}, f32[264,128]{1,0:T(8,128)S(1)}, u32[]{:S(2)}, u32[]{:S(2)}) collective-permute-start(f32[264,128]{1,0:T(8,128)S(1)} %get-tuple-element.14), channel_id=1, source_target_pairs={{0,4},{4,0},{8,12},{12,8},{1,5},{5,1},{9,13},{13,9},{2,6},{6,2},{1... | collective-permute-start | bytes 405512 | tf_op jit(solution)/shard_map/ppermute | solution.py:262
  50.4 12.8 %collective-permute-start.3 = (f32[264,128]{1,0:T(8,128)S(1)}, f32[264,128]{1,0:T(8,128)S(1)}, u32[]{:S(2)}, u32[]{:S(2)}) collective-permute-start(f32[264,128]{1,0:T(8,128)S(1)} %get-tuple-element.15), channel_id=1, source_target_pairs={{0,8},{4,12},{8,0},{12,4},{1,9},{5,13},{9,1},{13,5},{2,10},{6,14},... | collective-permute-start | bytes 405512 | tf_op jit(solution)/shard_map/ppermute | solution.py:262
  53.3 9.9 %collective-permute-start.2 = (f32[264,128]{1,0:T(8,128)S(1)}, f32[264,128]{1,0:T(8,128)S(1)}, u32[]{:S(2)}, u32[]{:S(2)}) collective-permute-start(f32[264,128]{1,0:T(8,128)S(1)} %get-tuple-element.16), channel_id=1, source_target_pairs={{0,12},{4,8},{8,4},{12,0},{1,13},{5,9},{9,5},{13,1},{2,14},{6,10},... | collective-permute-start | bytes 405512 | tf_op jit(solution)/shard_map/ppermute | solution.py:262
  54.7 8.6 %copy-start.1 = (f32[264,128]{1,0:T(8,128)}, f32[264,128]{1,0:T(8,128)S(1)}, u32[]{:S(2)}) copy-start(f32[264,128]{1,0:T(8,128)S(1)} %collective-permute-done.6.refs_2_) | copy-start | bytes 405508
  63.3 0.7 copy-start.2
  63.3 0.7 %copy-start.3 = (f32[264,128]{1,0:T(8,128)}, f32[264,128]{1,0:T(8,128)S(1)}, u32[]{:S(2)}) copy-start(f32[264,128]{1,0:T(8,128)S(1)} %collective-permute-done.2.refs_0_) | copy-start | bytes 405508

commit v3 on v0

--- a/solution.py
+++ b/solution.py
@@ -1,12 +1,339 @@
+import functools
 import math
 
 import jax
 import jax.numpy as jnp
+import numpy as np
 from jax import lax
+from jax.experimental import pallas as pl
+from jax.experimental.pallas import tpu as pltpu
 from jax.sharding import PartitionSpec as P
 
 BLOCK = 16
 HALF = 256
+LANES = 128
+TAB_ROWS = 272
+FRONT_VMEM = 50 * 2**20
+LAG_VMEM = 50 * 2**20
+LAG_ROWS = 264
+SIN_FIT = (7.0710677816e-01, -2.9462767175e-02, 3.6827228729e-04, -2.1886110623e-06, 7.1958213082e-09)
+COS_FIT = (1.4142134963e+00, -1.7677635964e-01, 3.6825748950e-03, -3.0612567514e-05, 1.2790438412e-07)
+
+
+def lag_tables(total_bins, bins_local, windows):
+    bins = np.arange(total_bins, dtype=np.int64)
+    lags = np.arange(TAB_ROWS, dtype=np.int64)
+    angles = np.mod(lags[:, None] * bins[None, :], 2 * total_bins) * (math.pi / total_bins)
+    weight = np.where(bins == 0, 1.0, 2.0) / math.sqrt(2.0 * windows * total_bins)
+    out = []
+    for values in (weight * np.cos(angles), weight * np.sin(angles)):
+        values = values.astype(np.float32)
+        high = values.astype(jnp.bfloat16)
+        low = (values - high.astype(np.float32)).astype(jnp.bfloat16)
+        out.append(np.stack([high, low]))
+    table = np.stack(out)
+    table = table.reshape(2, 2, TAB_ROWS, total_bins // bins_local, bins_local)
+    return np.ascontiguousarray(np.moveaxis(table, 3, 0))
+
+
+def horner(coefs, z):
+    acc = z * coefs[-1] + coefs[-2]
+    for coef in coefs[-3::-1]:
+        acc = acc * z + coef
+    return acc
+
+
+def sin_cos(x):
+    z = x * x
+    t = x * horner(SIN_FIT, z)
+    q = horner(COS_FIT, z)
+    return t * q, 1.0 - t * t
+
+
+def front_kernel(tiles, ids_ref, phases_ref, tables_ref, out_ref, tab_ref, *refs):
+    raw_ref, stage_ref, packed, turned = refs[0], refs[1], refs[2:4], refs[4:6]
+    raw_sem, stage_sem, tab_sem = refs[6:]
+    table_copy = pltpu.make_async_copy(tables_ref.at[ids_ref[0]], tab_ref, tab_sem)
+    windows, bins_local, channels = raw_ref.shape
+    units = bins_local // LANES
+    per_lane_tile = LANES // BLOCK
+
+    def raw_copy(unit):
+        bins = pl.ds(unit * LANES, LANES)
+        return pltpu.make_async_copy(phases_ref.at[:, bins, :], raw_ref.at[:, bins, :], raw_sem.at[unit])
+
+    for unit in range(units):
+        raw_copy(unit).start()
+    table_copy.start()
+
+    def stage_copy(unit):
+        slot = unit % 2
+        return pltpu.make_async_copy(stage_ref.at[slot], out_ref.at[:, unit], stage_sem.at[slot])
+
+    lane = lax.broadcasted_iota(jnp.int32, (8, LANES), 1)
+    at, col = lane % BLOCK, lane // BLOCK
+    chip, core = ids_ref[1] // 2, ids_ref[1] % 2
+    lead = ((at // 8) ^ core) * 4 + (((at // 4) % 2) ^ chip) * 8 + at % 4
+    block = jnp.zeros_like(lane)
+    for m in range(2 * tiles):
+        block = jnp.where(col == m, ids_ref[2 + 2 * (ids_ref[0] ^ (m // 2)) + m % 2], block)
+    row = jnp.where(col % 2 == 0, lead, at) + (block % per_lane_tile) * BLOCK
+    row = jnp.tile(row, (BLOCK // 8, 1))
+    source = jnp.tile(block // per_lane_tile, (BLOCK // 8, 1))
+
+    def gather(item, to, piece):
+        unit, w = item // windows, item % windows
+        first = pl.multiple_of(unit * LANES + piece * BLOCK, BLOCK)
+        value = None
+        for q in range(channels // LANES):
+            raw = raw_ref[w, pl.ds(first, BLOCK), q * LANES : (q + 1) * LANES]
+            moved = jnp.take_along_axis(raw, row, axis=1)
+            value = moved if value is None else jnp.where(source == q, moved, value)
+        to[piece * BLOCK : (piece + 1) * BLOCK] = value
+
+    def unfold(item, rows_ref, m):
+        unit, w = item // windows, item % windows
+        sin, cos = sin_cos(rows_ref[m * BLOCK : (m + 1) * BLOCK])
+        stage_ref[unit % 2, m // 2, 0, w, m % 2] = cos
+        stage_ref[unit % 2, m // 2, 1, w, m % 2] = sin
+
+    pieces = range(LANES // BLOCK)
+    raw_copy(0).wait()
+    for piece in pieces:
+        gather(0, packed[1], piece)
+    turned[0][...] = packed[1][...].T
+    for piece in pieces:
+        gather(1, packed[0], piece)
+
+    @pl.loop(0, units)
+    def _(unit):
+        @pl.when(unit + 1 < units)
+        def _():
+            raw_copy(unit + 1).wait()
+
+        @pl.when(unit >= 2)
+        def _():
+            stage_copy(unit - 2).wait()
+
+        @pl.loop(0, windows // 4)
+        def _(h):
+            for j in range(4):
+                item = unit * windows + 4 * h + j
+                here, there = j % 2, 1 - j % 2
+                turned[there][...] = packed[here][...].T
+                for piece in pieces:
+                    gather(jnp.minimum(item + 2, units * windows - 1), packed[there], piece)
+                    unfold(item, turned[here], piece)
+
+        stage_copy(unit).start()
+
+    table_copy.wait()
+    for unit in range(units - 2, units):
+        stage_copy(unit).wait()
+
+
+def waves_of(phases, ids, tables, tiles):
+    windows, bins_local, channels = phases.shape
+    table = jax.ShapeDtypeStruct(tables.shape[1:], tables.dtype)
+    out = jax.ShapeDtypeStruct((tiles, bins_local // LANES, 2, windows, 2, BLOCK, LANES), jnp.float32)
+    smem, vmem = pl.BlockSpec(memory_space=pltpu.SMEM), pl.BlockSpec(memory_space=pltpu.VMEM)
+    return pl.pallas_call(
+        functools.partial(front_kernel, tiles),
+        in_specs=[smem] + [pl.BlockSpec(memory_space=pl.ANY)] * 2,
+        out_specs=[pl.BlockSpec(memory_space=pl.ANY), vmem],
+        out_shape=[out, table],
+        scratch_shapes=[
+            pltpu.VMEM(phases.shape, jnp.float32),
+            pltpu.VMEM((2, tiles) + out.shape[2:], jnp.float32),
+        ]
+        + [pltpu.VMEM((LANES, LANES), jnp.float32)] * 4
+        + [pltpu.SemaphoreType.DMA((k,)) for k in (bins_local // LANES, 2)]
+        + [pltpu.SemaphoreType.DMA],
+        compiler_params=pltpu.CompilerParams(vmem_limit_bytes=FRONT_VMEM),
+        cost_estimate=pl.CostEstimate(flops=10**10, bytes_accessed=phases.size * 4, transcendentals=0),
+        name="waves",
+    )(ids, phases, tables)
+
+
+def lag_kernel(m, after_ref, waves_ref, tab_ref, keep_ref, send_ref, wave_ref, acc_ref, plane_ref, *scratch):
+    del after_ref
+    spectra, wave_sem = scratch[:2], scratch[2]
+    units, _, windows = wave_ref.shape[:3]
+
+    def wave_copy(unit):
+        return pltpu.make_async_copy(waves_ref.at[m, unit], wave_ref.at[unit], wave_sem.at[unit])
+
+    for unit in range(units):
+        wave_copy(unit).start()
+
+    subs = spectra[0].shape[0]
+    chunks = units // subs
+
+    def prepare(unit):
+        for w in range(windows):
+            lead_cos, trail_cos = wave_ref[unit, 0, w, 0], wave_ref[unit, 0, w, 1]
+            lead_sin, trail_sin = wave_ref[unit, 1, w, 0], wave_ref[unit, 1, w, 1]
+            plane_ref[0, w, 0], plane_ref[1, w, 0], plane_ref[2, w, 0] = lead_cos + lead_sin, lead_sin, lead_cos
+            plane_ref[0, w, 1], plane_ref[1, w, 1] = trail_cos, trail_cos - trail_sin
+            plane_ref[2, w, 1] = trail_cos + trail_sin
+
+    def cross(sub, parity, quads):
+        for quad in quads:
+            sums = [[None] * 3 for _ in range(4)]
+            for w in range(windows):
+                for p in range(3):
+                    right = plane_ref[p, w, 1]
+                    for i in range(4):
+                        row = quad * 4 + i
+                        prod = plane_ref[p, w, 0, row : row + 1, :] * right
+                        sums[i][p] = prod if w == 0 else sums[i][p] + prod
+            for i in range(4):
+                rows = slice((quad * 4 + i) * BLOCK, (quad * 4 + i + 1) * BLOCK)
+                for part in range(2):
+                    value = sums[i][0] - sums[i][1 + part]
+                    high = value.astype(jnp.bfloat16)
+                    low = value - high.astype(jnp.float32)
+                    spectra[parity][sub, part, 0, rows] = high
+                    spectra[parity][sub, part, 1, rows] = low.astype(jnp.bfloat16)
+
+    def product(table, values):
+        return lax.dot_general(
+            table, values, (((1,), (1,)), ((), ())), preferred_element_type=jnp.float32
+        )
+
+    def lags(k, part, parity):
+        bins = pl.ds(pl.multiple_of(k * subs * LANES, subs * LANES), subs * LANES)
+        high, low = (
+            jnp.concatenate([spectra[parity][sub, part, half] for sub in range(subs)], axis=1)
+            for half in range(2)
+        )
+        tab_high, tab_low = tab_ref[part, 0, :, bins], tab_ref[part, 1, :, bins]
+        total = product(tab_high, high) + product(tab_low, high) + product(tab_high, low)
+        acc_ref[part] += total
+
+    acc_ref[...] = jnp.zeros_like(acc_ref)
+    spectra[1][...] = jnp.zeros_like(spectra[1])
+
+    @pl.loop(0, chunks // 2)
+    def _(k):
+        for parity in range(2):
+
+            @pl.loop(0, 2)
+            def _(g):
+                unit = (2 * k + parity) * subs + g
+                wave_copy(unit).wait()
+                prepare(unit)
+                cross(g, parity, (0, 1))
+                lags(jnp.maximum(2 * k + parity - 1, 0), g, 1 - parity)
+                cross(g, parity, (2, 3))
+
+    for part in range(2):
+        lags(chunks - 1, part, 1)
+    middle = LANES // 2
+    low_lanes = lax.broadcasted_iota(jnp.int32, (LAG_ROWS, LANES), 1) < middle
+    for core, ref in enumerate((keep_ref, send_ref)):
+        cut = (slice(0, LAG_ROWS), slice(core * LANES, (core + 1) * LANES))
+        even, odd = acc_ref[(0,) + cut], acc_ref[(1,) + cut]
+        ref[0] = jnp.where(low_lanes, even, pltpu.roll(odd, middle, 1))
+        ref[1] = jnp.where(low_lanes, pltpu.roll(even, middle, 1), odd)
+
+
+def partial_lags(m, waves, table, after):
+    pairs = BLOCK * BLOCK
+    planes = pltpu.VMEM((3,) + waves.shape[3:], jnp.float32)
+    out = jax.ShapeDtypeStruct((2, LAG_ROWS, LANES), jnp.float32)
+    vmem = pl.BlockSpec(memory_space=pltpu.VMEM)
+    return pl.pallas_call(
+        functools.partial(lag_kernel, m),
+        in_specs=[pl.BlockSpec(memory_space=pltpu.SMEM), pl.BlockSpec(memory_space=pl.ANY), vmem],
+        out_specs=[vmem, vmem],
+        out_shape=[out, out],
+        scratch_shapes=[
+            pltpu.VMEM(waves.shape[1:], jnp.float32),
+            pltpu.VMEM((2, TAB_ROWS, pairs), jnp.float32),
+            planes,
+        ]
+        + [pltpu.VMEM((2, 2, 2, pairs, LANES), jnp.bfloat16)] * 2
+        + [pltpu.SemaphoreType.DMA(waves.shape[1:2])],
+        compiler_params=pltpu.CompilerParams(vmem_limit_bytes=LAG_VMEM),
+        cost_estimate=pl.CostEstimate(flops=4 * 10**9, bytes_accessed=waves.size, transcendentals=0),
+        name="partial_lags",
+    )(after, waves, table)
+
+
+def finish_kernel(*refs):
+    out_ref = refs[-1]
+    total = refs[0][...]
+    for ref in refs[1:-1]:
+        total = total + ref[...]
+    half = LANES // 2
+    other = pltpu.roll(total, half, 1)
+    low_lanes = lax.broadcasted_iota(jnp.int32, total.shape, 1) < half
+    both = jnp.where(low_lanes, total - other, total + other)
+    rows, trailing = out_ref.shape[0], out_ref.shape[1]
+    mirror = LANES - 1 - lax.broadcasted_iota(jnp.int32, (half, LANES), 1)
+    for k in range(HALF // LANES):
+        ahead = both[k * LANES : (k + 1) * LANES, :].T[:half]
+        first = HALF + k * LANES
+        out_ref[:, :, first : first + LANES] = ahead.reshape(rows, trailing, LANES)
+        turned = both[k * LANES + 1 : (k + 1) * LANES + 1, :].T
+        behind = jnp.take_along_axis(turned[half:], mirror, axis=1)
+        first = HALF - (k + 1) * LANES
+        out_ref[:, :, first : first + LANES] = behind.reshape(rows, trailing, LANES)
+    last = turned[:half, LANES - 1 :]
+    out_ref[:, :, 2 * HALF :] = last.reshape(rows, trailing, 1)
+
+
+def finish(parts):
+    rows = BLOCK // 4
+    return pl.pallas_call(
+        finish_kernel,
+        out_shape=jax.ShapeDtypeStruct((rows, BLOCK, 2 * HALF + 1), jnp.float32),
+        name="finish",
+    )(*parts)
+
+
+def by_lags(phases, tile_blocks):
+    tile_count = lax.axis_size("tile")
+    win_count = lax.axis_size("win")
+    windows, bins_local, _ = phases.shape
+    place = jnp.stack([lax.axis_index("tile"), lax.axis_index("win")])
+    ids = jnp.concatenate([place, tile_blocks.reshape(-1)])
+    tables = jnp.asarray(lag_tables(bins_local * tile_count, bins_local, windows * win_count))
+    cross_core = [(w, w ^ 1) for w in range(win_count)]
+    cross_chip = [(w, w ^ 2) for w in range(win_count)]
+    waves, table = waves_of(phases, ids, tables, tile_count)
+    after = ids[:1]
+    keep, came, away, part = {}, {}, {}, {}
+
+    def over_core(m):
+        keep[m], send = partial_lags(m, waves, table, after)
+        came[m] = lax.ppermute(send, "win", cross_core)
+
+    def over_chip(m):
+        part[m] = keep[m][0] + came[m][0] + lax.ppermute(away[m], "win", cross_chip)
+
+    def over_tile(m):
+        part[m] = lax.ppermute(part[m], "tile", [(z, z ^ m) for z in range(tile_count)])
+
+    over_core(3)
+    over_core(2)
+    away[3] = keep[3][1] + came[3][1]
+    after, away[3] = lax.optimization_barrier((after, away[3]))
+    over_chip(3)
+    over_core(1)
+    away[2] = keep[2][1] + came[2][1]
+    after, away[2], part[3] = lax.optimization_barrier((after, away[2], part[3]))
+    over_chip(2)
+    over_tile(3)
+    over_core(0)
+    over_tile(2)
+    for m in (1, 0):
+        away[m] = keep[m][1] + came[m][1]
+        over_chip(m)
+    over_tile(1)
+    parts = [part[m] for m in (3, 2, 1, 0)]
+    return finish(parts)[None]
 
 
 def tables_at(freq_index, bin_count, half_lags, windows):
@@ -46,7 +373,7 @@
     return lagged.reshape(rows_a, rows_b, cos_tab.shape[1])
 
 
-def on_device(phases, tile_blocks):
+def by_phases(phases, tile_blocks):
     tile_count = lax.axis_size("tile")
     win_count = lax.axis_size("win")
     win_local = phases.shape[0]
@@ -75,6 +402,23 @@
     return lagged[None]
 
 
+def on_device(phases, tile_blocks):
+    tile_count = lax.axis_size("tile")
+    windows, bins_local, _ = phases.shape
+    lag_values = tile_count * BLOCK * BLOCK * (2 * HALF + 1)
+    phase_values = tile_count * 2 * BLOCK * windows * bins_local
+    fits = (
+        lax.axis_size("win") == 4
+        and tile_count * 2 * BLOCK == LANES
+        and bins_local % (4 * LANES) == 0
+        and windows % 4 == 0
+        and phases.shape[2] % LANES == 0
+    )
+    if fits and lag_values < phase_values:
+        return by_lags(phases, tile_blocks)
+    return by_phases(phases, tile_blocks)
+
+
 def solution(mesh):
     placed = (P(("groups", "win"), "tile", None), P())
     return jax.shard_map(

time: 431 us -> 59.3 us (0.14); the launches traced: 424 us -> 59.1 us
  local copies, waits for them, and re-layouts: 134 us -> 1.51 us
  matrix products: 99.4 us -> 0 us
  blocking collectives: 99.3 us -> 0 us
  waiting for transfers between devices: 69.1 us -> 7.01 us
  Pallas kernels: 0 us -> 37.6 us
  between operations: 14 us -> 0.15 us
  starting transfers between devices: 4.87 us -> 11.9 us
    dot_general x6 -> x0, matrix products: 99.4 us -> none  [the longest x1 20.5 us: cross_spectra(): jnp.einsum('wfi,wfj->fij', sin_lead, sin_trail, precision=highest)]
    all_to_all x1 -> x0, blocking collectives: 99.3 us -> none  [on_device(): lax.all_to_all(chosen, 'tile', split_axis=2, concat_axis=1, tiled=True)]
    sin x1 -> x0, local copies, waits for them, and re-layouts: 60.2 us -> none  [cross_spectra(): cos_trail, sin_trail = (jnp.cos(trailing), jnp.sin(trailing))]
    all_to_all x1 -> x0, waiting for transfers between devices: 48.1 us -> none  [on_device(): lax.all_to_all(shaped, 'win', split_axis=2, concat_axis=0, tiled=True)]
    pallas_call x0 -> x6, Pallas kernels: none -> 37.6 us  [the longest x4 22.3 us: partial_lags(): pl.pallas_call(functools.partial(lag_kernel, m), in_specs=[pl.BlockSpec(m...]
    unnamed x8 -> x7, local copies, waits for them, and re-layouts: 31.1 us -> 1.42 us
    reduce_scatter x1 -> x0, waiting for transfers between devices: 21.1 us -> none  [on_device(): lax.psum_scatter(partial_lags, 'win', scatter_dimension=0, tiled=True)]
    ppermute x0 -> x11, starting transfers between devices: none -> 11.9 us  [the longest x4 6.47 us: over_chip(): part[m] = keep[m][0] + came[m][0] + lax.ppermute(away[m], 'win', cross_chip)]
  transfers between devices with their start and end apart: 2 -> 11, of which waited for: 2 -> 3; matrix products, arithmetic and copies ran while one was open for 0% -> 1% of each run, Pallas kernels for 0% -> 28%
where the time goes in v3:
time: 59.3 us; the launch traced here: 59.1 us
  Pallas kernels  37.6 us (63%)
  starting transfers between devices  11.9 us (20%)
  waiting for transfers between devices  7.01 us (12%)
  local copies, waits for them, and re-layouts  1.51 us (3%)
  other arithmetic  0.89 us (2%)
    pallas_call x4, Pallas kernels, partial_lags(): pl.pallas_call(functools.partial(lag_kernel, m), in_specs=[pl.BlockSpec(m...  22.3 us
    pallas_call x1, Pallas kernels, waves_of(): pl.pallas_call(functools.partial(front_kernel, tiles), in_specs=[smem] +...  13.2 us
    ppermute x4, starting transfers between devices, over_chip(): part[m] = keep[m][0] + came[m][0] + lax.ppermute(away[m], 'win', cross_chip)  6.47 us
    ppermute x4, waiting for transfers between devices, over_chip(): part[m] = keep[m][0] + came[m][0] + lax.ppermute(away[m], 'win', cross_chip)  5.03 us
    ppermute x3, starting transfers between devices, over_tile(): lax.ppermute(part[m], 'tile', [(z, z ^ m) for z in range(tile_count)])  4.67 us
    pallas_call x1, Pallas kernels, finish(): pl.pallas_call(finish_kernel, out_shape=jax.ShapeDtypeStruct((rows, BLOCK...  2.05 us
    ppermute x3, waiting for transfers between devices, over_tile(): lax.ppermute(part[m], 'tile', [(z, z ^ m) for z in range(tile_count)])  1.97 us
    unnamed x7, local copies, waits for them, and re-layouts  1.42 us
  transfers between devices with their start and end apart: 11, of which 3 were waited for; matrix products, arithmetic and copies ran while one was open for 1% of the time, Pallas kernels for 28%

profile of v3, /device:TPU:0, one launch (start us, length us, event | category | flops | bytes accessed | tf_op | source)
XLA Modules:
  0.0 59.1 jit_solution(11197143932423259266)
XLA Ops:
  0.0 0.8 %copy.5 = s32[4,2]{1,0:T(4,128)S(1)} copy(s32[4,2]{0,1:T(2,128)} %param.4) | data formatting | bytes 64 | tf_op args[1]
  0.8 0.1 reshape.11
  0.9 0.1 pad_add_fusion.ids_ref
  0.9 13.2 %waves.1 = (f32[4,8,2,8,2,16,128]{6,5,4,3,2,1,0:T(8,128)}, bf16[2,2,272,1024]{3,2,1,0:T(8,128)(2,1)S(1)}) custom-call(s32[10]{0:T(128)S(1)} %pad_add_fusion.ids_ref, f32[8,1024,512]{2,1,0:T(8,128)} %phases_ref.1, bf16[4,2,2,272,1024]{4,3,2,1,0:T(8,128)(2,1)} %constant.9.clone.tables_ref), custom_call_target="tpu_custom_call" | custom-call | flops 10000000000 | bytes 16777216 | tf_op jit(solution)/shard_map/waves/pallas_call | solution.py:140
  14.2 5.6 %partial_lags.4 = (f32[2,264,128]{2,1,0:T(8,128)S(1)}, f32[2,264,128]{2,1,0:T(8,128)S(1)}) custom-call(s32[1]{0:T(128)} %bitcast.after_ref, f32[4,8,2,8,2,16,128]{6,5,4,3,2,1,0:T(8,128)} %get-tuple-element.20.waves_ref, bf16[2,2,272,1024]{3,2,1,0:T(8,128)(2,1)S(1)} %get-tuple-element.21.tab_ref), custom_call_target="tpu_custom_call" | custom-call | flops 4000000000 | bytes 2097152 | tf_op jit(solution)/shard_map/partial_lags/pallas_call | solution.py:246
  19.7 0.5 collective-permute-start
  20.3 5.6 %partial_lags.5 = (f32[2,264,128]{2,1,0:T(8,128)S(1)}, f32[2,264,128]{2,1,0:T(8,128)S(1)}) custom-call(s32[1]{0:T(128)} %bitcast.after_ref, f32[4,8,2,8,2,16,128]{6,5,4,3,2,1,0:T(8,128)} %get-tuple-element.20.waves_ref, bf16[2,2,272,1024]{3,2,1,0:T(8,128)(2,1)S(1)} %get-tuple-element.21.tab_ref), custom_call_target="tpu_custom_call" | custom-call | flops 4000000000 | bytes 2097152 | tf_op jit(solution)/shard_map/partial_lags/pallas_call | solution.py:246
  25.9 0.1 collective-permute-start.1
  26.0 0.0 collective-permute-done
  26.0 3.0 %collective-permute-start.2 = (f32[264,128]{1,0:T(8,128)S(1)}, f32[264,128]{1,0:T(8,128)S(1)}, u32[]{:S(2)}, u32[]{:S(2)}) collective-permute-start(f32[264,128]{1,0:T(8,128)S(1)} %fusion.11), channel_id=1, source_target_pairs={{0,2},{1,3},{2,0},{3,1},{4,6},{5,7},{6,4},{7,5},{8,10},{9,11},{10,... | collective-permute-start | bytes 405512 | tf_op jit(solution)/shard_map/ppermute | solution.py:314
  29.0 5.6 %partial_lags.6 = (f32[2,264,128]{2,1,0:T(8,128)S(1)}, f32[2,264,128]{2,1,0:T(8,128)S(1)}) custom-call(s32[1]{0:T(128)} %bitcast.after_ref, f32[4,8,2,8,2,16,128]{6,5,4,3,2,1,0:T(8,128)} %get-tuple-element.20.waves_ref, bf16[2,2,272,1024]{3,2,1,0:T(8,128)(2,1)S(1)} %get-tuple-element.21.tab_ref), custom_call_target="tpu_custom_call" | custom-call | flops 4000000000 | bytes 2097152 | tf_op jit(solution)/shard_map/partial_lags/pallas_call | solution.py:246
  34.6 0.1 collective-permute-start.6
  34.7 0.0 collective-permute-done.1
  34.7 0.0 collective-permute-done.2
  34.8 3.7 %collective-permute-start.3 = (f32[264,128]{1,0:T(8,128)S(1)}, f32[264,128]{1,0:T(8,128)S(1)}, u32[]{:S(2)}, u32[]{:S(2)}) collective-permute-start(f32[264,128]{1,0:T(8,128)S(1)} %fusion.9), channel_id=1, source_target_pairs={{0,12},{4,8},{8,4},{12,0},{1,13},{5,9},{9,5},{13,1},{2,14},{6,10},... | collective-permute-start | bytes 405512 | tf_op jit(solution)/shard_map/ppermute | solution.py:317
  38.4 0.5 collective-permute-start.4
  39.0 5.6 %partial_lags.7 = (f32[2,264,128]{2,1,0:T(8,128)S(1)}, f32[2,264,128]{2,1,0:T(8,128)S(1)}) custom-call(s32[1]{0:T(128)} %bitcast.after_ref, f32[4,8,2,8,2,16,128]{6,5,4,3,2,1,0:T(8,128)} %get-tuple-element.20.waves_ref, bf16[2,2,272,1024]{3,2,1,0:T(8,128)(2,1)S(1)} %get-tuple-element.21.tab_ref), custom_call_target="tpu_custom_call" | custom-call | flops 4000000000 | bytes 2097152 | tf_op jit(solution)/shard_map/partial_lags/pallas_call | solution.py:246
  44.5 0.1 collective-permute-start.9
  44.6 0.0 collective-permute-done.4
  44.7 0.1 collective-permute-start.5
  44.7 0.0 collective-permute-done.6
  44.8 1.6 %collective-permute-start.7 = (f32[264,128]{1,0:T(8,128)S(1)}, f32[264,128]{1,0:T(8,128)S(1)}, u32[]{:S(2)}, u32[]{:S(2)}) collective-permute-start(f32[264,128]{1,0:T(8,128)S(1)} %fusion.3), channel_id=1, source_target_pairs={{0,2},{1,3},{2,0},{3,1},{4,6},{5,7},{6,4},{7,5},{8,10},{9,11},{10,... | collective-permute-start | bytes 405512 | tf_op jit(solution)/shard_map/ppermute | solution.py:314
  46.3 0.0 collective-permute-done.9
  46.4 1.4 %collective-permute-start.10 = (f32[264,128]{1,0:T(8,128)S(1)}, f32[264,128]{1,0:T(8,128)S(1)}, u32[]{:S(2)}, u32[]{:S(2)}) collective-permute-start(f32[264,128]{1,0:T(8,128)S(1)} %fusion), channel_id=1, source_target_pairs={{0,2},{1,3},{2,0},{3,1},{4,6},{5,7},{6,4},{7,5},{8,10},{9,11},{10,... | collective-permute-start | bytes 405512 | tf_op jit(solution)/shard_map/ppermute | solution.py:314
  47.7 3.5 %collective-permute-done.7 = f32[264,128]{1,0:T(8,128)S(1)} collective-permute-done((f32[264,128]{1,0:T(8,128)S(1)}, f32[264,128]{1,0:T(8,128)S(1)}, u32[]{:S(2)}, u32[]{:S(2)}) %collective-permute-start.7) | collective-permute-done | bytes 135200 | tf_op jit(solution)/shard_map/ppermute | solution.py:314
  51.2 0.9 %collective-permute-start.8 = (f32[264,128]{1,0:T(8,128)S(1)}, f32[264,128]{1,0:T(8,128)S(1)}, u32[]{:S(2)}, u32[]{:S(2)}) collective-permute-start(f32[264,128]{1,0:T(8,128)S(1)} %fusion.5), channel_id=1, source_target_pairs={{0,4},{4,0},{8,12},{12,8},{1,5},{5,1},{9,13},{13,9},{2,6},{6,2},{1... | collective-permute-start | bytes 405512 | tf_op jit(solution)/shard_map/ppermute | solution.py:317
  52.2 1.5 %collective-permute-done.10 = f32[264,128]{1,0:T(8,128)S(1)} collective-permute-done((f32[264,128]{1,0:T(8,128)S(1)}, f32[264,128]{1,0:T(8,128)S(1)}, u32[]{:S(2)}, u32[]{:S(2)}) %collective-permute-start.10) | collective-permute-done | bytes 135200 | tf_op jit(solution)/shard_map/ppermute | solution.py:314
  53.7 0.7 %fusion.2.refs_3_ = f32[264,128]{1,0:T(8,128)} fusion(f32[264,128]{1,0:T(8,128)S(1)} %collective-permute-done.10, f32[2,264,128]{2,1,0:T(8,128)S(1)} %collective-permute-done.9, f32[2,264,128]{2,1,0:T(8,128)S(1)} %get-tuple-element.33), kind=kLoop, calls=%fused_computation.4 | loop fusion | flops 67584 | bytes 540672 | tf_op jit(solution)/shard_map/add | solution.py:314
  54.4 0.0 collective-permute-done.3.refs_0_
  54.4 2.0 %collective-permute-done.8.refs_2_ = f32[264,128]{1,0:T(8,128)S(1)} collective-permute-done((f32[264,128]{1,0:T(8,128)S(1)}, f32[264,128]{1,0:T(8,128)S(1)}, u32[]{:S(2)}, u32[]{:S(2)}) %collective-permute-start.8) | collective-permute-done | bytes 135200 | tf_op jit(solution)/shard_map/ppermute | solution.py:317
  56.4 0.7 %copy-done.2 = f32[264,128]{1,0:T(8,128)} copy-done((f32[264,128]{1,0:T(8,128)}, f32[264,128]{1,0:T(8,128)S(1)}, u32[]{:S(2)}) %copy-start.2) | copy-done | bytes 135192
  57.0 2.1 %finish.1 = f32[4,16,513]{2,1,0:T(8,128)} custom-call(f32[264,128]{1,0:T(8,128)} %copy-done, f32[264,128]{1,0:T(8,128)} %copy-done.1, f32[264,128]{1,0:T(8,128)} %copy-done.2, f32[264,128]{1,0:T(8,128)} %fusion.2.refs_3_), custom_call_target="tpu_custom_call" | custom-call | tf_op jit(solution)/shard_map/finish/pallas_call | solution.py:289
  (13 shorter events, 0.2 us)
Async XLA Ops:
  19.7 6.2 %collective-permute-start = (f32[2,264,128]{2,1,0:T(8,128)S(1)}, f32[2,264,128]{2,1,0:T(8,128)S(1)}, u32[]{:S(2)}, u32[]{:S(2)}) collective-permute-start(f32[2,264,128]{2,1,0:T(8,128)S(1)} %get-tuple-element.23), channel_id=1, source_target_pairs={{0,1},{1,0},{2,3},{3,2},{4,5},{5,4},{6,7},{7,6},{8,9},{9,8},{10,11... | collective-permute-start | bytes 811016 | tf_op jit(solution)/shard_map/ppermute | solution.py:311
  25.9 8.8 %collective-permute-start.1 = (f32[2,264,128]{2,1,0:T(8,128)S(1)}, f32[2,264,128]{2,1,0:T(8,128)S(1)}, u32[]{:S(2)}, u32[]{:S(2)}) collective-permute-start(f32[2,264,128]{2,1,0:T(8,128)S(1)} %get-tuple-element.26), channel_id=1, source_target_pairs={{0,1},{1,0},{2,3},{3,2},{4,5},{5,4},{6,7},{7,6},{8,9},{9,8},{10,11... | collective-permute-start | bytes 811016 | tf_op jit(solution)/shard_map/ppermute | solution.py:311
  26.0 8.7 %collective-permute-start.2 = (f32[264,128]{1,0:T(8,128)S(1)}, f32[264,128]{1,0:T(8,128)S(1)}, u32[]{:S(2)}, u32[]{:S(2)}) collective-permute-start(f32[264,128]{1,0:T(8,128)S(1)} %fusion.11), channel_id=1, source_target_pairs={{0,2},{1,3},{2,0},{3,1},{4,6},{5,7},{6,4},{7,5},{8,10},{9,11},{10,... | collective-permute-start | bytes 405512 | tf_op jit(solution)/shard_map/ppermute | solution.py:314
  34.6 10.1 %collective-permute-start.6 = (f32[2,264,128]{2,1,0:T(8,128)S(1)}, f32[2,264,128]{2,1,0:T(8,128)S(1)}, u32[]{:S(2)}, u32[]{:S(2)}) collective-permute-start(f32[2,264,128]{2,1,0:T(8,128)S(1)} %get-tuple-element.31), channel_id=1, source_target_pairs={{0,1},{1,0},{2,3},{3,2},{4,5},{5,4},{6,7},{7,6},{8,9},{9,8},{10,11... | collective-permute-start | bytes 811016 | tf_op jit(solution)/shard_map/ppermute | solution.py:311
  34.8 19.6 %collective-permute-start.3 = (f32[264,128]{1,0:T(8,128)S(1)}, f32[264,128]{1,0:T(8,128)S(1)}, u32[]{:S(2)}, u32[]{:S(2)}) collective-permute-start(f32[264,128]{1,0:T(8,128)S(1)} %fusion.9), channel_id=1, source_target_pairs={{0,12},{4,8},{8,4},{12,0},{1,13},{5,9},{9,5},{13,1},{2,14},{6,10},... | collective-permute-start | bytes 405512 | tf_op jit(solution)/shard_map/ppermute | solution.py:317
  38.4 6.2 %collective-permute-start.4 = (f32[264,128]{1,0:T(8,128)S(1)}, f32[264,128]{1,0:T(8,128)S(1)}, u32[]{:S(2)}, u32[]{:S(2)}) collective-permute-start(f32[264,128]{1,0:T(8,128)S(1)} %fusion.10), channel_id=1, source_target_pairs={{0,2},{1,3},{2,0},{3,1},{4,6},{5,7},{6,4},{7,5},{8,10},{9,11},{10,... | collective-permute-start | bytes 405512 | tf_op jit(solution)/shard_map/ppermute | solution.py:314
  44.5 1.8 %collective-permute-start.9 = (f32[2,264,128]{2,1,0:T(8,128)S(1)}, f32[2,264,128]{2,1,0:T(8,128)S(1)}, u32[]{:S(2)}, u32[]{:S(2)}) collective-permute-start(f32[2,264,128]{2,1,0:T(8,128)S(1)} %get-tuple-element.34), channel_id=1, source_target_pairs={{0,1},{1,0},{2,3},{3,2},{4,5},{5,4},{6,7},{7,6},{8,9},{9,8},{10,11... | collective-permute-start | bytes 811016 | tf_op jit(solution)/shard_map/ppermute | solution.py:311
  44.7 9.7 %collective-permute-start.5 = (f32[264,128]{1,0:T(8,128)S(1)}, f32[264,128]{1,0:T(8,128)S(1)}, u32[]{:S(2)}, u32[]{:S(2)}) collective-permute-start(f32[264,128]{1,0:T(8,128)S(1)} %fusion.7), channel_id=1, source_target_pairs={{0,8},{4,12},{8,0},{12,4},{1,9},{5,13},{9,1},{13,5},{2,10},{6,14},... | collective-permute-start | bytes 405512 | tf_op jit(solution)/shard_map/ppermute | solution.py:317
  44.8 6.4 %collective-permute-start.7 = (f32[264,128]{1,0:T(8,128)S(1)}, f32[264,128]{1,0:T(8,128)S(1)}, u32[]{:S(2)}, u32[]{:S(2)}) collective-permute-start(f32[264,128]{1,0:T(8,128)S(1)} %fusion.3), channel_id=1, source_target_pairs={{0,2},{1,3},{2,0},{3,1},{4,6},{5,7},{6,4},{7,5},{8,10},{9,11},{10,... | collective-permute-start | bytes 405512 | tf_op jit(solution)/shard_map/ppermute | solution.py:314
  46.4 7.4 %collective-permute-start.10 = (f32[264,128]{1,0:T(8,128)S(1)}, f32[264,128]{1,0:T(8,128)S(1)}, u32[]{:S(2)}, u32[]{:S(2)}) collective-permute-start(f32[264,128]{1,0:T(8,128)S(1)} %fusion), channel_id=1, source_target_pairs={{0,2},{1,3},{2,0},{3,1},{4,6},{5,7},{6,4},{7,5},{8,10},{9,11},{10,... | collective-permute-start | bytes 405512 | tf_op jit(solution)/shard_map/ppermute | solution.py:314
  51.2 5.1 %collective-permute-start.8 = (f32[264,128]{1,0:T(8,128)S(1)}, f32[264,128]{1,0:T(8,128)S(1)}, u32[]{:S(2)}, u32[]{:S(2)}) collective-permute-start(f32[264,128]{1,0:T(8,128)S(1)} %fusion.5), channel_id=1, source_target_pairs={{0,4},{4,0},{8,12},{12,8},{1,5},{5,1},{9,13},{13,9},{2,6},{6,2},{1... | collective-permute-start | bytes 405512 | tf_op jit(solution)/shard_map/ppermute | solution.py:317
  54.4 2.0 %copy-start = (f32[264,128]{1,0:T(8,128)}, f32[264,128]{1,0:T(8,128)S(1)}, u32[]{:S(2)}) copy-start(f32[264,128]{1,0:T(8,128)S(1)} %collective-permute-done.3.refs_0_) | copy-start | bytes 405508
  54.4 2.0 %copy-start.1 = (f32[264,128]{1,0:T(8,128)}, f32[264,128]{1,0:T(8,128)S(1)}, u32[]{:S(2)}) copy-start(f32[264,128]{1,0:T(8,128)S(1)} %collective-permute-done.5.refs_1_) | copy-start | bytes 405508
  56.4 0.7 %copy-start.2 = (f32[264,128]{1,0:T(8,128)}, f32[264,128]{1,0:T(8,128)S(1)}, u32[]{:S(2)}) copy-start(f32[264,128]{1,0:T(8,128)S(1)} %collective-permute-done.8.refs_2_) | copy-start | bytes 405508

commit v4 on v3

--- a/solution.py
+++ b/solution.py
@@ -62,9 +62,9 @@
         bins = pl.ds(unit * LANES, LANES)
         return pltpu.make_async_copy(phases_ref.at[:, bins, :], raw_ref.at[:, bins, :], raw_sem.at[unit])
 
-    for unit in range(units):
+    ahead = min(units, 4)
+    for unit in range(ahead):
         raw_copy(unit).start()
-    table_copy.start()
 
     def stage_copy(unit):
         slot = unit % 2
@@ -110,6 +110,14 @@
         @pl.when(unit + 1 < units)
         def _():
             raw_copy(unit + 1).wait()
+
+        @pl.when(unit + ahead < units)
+        def _():
+            raw_copy(unit + ahead).start()
+
+        @pl.when(unit == units // 2)
+        def _():
+            table_copy.start()
 
         @pl.when(unit >= 2)
         def _():
@@ -155,9 +163,8 @@
     )(ids, phases, tables)
 
 
-def lag_kernel(m, after_ref, waves_ref, tab_ref, keep_ref, send_ref, wave_ref, acc_ref, plane_ref, *scratch):
+def lag_kernel(m, after_ref, waves_ref, tab_ref, keep_ref, send_ref, wave_ref, plane_ref, spectra_ref, wave_sem):
     del after_ref
-    spectra, wave_sem = scratch[:2], scratch[2]
     units, _, windows = wave_ref.shape[:3]
 
     def wave_copy(unit):
@@ -166,19 +173,16 @@
     for unit in range(units):
         wave_copy(unit).start()
 
-    subs = spectra[0].shape[0]
-    chunks = units // subs
-
-    def prepare(unit):
+    @pl.loop(0, units)
+    def _(unit):
+        wave_copy(unit).wait()
         for w in range(windows):
             lead_cos, trail_cos = wave_ref[unit, 0, w, 0], wave_ref[unit, 0, w, 1]
             lead_sin, trail_sin = wave_ref[unit, 1, w, 0], wave_ref[unit, 1, w, 1]
             plane_ref[0, w, 0], plane_ref[1, w, 0], plane_ref[2, w, 0] = lead_cos + lead_sin, lead_sin, lead_cos
             plane_ref[0, w, 1], plane_ref[1, w, 1] = trail_cos, trail_cos - trail_sin
             plane_ref[2, w, 1] = trail_cos + trail_sin
-
-    def cross(sub, parity, quads):
-        for quad in quads:
+        for quad in range(BLOCK // 4):
             sums = [[None] * 3 for _ in range(4)]
             for w in range(windows):
                 for p in range(3):
@@ -193,47 +197,26 @@
                     value = sums[i][0] - sums[i][1 + part]
                     high = value.astype(jnp.bfloat16)
                     low = value - high.astype(jnp.float32)
-                    spectra[parity][sub, part, 0, rows] = high
-                    spectra[parity][sub, part, 1, rows] = low.astype(jnp.bfloat16)
+                    spectra_ref[unit, part, 0, rows] = high
+                    spectra_ref[unit, part, 1, rows] = low.astype(jnp.bfloat16)
 
     def product(table, values):
         return lax.dot_general(
             table, values, (((1,), (1,)), ((), ())), preferred_element_type=jnp.float32
         )
 
-    def lags(k, part, parity):
-        bins = pl.ds(pl.multiple_of(k * subs * LANES, subs * LANES), subs * LANES)
+    totals = []
+    for part in range(2):
         high, low = (
-            jnp.concatenate([spectra[parity][sub, part, half] for sub in range(subs)], axis=1)
+            jnp.concatenate([spectra_ref[unit, part, half] for unit in range(units)], axis=1)
             for half in range(2)
         )
-        tab_high, tab_low = tab_ref[part, 0, :, bins], tab_ref[part, 1, :, bins]
-        total = product(tab_high, high) + product(tab_low, high) + product(tab_high, low)
-        acc_ref[part] += total
-
-    acc_ref[...] = jnp.zeros_like(acc_ref)
-    spectra[1][...] = jnp.zeros_like(spectra[1])
-
-    @pl.loop(0, chunks // 2)
-    def _(k):
-        for parity in range(2):
-
-            @pl.loop(0, 2)
-            def _(g):
-                unit = (2 * k + parity) * subs + g
-                wave_copy(unit).wait()
-                prepare(unit)
-                cross(g, parity, (0, 1))
-                lags(jnp.maximum(2 * k + parity - 1, 0), g, 1 - parity)
-                cross(g, parity, (2, 3))
-
-    for part in range(2):
-        lags(chunks - 1, part, 1)
+        tab_high, tab_low = tab_ref[part, 0], tab_ref[part, 1]
+        totals.append(product(tab_high, high) + product(tab_low, high) + product(tab_high, low))
     middle = LANES // 2
     low_lanes = lax.broadcasted_iota(jnp.int32, (LAG_ROWS, LANES), 1) < middle
     for core, ref in enumerate((keep_ref, send_ref)):
-        cut = (slice(0, LAG_ROWS), slice(core * LANES, (core + 1) * LANES))
-        even, odd = acc_ref[(0,) + cut], acc_ref[(1,) + cut]
+        even, odd = (total[:LAG_ROWS, core * LANES : (core + 1) * LANES] for total in totals)
         ref[0] = jnp.where(low_lanes, even, pltpu.roll(odd, middle, 1))
         ref[1] = jnp.where(low_lanes, pltpu.roll(even, middle, 1), odd)
 
@@ -250,11 +233,10 @@
         out_shape=[out, out],
         scratch_shapes=[
             pltpu.VMEM(waves.shape[1:], jnp.float32),
-            pltpu.VMEM((2, TAB_ROWS, pairs), jnp.float32),
             planes,
-        ]
-        + [pltpu.VMEM((2, 2, 2, pairs, LANES), jnp.bfloat16)] * 2
-        + [pltpu.SemaphoreType.DMA(waves.shape[1:2])],
+            pltpu.VMEM((waves.shape[1], 2, 2, pairs, LANES), jnp.bfloat16),
+            pltpu.SemaphoreType.DMA(waves.shape[1:2]),
+        ],
         compiler_params=pltpu.CompilerParams(vmem_limit_bytes=LAG_VMEM),
         cost_estimate=pl.CostEstimate(flops=4 * 10**9, bytes_accessed=waves.size, transcendentals=0),
         name="partial_lags",

time: 59.3 us -> 54.9 us (0.926)
  Pallas kernels: 37.6 us -> 32.4 us
  waiting for transfers between devices: 7.01 us -> 8.3 us
    pallas_call x4, Pallas kernels: 22.3 us -> 17.1 us  [partial_lags(): pl.pallas_call(functools.partial(lag_kernel, m), in_specs=[pl.BlockSpec(m...]
    ppermute x4, waiting for transfers between devices: 5.03 us -> 5.73 us  [over_chip(): part[m] = keep[m][0] + came[m][0] + lax.ppermute(away[m], 'win', cross_chip)]
  transfers between devices with their start and end apart: 11 -> 11, of which waited for: 3 -> 5; matrix products, arithmetic and copies ran while one was open for 1% -> 1% of each run, Pallas kernels for 28% -> 23%
where the time goes in v4:
time: 54.9 us; the launch traced here: 54.7 us
  Pallas kernels  32.4 us (59%)
  starting transfers between devices  11.4 us (21%)
  waiting for transfers between devices  8.3 us (15%)
  local copies, waits for them, and re-layouts  1.51 us (3%)
  other arithmetic  0.89 us (2%)
    pallas_call x4, Pallas kernels, partial_lags(): pl.pallas_call(functools.partial(lag_kernel, m), in_specs=[pl.BlockSpec(m...  17.1 us
    pallas_call x1, Pallas kernels, waves_of(): pl.pallas_call(functools.partial(front_kernel, tiles), in_specs=[smem] +...  13.3 us
    ppermute x4, starting transfers between devices, over_chip(): part[m] = keep[m][0] + came[m][0] + lax.ppermute(away[m], 'win', cross_chip)  5.89 us
    ppermute x4, waiting for transfers between devices, over_chip(): part[m] = keep[m][0] + came[m][0] + lax.ppermute(away[m], 'win', cross_chip)  5.73 us
    ppermute x3, starting transfers between devices, over_tile(): lax.ppermute(part[m], 'tile', [(z, z ^ m) for z in range(tile_count)])  4.75 us
    ppermute x3, waiting for transfers between devices, over_tile(): lax.ppermute(part[m], 'tile', [(z, z ^ m) for z in range(tile_count)])  2.17 us
    pallas_call x1, Pallas kernels, finish(): pl.pallas_call(finish_kernel, out_shape=jax.ShapeDtypeStruct((rows, BLOCK...  2.05 us
    unnamed x7, local copies, waits for them, and re-layouts  1.42 us
  transfers between devices with their start and end apart: 11, of which 5 were waited for; matrix products, arithmetic and copies ran while one was open for 1% of the time, Pallas kernels for 23%

profile of v4, /device:TPU:0, one launch (start us, length us, event | category | flops | bytes accessed | tf_op | source)
XLA Modules:
  0.0 54.7 jit_solution(11566313872734063403)
XLA Ops:
  0.0 0.8 %copy.5 = s32[4,2]{1,0:T(4,128)S(1)} copy(s32[4,2]{0,1:T(2,128)} %param.4) | data formatting | bytes 64 | tf_op args[1]
  0.8 0.1 reshape.11
  0.9 0.1 pad_add_fusion.ids_ref
  0.9 13.3 %waves.1 = (f32[4,8,2,8,2,16,128]{6,5,4,3,2,1,0:T(8,128)}, bf16[2,2,272,1024]{3,2,1,0:T(8,128)(2,1)S(1)}) custom-call(s32[10]{0:T(128)S(1)} %pad_add_fusion.ids_ref, f32[8,1024,512]{2,1,0:T(8,128)} %phases_ref.1, bf16[4,2,2,272,1024]{4,3,2,1,0:T(8,128)(2,1)} %constant.9.clone.tables_ref), custom_call_target="tpu_custom_call" | custom-call | flops 10000000000 | bytes 16777216 | tf_op jit(solution)/shard_map/waves/pallas_call | solution.py:148
  14.2 4.3 %partial_lags.4 = (f32[2,264,128]{2,1,0:T(8,128)S(1)}, f32[2,264,128]{2,1,0:T(8,128)S(1)}) custom-call(s32[1]{0:T(128)} %bitcast.after_ref, f32[4,8,2,8,2,16,128]{6,5,4,3,2,1,0:T(8,128)} %get-tuple-element.20.waves_ref, bf16[2,2,272,1024]{3,2,1,0:T(8,128)(2,1)S(1)} %get-tuple-element.21.tab_ref), custom_call_target="tpu_custom_call" | custom-call | flops 4000000000 | bytes 2097152 | tf_op jit(solution)/shard_map/partial_lags/pallas_call | solution.py:229
  18.5 0.5 collective-permute-start
  19.0 4.3 %partial_lags.5 = (f32[2,264,128]{2,1,0:T(8,128)S(1)}, f32[2,264,128]{2,1,0:T(8,128)S(1)}) custom-call(s32[1]{0:T(128)} %bitcast.after_ref, f32[4,8,2,8,2,16,128]{6,5,4,3,2,1,0:T(8,128)} %get-tuple-element.20.waves_ref, bf16[2,2,272,1024]{3,2,1,0:T(8,128)(2,1)S(1)} %get-tuple-element.21.tab_ref), custom_call_target="tpu_custom_call" | custom-call | flops 4000000000 | bytes 2097152 | tf_op jit(solution)/shard_map/partial_lags/pallas_call | solution.py:229
  23.3 0.1 collective-permute-start.1
  23.4 0.0 collective-permute-done
  23.4 3.0 %collective-permute-start.2 = (f32[264,128]{1,0:T(8,128)S(1)}, f32[264,128]{1,0:T(8,128)S(1)}, u32[]{:S(2)}, u32[]{:S(2)}) collective-permute-start(f32[264,128]{1,0:T(8,128)S(1)} %fusion.11), channel_id=1, source_target_pairs={{0,2},{1,3},{2,0},{3,1},{4,6},{5,7},{6,4},{7,5},{8,10},{9,11},{10,... | collective-permute-start | bytes 405512 | tf_op jit(solution)/shard_map/ppermute | solution.py:296
  26.4 4.3 %partial_lags.6 = (f32[2,264,128]{2,1,0:T(8,128)S(1)}, f32[2,264,128]{2,1,0:T(8,128)S(1)}) custom-call(s32[1]{0:T(128)} %bitcast.after_ref, f32[4,8,2,8,2,16,128]{6,5,4,3,2,1,0:T(8,128)} %get-tuple-element.20.waves_ref, bf16[2,2,272,1024]{3,2,1,0:T(8,128)(2,1)S(1)} %get-tuple-element.21.tab_ref), custom_call_target="tpu_custom_call" | custom-call | flops 4000000000 | bytes 2097152 | tf_op jit(solution)/shard_map/partial_lags/pallas_call | solution.py:229
  30.7 0.1 collective-permute-start.6
  30.8 0.0 collective-permute-done.1
  30.9 3.7 %collective-permute-start.3 = (f32[264,128]{1,0:T(8,128)S(1)}, f32[264,128]{1,0:T(8,128)S(1)}, u32[]{:S(2)}, u32[]{:S(2)}) collective-permute-start(f32[264,128]{1,0:T(8,128)S(1)} %fusion.9), channel_id=1, source_target_pairs={{0,12},{4,8},{8,4},{12,0},{1,13},{5,9},{9,5},{13,1},{2,14},{6,10},... | collective-permute-start | bytes 405512 | tf_op jit(solution)/shard_map/ppermute | solution.py:299
  34.5 1.1 %collective-permute-start.4 = (f32[264,128]{1,0:T(8,128)S(1)}, f32[264,128]{1,0:T(8,128)S(1)}, u32[]{:S(2)}, u32[]{:S(2)}) collective-permute-start(f32[264,128]{1,0:T(8,128)S(1)} %fusion.10), channel_id=1, source_target_pairs={{0,2},{1,3},{2,0},{3,1},{4,6},{5,7},{6,4},{7,5},{8,10},{9,11},{10,... | collective-permute-start | bytes 405512 | tf_op jit(solution)/shard_map/ppermute | solution.py:296
  35.6 4.3 %partial_lags.7 = (f32[2,264,128]{2,1,0:T(8,128)S(1)}, f32[2,264,128]{2,1,0:T(8,128)S(1)}) custom-call(s32[1]{0:T(128)} %bitcast.after_ref, f32[4,8,2,8,2,16,128]{6,5,4,3,2,1,0:T(8,128)} %get-tuple-element.20.waves_ref, bf16[2,2,272,1024]{3,2,1,0:T(8,128)(2,1)S(1)} %get-tuple-element.21.tab_ref), custom_call_target="tpu_custom_call" | custom-call | flops 4000000000 | bytes 2097152 | tf_op jit(solution)/shard_map/partial_lags/pallas_call | solution.py:229
  39.9 0.1 collective-permute-start.9
  40.0 0.2 collective-permute-done.4
  40.2 0.1 collective-permute-start.5
  40.3 0.0 collective-permute-done.6
  40.4 0.8 %collective-permute-start.7 = (f32[264,128]{1,0:T(8,128)S(1)}, f32[264,128]{1,0:T(8,128)S(1)}, u32[]{:S(2)}, u32[]{:S(2)}) collective-permute-start(f32[264,128]{1,0:T(8,128)S(1)} %fusion.3), channel_id=1, source_target_pairs={{0,2},{1,3},{2,0},{3,1},{4,6},{5,7},{6,4},{7,5},{8,10},{9,11},{10,... | collective-permute-start | bytes 405512 | tf_op jit(solution)/shard_map/ppermute | solution.py:296
  41.1 0.4 collective-permute-done.9
  41.5 1.0 %collective-permute-start.10 = (f32[264,128]{1,0:T(8,128)S(1)}, f32[264,128]{1,0:T(8,128)S(1)}, u32[]{:S(2)}, u32[]{:S(2)}) collective-permute-start(f32[264,128]{1,0:T(8,128)S(1)} %fusion), channel_id=1, source_target_pairs={{0,2},{1,3},{2,0},{3,1},{4,6},{5,7},{6,4},{7,5},{8,10},{9,11},{10,... | collective-permute-start | bytes 405512 | tf_op jit(solution)/shard_map/ppermute | solution.py:296
  42.5 4.3 %collective-permute-done.7 = f32[264,128]{1,0:T(8,128)S(1)} collective-permute-done((f32[264,128]{1,0:T(8,128)S(1)}, f32[264,128]{1,0:T(8,128)S(1)}, u32[]{:S(2)}, u32[]{:S(2)}) %collective-permute-start.7) | collective-permute-done | bytes 135200 | tf_op jit(solution)/shard_map/ppermute | solution.py:296
  46.9 1.0 %collective-permute-start.8 = (f32[264,128]{1,0:T(8,128)S(1)}, f32[264,128]{1,0:T(8,128)S(1)}, u32[]{:S(2)}, u32[]{:S(2)}) collective-permute-start(f32[264,128]{1,0:T(8,128)S(1)} %fusion.5), channel_id=1, source_target_pairs={{0,4},{4,0},{8,12},{12,8},{1,5},{5,1},{9,13},{13,9},{2,6},{6,2},{1... | collective-permute-start | bytes 405512 | tf_op jit(solution)/shard_map/ppermute | solution.py:299
  47.9 1.2 %collective-permute-done.10 = f32[264,128]{1,0:T(8,128)S(1)} collective-permute-done((f32[264,128]{1,0:T(8,128)S(1)}, f32[264,128]{1,0:T(8,128)S(1)}, u32[]{:S(2)}, u32[]{:S(2)}) %collective-permute-start.10) | collective-permute-done | bytes 135200 | tf_op jit(solution)/shard_map/ppermute | solution.py:296
  49.1 0.7 %fusion.2.refs_3_ = f32[264,128]{1,0:T(8,128)} fusion(f32[264,128]{1,0:T(8,128)S(1)} %collective-permute-done.10, f32[2,264,128]{2,1,0:T(8,128)S(1)} %collective-permute-done.9, f32[2,264,128]{2,1,0:T(8,128)S(1)} %get-tuple-element.33), kind=kLoop, calls=%fused_computation.4 | loop fusion | flops 67584 | bytes 540672 | tf_op jit(solution)/shard_map/add | solution.py:296
  49.8 0.0 collective-permute-done.3.refs_0_
  49.8 0.0 collective-permute-done.5.refs_1_
  49.8 2.2 %collective-permute-done.8.refs_2_ = f32[264,128]{1,0:T(8,128)S(1)} collective-permute-done((f32[264,128]{1,0:T(8,128)S(1)}, f32[264,128]{1,0:T(8,128)S(1)}, u32[]{:S(2)}, u32[]{:S(2)}) %collective-permute-start.8) | collective-permute-done | bytes 135200 | tf_op jit(solution)/shard_map/ppermute | solution.py:299
  52.0 0.7 %copy-done.2 = f32[264,128]{1,0:T(8,128)} copy-done((f32[264,128]{1,0:T(8,128)}, f32[264,128]{1,0:T(8,128)S(1)}, u32[]{:S(2)}) %copy-start.2) | copy-done | bytes 135192
  52.6 2.1 %finish.1 = f32[4,16,513]{2,1,0:T(8,128)} custom-call(f32[264,128]{1,0:T(8,128)} %copy-done, f32[264,128]{1,0:T(8,128)} %copy-done.1, f32[264,128]{1,0:T(8,128)} %copy-done.2, f32[264,128]{1,0:T(8,128)} %fusion.2.refs_3_), custom_call_target="tpu_custom_call" | custom-call | tf_op jit(solution)/shard_map/finish/pallas_call | solution.py:271
  (13 shorter events, 0.2 us)
Async XLA Ops:
  18.5 4.9 %collective-permute-start = (f32[2,264,128]{2,1,0:T(8,128)S(1)}, f32[2,264,128]{2,1,0:T(8,128)S(1)}, u32[]{:S(2)}, u32[]{:S(2)}) collective-permute-start(f32[2,264,128]{2,1,0:T(8,128)S(1)} %get-tuple-element.23), channel_id=1, source_target_pairs={{0,1},{1,0},{2,3},{3,2},{4,5},{5,4},{6,7},{7,6},{8,9},{9,8},{10,11... | collective-permute-start | bytes 811016 | tf_op jit(solution)/shard_map/ppermute | solution.py:293
  23.3 7.5 %collective-permute-start.1 = (f32[2,264,128]{2,1,0:T(8,128)S(1)}, f32[2,264,128]{2,1,0:T(8,128)S(1)}, u32[]{:S(2)}, u32[]{:S(2)}) collective-permute-start(f32[2,264,128]{2,1,0:T(8,128)S(1)} %get-tuple-element.26), channel_id=1, source_target_pairs={{0,1},{1,0},{2,3},{3,2},{4,5},{5,4},{6,7},{7,6},{8,9},{9,8},{10,11... | collective-permute-start | bytes 811016 | tf_op jit(solution)/shard_map/ppermute | solution.py:293
  23.4 7.4 %collective-permute-start.2 = (f32[264,128]{1,0:T(8,128)S(1)}, f32[264,128]{1,0:T(8,128)S(1)}, u32[]{:S(2)}, u32[]{:S(2)}) collective-permute-start(f32[264,128]{1,0:T(8,128)S(1)} %fusion.11), channel_id=1, source_target_pairs={{0,2},{1,3},{2,0},{3,1},{4,6},{5,7},{6,4},{7,5},{8,10},{9,11},{10,... | collective-permute-start | bytes 405512 | tf_op jit(solution)/shard_map/ppermute | solution.py:296
  30.7 9.6 %collective-permute-start.6 = (f32[2,264,128]{2,1,0:T(8,128)S(1)}, f32[2,264,128]{2,1,0:T(8,128)S(1)}, u32[]{:S(2)}, u32[]{:S(2)}) collective-permute-start(f32[2,264,128]{2,1,0:T(8,128)S(1)} %get-tuple-element.31), channel_id=1, source_target_pairs={{0,1},{1,0},{2,3},{3,2},{4,5},{5,4},{6,7},{7,6},{8,9},{9,8},{10,11... | collective-permute-start | bytes 811016 | tf_op jit(solution)/shard_map/ppermute | solution.py:293
  30.9 18.9 %collective-permute-start.3 = (f32[264,128]{1,0:T(8,128)S(1)}, f32[264,128]{1,0:T(8,128)S(1)}, u32[]{:S(2)}, u32[]{:S(2)}) collective-permute-start(f32[264,128]{1,0:T(8,128)S(1)} %fusion.9), channel_id=1, source_target_pairs={{0,12},{4,8},{8,4},{12,0},{1,13},{5,9},{9,5},{13,1},{2,14},{6,10},... | collective-permute-start | bytes 405512 | tf_op jit(solution)/shard_map/ppermute | solution.py:299
  34.5 5.7 %collective-permute-start.4 = (f32[264,128]{1,0:T(8,128)S(1)}, f32[264,128]{1,0:T(8,128)S(1)}, u32[]{:S(2)}, u32[]{:S(2)}) collective-permute-start(f32[264,128]{1,0:T(8,128)S(1)} %fusion.10), channel_id=1, source_target_pairs={{0,2},{1,3},{2,0},{3,1},{4,6},{5,7},{6,4},{7,5},{8,10},{9,11},{10,... | collective-permute-start | bytes 405512 | tf_op jit(solution)/shard_map/ppermute | solution.py:296
  39.9 1.6 %collective-permute-start.9 = (f32[2,264,128]{2,1,0:T(8,128)S(1)}, f32[2,264,128]{2,1,0:T(8,128)S(1)}, u32[]{:S(2)}, u32[]{:S(2)}) collective-permute-start(f32[2,264,128]{2,1,0:T(8,128)S(1)} %get-tuple-element.34), channel_id=1, source_target_pairs={{0,1},{1,0},{2,3},{3,2},{4,5},{5,4},{6,7},{7,6},{8,9},{9,8},{10,11... | collective-permute-start | bytes 811016 | tf_op jit(solution)/shard_map/ppermute | solution.py:293
  40.2 9.5 %collective-permute-start.5 = (f32[264,128]{1,0:T(8,128)S(1)}, f32[264,128]{1,0:T(8,128)S(1)}, u32[]{:S(2)}, u32[]{:S(2)}) collective-permute-start(f32[264,128]{1,0:T(8,128)S(1)} %fusion.7), channel_id=1, source_target_pairs={{0,8},{4,12},{8,0},{12,4},{1,9},{5,13},{9,1},{13,5},{2,10},{6,14},... | collective-permute-start | bytes 405512 | tf_op jit(solution)/shard_map/ppermute | solution.py:299
  40.4 6.5 %collective-permute-start.7 = (f32[264,128]{1,0:T(8,128)S(1)}, f32[264,128]{1,0:T(8,128)S(1)}, u32[]{:S(2)}, u32[]{:S(2)}) collective-permute-start(f32[264,128]{1,0:T(8,128)S(1)} %fusion.3), channel_id=1, source_target_pairs={{0,2},{1,3},{2,0},{3,1},{4,6},{5,7},{6,4},{7,5},{8,10},{9,11},{10,... | collective-permute-start | bytes 405512 | tf_op jit(solution)/shard_map/ppermute | solution.py:296
  41.5 7.5 %collective-permute-start.10 = (f32[264,128]{1,0:T(8,128)S(1)}, f32[264,128]{1,0:T(8,128)S(1)}, u32[]{:S(2)}, u32[]{:S(2)}) collective-permute-start(f32[264,128]{1,0:T(8,128)S(1)} %fusion), channel_id=1, source_target_pairs={{0,2},{1,3},{2,0},{3,1},{4,6},{5,7},{6,4},{7,5},{8,10},{9,11},{10,... | collective-permute-start | bytes 405512 | tf_op jit(solution)/shard_map/ppermute | solution.py:296
  46.9 5.1 %collective-permute-start.8 = (f32[264,128]{1,0:T(8,128)S(1)}, f32[264,128]{1,0:T(8,128)S(1)}, u32[]{:S(2)}, u32[]{:S(2)}) collective-permute-start(f32[264,128]{1,0:T(8,128)S(1)} %fusion.5), channel_id=1, source_target_pairs={{0,4},{4,0},{8,12},{12,8},{1,5},{5,1},{9,13},{13,9},{2,6},{6,2},{1... | collective-permute-start | bytes 405512 | tf_op jit(solution)/shard_map/ppermute | solution.py:299
  49.8 2.2 %copy-start = (f32[264,128]{1,0:T(8,128)}, f32[264,128]{1,0:T(8,128)S(1)}, u32[]{:S(2)}) copy-start(f32[264,128]{1,0:T(8,128)S(1)} %collective-permute-done.3.refs_0_) | copy-start | bytes 405508
  49.8 2.2 %copy-start.1 = (f32[264,128]{1,0:T(8,128)}, f32[264,128]{1,0:T(8,128)S(1)}, u32[]{:S(2)}) copy-start(f32[264,128]{1,0:T(8,128)S(1)} %collective-permute-done.5.refs_1_) | copy-start | bytes 405508
  51.9 0.7 %copy-start.2 = (f32[264,128]{1,0:T(8,128)}, f32[264,128]{1,0:T(8,128)S(1)}, u32[]{:S(2)}) copy-start(f32[264,128]{1,0:T(8,128)S(1)} %collective-permute-done.8.refs_2_) | copy-start | bytes 405508

commit v5 on v4

--- a/solution.py
+++ b/solution.py
@@ -97,11 +97,23 @@
         stage_ref[unit % 2, m // 2, 0, w, m % 2] = cos
         stage_ref[unit % 2, m // 2, 1, w, m % 2] = sin
 
+    eye = lax.broadcasted_iota(jnp.int32, (LANES, LANES), 0) == lax.broadcasted_iota(jnp.int32, (LANES, LANES), 1)
+    eye = eye.astype(jnp.float32).astype(jnp.bfloat16)
+
+    def turn(value):
+        total = None
+        for _ in range(3):
+            term = value.astype(jnp.bfloat16)
+            value = value - term.astype(jnp.float32)
+            part = lax.dot_general(eye, term, (((1,), (1,)), ((), ())), preferred_element_type=jnp.float32)
+            total = part if total is None else total + part
+        return total
+
     pieces = range(LANES // BLOCK)
     raw_copy(0).wait()
     for piece in pieces:
         gather(0, packed[1], piece)
-    turned[0][...] = packed[1][...].T
+    turned[0][...] = turn(packed[1][...])
     for piece in pieces:
         gather(1, packed[0], piece)
 
@@ -123,15 +135,15 @@
         def _():
             stage_copy(unit - 2).wait()
 
-        @pl.loop(0, windows // 4)
+        @pl.loop(0, windows // 8)
         def _(h):
-            for j in range(4):
-                item = unit * windows + 4 * h + j
+            for j in range(8):
+                item = unit * windows + 8 * h + j
                 here, there = j % 2, 1 - j % 2
-                turned[there][...] = packed[here][...].T
                 for piece in pieces:
+                    unfold(item, turned[here], piece)
                     gather(jnp.minimum(item + 2, units * windows - 1), packed[there], piece)
-                    unfold(item, turned[here], piece)
+                turned[there][...] = turn(packed[here][...])
 
         stage_copy(unit).start()
 

time: 54.9 us -> 52.8 us (0.962)
  Pallas kernels: 32.4 us -> 30.4 us
    pallas_call x1, Pallas kernels: 13.3 us -> 11.2 us  [waves_of(): pl.pallas_call(functools.partial(front_kernel, tiles), in_specs=[smem] +...]
  transfers between devices with their start and end apart: 11 -> 11, of which waited for: 5 -> 5; matrix products, arithmetic and copies ran while one was open for 1% -> 2% of each run, Pallas kernels for 23% -> 24%
where the time goes in v5:
time: 52.8 us; the launch traced here: 52.6 us
  Pallas kernels  30.4 us (58%)
  starting transfers between devices  11.4 us (22%)
  waiting for transfers between devices  8.3 us (16%)
  local copies, waits for them, and re-layouts  1.51 us (3%)
  other arithmetic  0.89 us (2%)
    pallas_call x4, Pallas kernels, partial_lags(): pl.pallas_call(functools.partial(lag_kernel, m), in_specs=[pl.BlockSpec(m...  17.1 us
    pallas_call x1, Pallas kernels, waves_of(): pl.pallas_call(functools.partial(front_kernel, tiles), in_specs=[smem] +...  11.2 us
    ppermute x4, starting transfers between devices, over_chip(): part[m] = keep[m][0] + came[m][0] + lax.ppermute(away[m], 'win', cross_chip)  5.88 us
    ppermute x4, waiting for transfers between devices, over_chip(): part[m] = keep[m][0] + came[m][0] + lax.ppermute(away[m], 'win', cross_chip)  5.73 us
    ppermute x3, starting transfers between devices, over_tile(): lax.ppermute(part[m], 'tile', [(z, z ^ m) for z in range(tile_count)])  4.74 us
    ppermute x3, waiting for transfers between devices, over_tile(): lax.ppermute(part[m], 'tile', [(z, z ^ m) for z in range(tile_count)])  2.17 us
    pallas_call x1, Pallas kernels, finish(): pl.pallas_call(finish_kernel, out_shape=jax.ShapeDtypeStruct((rows, BLOCK...  2.05 us
    unnamed x7, local copies, waits for them, and re-layouts  1.42 us
  transfers between devices with their start and end apart: 11, of which 5 were waited for; matrix products, arithmetic and copies ran while one was open for 2% of the time, Pallas kernels for 24%

profile of v5, /device:TPU:0, one launch (start us, length us, event | category | flops | bytes accessed | tf_op | source)
XLA Modules:
  0.0 52.6 jit_solution(7679222952664054840)
XLA Ops:
  0.0 0.8 %copy.5 = s32[4,2]{1,0:T(4,128)S(1)} copy(s32[4,2]{0,1:T(2,128)} %param.4) | data formatting | bytes 64 | tf_op args[1]
  0.8 0.1 reshape.11
  0.9 0.1 pad_add_fusion.ids_ref
  0.9 11.2 %waves.1 = (f32[4,8,2,8,2,16,128]{6,5,4,3,2,1,0:T(8,128)}, bf16[2,2,272,1024]{3,2,1,0:T(8,128)(2,1)S(1)}) custom-call(s32[10]{0:T(128)S(1)} %pad_add_fusion.ids_ref, f32[8,1024,512]{2,1,0:T(8,128)} %phases_ref.1, bf16[4,2,2,272,1024]{4,3,2,1,0:T(8,128)(2,1)} %constant.9.clone.tables_ref), custom_call_target="tpu_custom_call" | custom-call | flops 10000000000 | bytes 16777216 | tf_op jit(solution)/shard_map/waves/pallas_call | solution.py:160
  12.2 4.3 %partial_lags.4 = (f32[2,264,128]{2,1,0:T(8,128)S(1)}, f32[2,264,128]{2,1,0:T(8,128)S(1)}) custom-call(s32[1]{0:T(128)} %bitcast.after_ref, f32[4,8,2,8,2,16,128]{6,5,4,3,2,1,0:T(8,128)} %get-tuple-element.20.waves_ref, bf16[2,2,272,1024]{3,2,1,0:T(8,128)(2,1)S(1)} %get-tuple-element.21.tab_ref), custom_call_target="tpu_custom_call" | custom-call | flops 4000000000 | bytes 2097152 | tf_op jit(solution)/shard_map/partial_lags/pallas_call | solution.py:241
  16.5 0.5 collective-permute-start
  17.0 4.3 %partial_lags.5 = (f32[2,264,128]{2,1,0:T(8,128)S(1)}, f32[2,264,128]{2,1,0:T(8,128)S(1)}) custom-call(s32[1]{0:T(128)} %bitcast.after_ref, f32[4,8,2,8,2,16,128]{6,5,4,3,2,1,0:T(8,128)} %get-tuple-element.20.waves_ref, bf16[2,2,272,1024]{3,2,1,0:T(8,128)(2,1)S(1)} %get-tuple-element.21.tab_ref), custom_call_target="tpu_custom_call" | custom-call | flops 4000000000 | bytes 2097152 | tf_op jit(solution)/shard_map/partial_lags/pallas_call | solution.py:241
  21.2 0.1 collective-permute-start.1
  21.4 3.0 %collective-permute-start.2 = (f32[264,128]{1,0:T(8,128)S(1)}, f32[264,128]{1,0:T(8,128)S(1)}, u32[]{:S(2)}, u32[]{:S(2)}) collective-permute-start(f32[264,128]{1,0:T(8,128)S(1)} %fusion.11), channel_id=1, source_target_pairs={{0,2},{1,3},{2,0},{3,1},{4,6},{5,7},{6,4},{7,5},{8,10},{9,11},{10,... | collective-permute-start | bytes 405512 | tf_op jit(solution)/shard_map/ppermute | solution.py:308
  24.4 4.3 %partial_lags.6 = (f32[2,264,128]{2,1,0:T(8,128)S(1)}, f32[2,264,128]{2,1,0:T(8,128)S(1)}) custom-call(s32[1]{0:T(128)} %bitcast.after_ref, f32[4,8,2,8,2,16,128]{6,5,4,3,2,1,0:T(8,128)} %get-tuple-element.20.waves_ref, bf16[2,2,272,1024]{3,2,1,0:T(8,128)(2,1)S(1)} %get-tuple-element.21.tab_ref), custom_call_target="tpu_custom_call" | custom-call | flops 4000000000 | bytes 2097152 | tf_op jit(solution)/shard_map/partial_lags/pallas_call | solution.py:241
  28.7 0.1 collective-permute-start.6
  28.8 0.0 collective-permute-done.1
  28.8 0.0 collective-permute-done.2
  28.8 3.7 %collective-permute-start.3 = (f32[264,128]{1,0:T(8,128)S(1)}, f32[264,128]{1,0:T(8,128)S(1)}, u32[]{:S(2)}, u32[]{:S(2)}) collective-permute-start(f32[264,128]{1,0:T(8,128)S(1)} %fusion.9), channel_id=1, source_target_pairs={{0,12},{4,8},{8,4},{12,0},{1,13},{5,9},{9,5},{13,1},{2,14},{6,10},... | collective-permute-start | bytes 405512 | tf_op jit(solution)/shard_map/ppermute | solution.py:311
  32.5 1.1 %collective-permute-start.4 = (f32[264,128]{1,0:T(8,128)S(1)}, f32[264,128]{1,0:T(8,128)S(1)}, u32[]{:S(2)}, u32[]{:S(2)}) collective-permute-start(f32[264,128]{1,0:T(8,128)S(1)} %fusion.10), channel_id=1, source_target_pairs={{0,2},{1,3},{2,0},{3,1},{4,6},{5,7},{6,4},{7,5},{8,10},{9,11},{10,... | collective-permute-start | bytes 405512 | tf_op jit(solution)/shard_map/ppermute | solution.py:308
  33.6 4.3 %partial_lags.7 = (f32[2,264,128]{2,1,0:T(8,128)S(1)}, f32[2,264,128]{2,1,0:T(8,128)S(1)}) custom-call(s32[1]{0:T(128)} %bitcast.after_ref, f32[4,8,2,8,2,16,128]{6,5,4,3,2,1,0:T(8,128)} %get-tuple-element.20.waves_ref, bf16[2,2,272,1024]{3,2,1,0:T(8,128)(2,1)S(1)} %get-tuple-element.21.tab_ref), custom_call_target="tpu_custom_call" | custom-call | flops 4000000000 | bytes 2097152 | tf_op jit(solution)/shard_map/partial_lags/pallas_call | solution.py:241
  37.9 0.1 collective-permute-start.9
  38.0 0.2 collective-permute-done.4
  38.2 0.1 collective-permute-start.5
  38.3 0.0 collective-permute-done.6
  38.3 0.8 %collective-permute-start.7 = (f32[264,128]{1,0:T(8,128)S(1)}, f32[264,128]{1,0:T(8,128)S(1)}, u32[]{:S(2)}, u32[]{:S(2)}) collective-permute-start(f32[264,128]{1,0:T(8,128)S(1)} %fusion.3), channel_id=1, source_target_pairs={{0,2},{1,3},{2,0},{3,1},{4,6},{5,7},{6,4},{7,5},{8,10},{9,11},{10,... | collective-permute-start | bytes 405512 | tf_op jit(solution)/shard_map/ppermute | solution.py:308
  39.1 0.4 collective-permute-done.9
  39.5 1.0 %collective-permute-start.10 = (f32[264,128]{1,0:T(8,128)S(1)}, f32[264,128]{1,0:T(8,128)S(1)}, u32[]{:S(2)}, u32[]{:S(2)}) collective-permute-start(f32[264,128]{1,0:T(8,128)S(1)} %fusion), channel_id=1, source_target_pairs={{0,2},{1,3},{2,0},{3,1},{4,6},{5,7},{6,4},{7,5},{8,10},{9,11},{10,... | collective-permute-start | bytes 405512 | tf_op jit(solution)/shard_map/ppermute | solution.py:308
  40.5 4.3 %collective-permute-done.7 = f32[264,128]{1,0:T(8,128)S(1)} collective-permute-done((f32[264,128]{1,0:T(8,128)S(1)}, f32[264,128]{1,0:T(8,128)S(1)}, u32[]{:S(2)}, u32[]{:S(2)}) %collective-permute-start.7) | collective-permute-done | bytes 135200 | tf_op jit(solution)/shard_map/ppermute | solution.py:308
  44.8 1.0 %collective-permute-start.8 = (f32[264,128]{1,0:T(8,128)S(1)}, f32[264,128]{1,0:T(8,128)S(1)}, u32[]{:S(2)}, u32[]{:S(2)}) collective-permute-start(f32[264,128]{1,0:T(8,128)S(1)} %fusion.5), channel_id=1, source_target_pairs={{0,4},{4,0},{8,12},{12,8},{1,5},{5,1},{9,13},{13,9},{2,6},{6,2},{1... | collective-permute-start | bytes 405512 | tf_op jit(solution)/shard_map/ppermute | solution.py:311
  45.9 1.2 %collective-permute-done.10 = f32[264,128]{1,0:T(8,128)S(1)} collective-permute-done((f32[264,128]{1,0:T(8,128)S(1)}, f32[264,128]{1,0:T(8,128)S(1)}, u32[]{:S(2)}, u32[]{:S(2)}) %collective-permute-start.10) | collective-permute-done | bytes 135200 | tf_op jit(solution)/shard_map/ppermute | solution.py:308
  47.1 0.7 %fusion.2.refs_3_ = f32[264,128]{1,0:T(8,128)} fusion(f32[264,128]{1,0:T(8,128)S(1)} %collective-permute-done.10, f32[2,264,128]{2,1,0:T(8,128)S(1)} %collective-permute-done.9, f32[2,264,128]{2,1,0:T(8,128)S(1)} %get-tuple-element.33), kind=kLoop, calls=%fused_computation.4 | loop fusion | flops 67584 | bytes 540672 | tf_op jit(solution)/shard_map/add | solution.py:308
  47.7 0.0 collective-permute-done.3.refs_0_
  47.7 0.0 collective-permute-done.5.refs_1_
  47.8 2.2 %collective-permute-done.8.refs_2_ = f32[264,128]{1,0:T(8,128)S(1)} collective-permute-done((f32[264,128]{1,0:T(8,128)S(1)}, f32[264,128]{1,0:T(8,128)S(1)}, u32[]{:S(2)}, u32[]{:S(2)}) %collective-permute-start.8) | collective-permute-done | bytes 135200 | tf_op jit(solution)/shard_map/ppermute | solution.py:311
  49.9 0.7 %copy-done.2 = f32[264,128]{1,0:T(8,128)} copy-done((f32[264,128]{1,0:T(8,128)}, f32[264,128]{1,0:T(8,128)S(1)}, u32[]{:S(2)}) %copy-start.2) | copy-done | bytes 135192
  50.6 2.1 %finish.1 = f32[4,16,513]{2,1,0:T(8,128)} custom-call(f32[264,128]{1,0:T(8,128)} %copy-done, f32[264,128]{1,0:T(8,128)} %copy-done.1, f32[264,128]{1,0:T(8,128)} %copy-done.2, f32[264,128]{1,0:T(8,128)} %fusion.2.refs_3_), custom_call_target="tpu_custom_call" | custom-call | tf_op jit(solution)/shard_map/finish/pallas_call | solution.py:283
  (13 shorter events, 0.2 us)
Async XLA Ops:
  16.5 4.9 %collective-permute-start = (f32[2,264,128]{2,1,0:T(8,128)S(1)}, f32[2,264,128]{2,1,0:T(8,128)S(1)}, u32[]{:S(2)}, u32[]{:S(2)}) collective-permute-start(f32[2,264,128]{2,1,0:T(8,128)S(1)} %get-tuple-element.23), channel_id=1, source_target_pairs={{0,1},{1,0},{2,3},{3,2},{4,5},{5,4},{6,7},{7,6},{8,9},{9,8},{10,11... | collective-permute-start | bytes 811016 | tf_op jit(solution)/shard_map/ppermute | solution.py:305
  21.2 7.5 %collective-permute-start.1 = (f32[2,264,128]{2,1,0:T(8,128)S(1)}, f32[2,264,128]{2,1,0:T(8,128)S(1)}, u32[]{:S(2)}, u32[]{:S(2)}) collective-permute-start(f32[2,264,128]{2,1,0:T(8,128)S(1)} %get-tuple-element.26), channel_id=1, source_target_pairs={{0,1},{1,0},{2,3},{3,2},{4,5},{5,4},{6,7},{7,6},{8,9},{9,8},{10,11... | collective-permute-start | bytes 811016 | tf_op jit(solution)/shard_map/ppermute | solution.py:305
  21.4 7.4 %collective-permute-start.2 = (f32[264,128]{1,0:T(8,128)S(1)}, f32[264,128]{1,0:T(8,128)S(1)}, u32[]{:S(2)}, u32[]{:S(2)}) collective-permute-start(f32[264,128]{1,0:T(8,128)S(1)} %fusion.11), channel_id=1, source_target_pairs={{0,2},{1,3},{2,0},{3,1},{4,6},{5,7},{6,4},{7,5},{8,10},{9,11},{10,... | collective-permute-start | bytes 405512 | tf_op jit(solution)/shard_map/ppermute | solution.py:308
  28.7 9.6 %collective-permute-start.6 = (f32[2,264,128]{2,1,0:T(8,128)S(1)}, f32[2,264,128]{2,1,0:T(8,128)S(1)}, u32[]{:S(2)}, u32[]{:S(2)}) collective-permute-start(f32[2,264,128]{2,1,0:T(8,128)S(1)} %get-tuple-element.31), channel_id=1, source_target_pairs={{0,1},{1,0},{2,3},{3,2},{4,5},{5,4},{6,7},{7,6},{8,9},{9,8},{10,11... | collective-permute-start | bytes 811016 | tf_op jit(solution)/shard_map/ppermute | solution.py:305
  28.8 18.9 %collective-permute-start.3 = (f32[264,128]{1,0:T(8,128)S(1)}, f32[264,128]{1,0:T(8,128)S(1)}, u32[]{:S(2)}, u32[]{:S(2)}) collective-permute-start(f32[264,128]{1,0:T(8,128)S(1)} %fusion.9), channel_id=1, source_target_pairs={{0,12},{4,8},{8,4},{12,0},{1,13},{5,9},{9,5},{13,1},{2,14},{6,10},... | collective-permute-start | bytes 405512 | tf_op jit(solution)/shard_map/ppermute | solution.py:311
  32.5 5.7 %collective-permute-start.4 = (f32[264,128]{1,0:T(8,128)S(1)}, f32[264,128]{1,0:T(8,128)S(1)}, u32[]{:S(2)}, u32[]{:S(2)}) collective-permute-start(f32[264,128]{1,0:T(8,128)S(1)} %fusion.10), channel_id=1, source_target_pairs={{0,2},{1,3},{2,0},{3,1},{4,6},{5,7},{6,4},{7,5},{8,10},{9,11},{10,... | collective-permute-start | bytes 405512 | tf_op jit(solution)/shard_map/ppermute | solution.py:308
  37.9 1.6 %collective-permute-start.9 = (f32[2,264,128]{2,1,0:T(8,128)S(1)}, f32[2,264,128]{2,1,0:T(8,128)S(1)}, u32[]{:S(2)}, u32[]{:S(2)}) collective-permute-start(f32[2,264,128]{2,1,0:T(8,128)S(1)} %get-tuple-element.34), channel_id=1, source_target_pairs={{0,1},{1,0},{2,3},{3,2},{4,5},{5,4},{6,7},{7,6},{8,9},{9,8},{10,11... | collective-permute-start | bytes 811016 | tf_op jit(solution)/shard_map/ppermute | solution.py:305
  38.2 9.5 %collective-permute-start.5 = (f32[264,128]{1,0:T(8,128)S(1)}, f32[264,128]{1,0:T(8,128)S(1)}, u32[]{:S(2)}, u32[]{:S(2)}) collective-permute-start(f32[264,128]{1,0:T(8,128)S(1)} %fusion.7), channel_id=1, source_target_pairs={{0,8},{4,12},{8,0},{12,4},{1,9},{5,13},{9,1},{13,5},{2,10},{6,14},... | collective-permute-start | bytes 405512 | tf_op jit(solution)/shard_map/ppermute | solution.py:311
  38.3 6.5 %collective-permute-start.7 = (f32[264,128]{1,0:T(8,128)S(1)}, f32[264,128]{1,0:T(8,128)S(1)}, u32[]{:S(2)}, u32[]{:S(2)}) collective-permute-start(f32[264,128]{1,0:T(8,128)S(1)} %fusion.3), channel_id=1, source_target_pairs={{0,2},{1,3},{2,0},{3,1},{4,6},{5,7},{6,4},{7,5},{8,10},{9,11},{10,... | collective-permute-start | bytes 405512 | tf_op jit(solution)/shard_map/ppermute | solution.py:308
  39.5 7.5 %collective-permute-start.10 = (f32[264,128]{1,0:T(8,128)S(1)}, f32[264,128]{1,0:T(8,128)S(1)}, u32[]{:S(2)}, u32[]{:S(2)}) collective-permute-start(f32[264,128]{1,0:T(8,128)S(1)} %fusion), channel_id=1, source_target_pairs={{0,2},{1,3},{2,0},{3,1},{4,6},{5,7},{6,4},{7,5},{8,10},{9,11},{10,... | collective-permute-start | bytes 405512 | tf_op jit(solution)/shard_map/ppermute | solution.py:308
  44.8 5.1 %collective-permute-start.8 = (f32[264,128]{1,0:T(8,128)S(1)}, f32[264,128]{1,0:T(8,128)S(1)}, u32[]{:S(2)}, u32[]{:S(2)}) collective-permute-start(f32[264,128]{1,0:T(8,128)S(1)} %fusion.5), channel_id=1, source_target_pairs={{0,4},{4,0},{8,12},{12,8},{1,5},{5,1},{9,13},{13,9},{2,6},{6,2},{1... | collective-permute-start | bytes 405512 | tf_op jit(solution)/shard_map/ppermute | solution.py:311
  47.7 2.2 %copy-start = (f32[264,128]{1,0:T(8,128)}, f32[264,128]{1,0:T(8,128)S(1)}, u32[]{:S(2)}) copy-start(f32[264,128]{1,0:T(8,128)S(1)} %collective-permute-done.3.refs_0_) | copy-start | bytes 405508
  47.7 2.2 %copy-start.1 = (f32[264,128]{1,0:T(8,128)}, f32[264,128]{1,0:T(8,128)S(1)}, u32[]{:S(2)}) copy-start(f32[264,128]{1,0:T(8,128)S(1)} %collective-permute-done.5.refs_1_) | copy-start | bytes 405508
  49.9 0.7 %copy-start.2 = (f32[264,128]{1,0:T(8,128)}, f32[264,128]{1,0:T(8,128)S(1)}, u32[]{:S(2)}) copy-start(f32[264,128]{1,0:T(8,128)S(1)} %collective-permute-done.8.refs_2_) | copy-start | bytes 405508

commit v6 on v5

--- a/solution.py
+++ b/solution.py
@@ -50,10 +50,13 @@
     return t * q, 1.0 - t * t
 
 
-def front_kernel(tiles, ids_ref, phases_ref, tables_ref, out_ref, tab_ref, *refs):
+def front_kernel(tiles, blocks_ref, phases_ref, tables_ref, out_ref, tab_ref, *refs):
     raw_ref, stage_ref, packed, turned = refs[0], refs[1], refs[2:4], refs[4:6]
-    raw_sem, stage_sem, tab_sem = refs[6:]
-    table_copy = pltpu.make_async_copy(tables_ref.at[ids_ref[0]], tab_ref, tab_sem)
+    held_ref, raw_sem, stage_sem, tab_sem, blocks_sem = refs[6:]
+    place, me = lax.axis_index("tile"), lax.axis_index("win")
+    table_copy = pltpu.make_async_copy(tables_ref.at[place], tab_ref, tab_sem)
+    blocks_copy = pltpu.make_async_copy(blocks_ref, held_ref, blocks_sem)
+    blocks_copy.start()
     windows, bins_local, channels = raw_ref.shape
     units = bins_local // LANES
     per_lane_tile = LANES // BLOCK
@@ -72,11 +75,14 @@
 
     lane = lax.broadcasted_iota(jnp.int32, (8, LANES), 1)
     at, col = lane % BLOCK, lane // BLOCK
-    chip, core = ids_ref[1] // 2, ids_ref[1] % 2
+    chip, core = me // 2, me % 2
+    blocks_copy.wait()
     lead = ((at // 8) ^ core) * 4 + (((at // 4) % 2) ^ chip) * 8 + at % 4
     block = jnp.zeros_like(lane)
-    for m in range(2 * tiles):
-        block = jnp.where(col == m, ids_ref[2 + 2 * (ids_ref[0] ^ (m // 2)) + m % 2], block)
+    for t in range(tiles):
+        for side in range(2):
+            here = ((col // 2) ^ place == t) & (col % 2 == side)
+            block = jnp.where(here, held_ref[t : t + 1, side : side + 1], block)
     row = jnp.where(col % 2 == 0, lead, at) + (block % per_lane_tile) * BLOCK
     row = jnp.tile(row, (BLOCK // 8, 1))
     source = jnp.tile(block // per_lane_tile, (BLOCK // 8, 1))
@@ -152,14 +158,14 @@
         stage_copy(unit).wait()
 
 
-def waves_of(phases, ids, tables, tiles):
+def waves_of(phases, tile_blocks, tables, tiles):
     windows, bins_local, channels = phases.shape
     table = jax.ShapeDtypeStruct(tables.shape[1:], tables.dtype)
     out = jax.ShapeDtypeStruct((tiles, bins_local // LANES, 2, windows, 2, BLOCK, LANES), jnp.float32)
-    smem, vmem = pl.BlockSpec(memory_space=pltpu.SMEM), pl.BlockSpec(memory_space=pltpu.VMEM)
+    vmem = pl.BlockSpec(memory_space=pltpu.VMEM)
     return pl.pallas_call(
         functools.partial(front_kernel, tiles),
-        in_specs=[smem] + [pl.BlockSpec(memory_space=pl.ANY)] * 2,
+        in_specs=[pl.BlockSpec(memory_space=pl.ANY)] * 3,
         out_specs=[pl.BlockSpec(memory_space=pl.ANY), vmem],
         out_shape=[out, table],
         scratch_shapes=[
@@ -167,12 +173,13 @@
             pltpu.VMEM((2, tiles) + out.shape[2:], jnp.float32),
         ]
         + [pltpu.VMEM((LANES, LANES), jnp.float32)] * 4
+        + [pltpu.VMEM(tile_blocks.shape, jnp.int32)]
         + [pltpu.SemaphoreType.DMA((k,)) for k in (bins_local // LANES, 2)]
-        + [pltpu.SemaphoreType.DMA],
+        + [pltpu.SemaphoreType.DMA] * 2,
         compiler_params=pltpu.CompilerParams(vmem_limit_bytes=FRONT_VMEM),
         cost_estimate=pl.CostEstimate(flops=10**10, bytes_accessed=phases.size * 4, transcendentals=0),
         name="waves",
-    )(ids, phases, tables)
+    )(tile_blocks, phases, tables)
 
 
 def lag_kernel(m, after_ref, waves_ref, tab_ref, keep_ref, send_ref, wave_ref, plane_ref, spectra_ref, wave_sem):
@@ -291,13 +298,11 @@
     tile_count = lax.axis_size("tile")
     win_count = lax.axis_size("win")
     windows, bins_local, _ = phases.shape
-    place = jnp.stack([lax.axis_index("tile"), lax.axis_index("win")])
-    ids = jnp.concatenate([place, tile_blocks.reshape(-1)])
     tables = jnp.asarray(lag_tables(bins_local * tile_count, bins_local, windows * win_count))
     cross_core = [(w, w ^ 1) for w in range(win_count)]
     cross_chip = [(w, w ^ 2) for w in range(win_count)]
-    waves, table = waves_of(phases, ids, tables, tile_count)
-    after = ids[:1]
+    waves, table = waves_of(phases, tile_blocks, tables, tile_count)
+    after = jnp.zeros(1, jnp.int32)
     keep, came, away, part = {}, {}, {}, {}
 
     def over_core(m):

time: 52.8 us -> 52.2 us (0.989)
  Pallas kernels: 30.4 us -> 29.8 us
    pallas_call x1, Pallas kernels: 11.2 us -> 10.7 us  [waves_of(): pl.pallas_call(functools.partial(front_kernel, tiles), in_specs=[pl.Block...]
  transfers between devices with their start and end apart: 11 -> 11, of which waited for: 5 -> 5; matrix products, arithmetic and copies ran while one was open for 2% -> 2% of each run, Pallas kernels for 24% -> 25%
where the time goes in v6:
time: 52.2 us; the launch traced here: 51.9 us
  Pallas kernels  29.8 us (57%)
  starting transfers between devices  11.4 us (22%)
  waiting for transfers between devices  8.29 us (16%)
  local copies, waits for them, and re-layouts  1.42 us (3%)
  other arithmetic  0.81 us (2%)
    pallas_call x4, Pallas kernels, partial_lags(): pl.pallas_call(functools.partial(lag_kernel, m), in_specs=[pl.BlockSpec(m...  17.1 us
    pallas_call x1, Pallas kernels, waves_of(): pl.pallas_call(functools.partial(front_kernel, tiles), in_specs=[pl.Block...  10.7 us
    ppermute x4, starting transfers between devices, over_chip(): part[m] = keep[m][0] + came[m][0] + lax.ppermute(away[m], 'win', cross_chip)  5.88 us
    ppermute x4, waiting for transfers between devices, over_chip(): part[m] = keep[m][0] + came[m][0] + lax.ppermute(away[m], 'win', cross_chip)  5.72 us
    ppermute x3, starting transfers between devices, over_tile(): lax.ppermute(part[m], 'tile', [(z, z ^ m) for z in range(tile_count)])  4.77 us
    ppermute x3, waiting for transfers between devices, over_tile(): lax.ppermute(part[m], 'tile', [(z, z ^ m) for z in range(tile_count)])  2.17 us
    pallas_call x1, Pallas kernels, finish(): pl.pallas_call(finish_kernel, out_shape=jax.ShapeDtypeStruct((rows, BLOCK...  2.05 us
    unnamed x7, local copies, waits for them, and re-layouts  1.42 us
  transfers between devices with their start and end apart: 11, of which 5 were waited for; matrix products, arithmetic and copies ran while one was open for 2% of the time, Pallas kernels for 25%

profile of v6, /device:TPU:0, one launch (start us, length us, event | category | flops | bytes accessed | tf_op | source)
XLA Modules:
  0.0 51.9 jit_solution(17874626429280046847)
XLA Ops:
  0.0 0.8 %copy.4.blocks_ref = s32[4,2]{1,0:T(4,128)S(1)} copy(s32[4,2]{0,1:T(2,128)} %param.4) | data formatting | bytes 64 | tf_op args[1]
  0.8 10.7 %waves.1 = (f32[4,8,2,8,2,16,128]{6,5,4,3,2,1,0:T(8,128)}, bf16[2,2,272,1024]{3,2,1,0:T(8,128)(2,1)S(1)}) custom-call(s32[4,2]{1,0:T(4,128)S(1)} %copy.4.blocks_ref, f32[8,1024,512]{2,1,0:T(8,128)} %phases_ref.1, bf16[4,2,2,272,1024]{4,3,2,1,0:T(8,128)(2,1)} %constant.4.clone.tables_ref), custom_call_target="tpu_custom_call" | custom-call | flops 10000000000 | bytes 16777216 | tf_op jit(solution)/shard_map/waves/pallas_call | solution.py:166
  11.5 4.3 %partial_lags.4 = (f32[2,264,128]{2,1,0:T(8,128)S(1)}, f32[2,264,128]{2,1,0:T(8,128)S(1)}) custom-call(s32[1]{0:T(128)} %constant.1.clone.1.after_ref, f32[4,8,2,8,2,16,128]{6,5,4,3,2,1,0:T(8,128)} %get-tuple-element.20.waves_ref, bf16[2,2,272,1024]{3,2,1,0:T(8,128)(2,1)S(1)} %get-tuple-element.21.tab_ref), custom_call_target="tpu_custom_call" | custom-call | flops 4000000000 | bytes 2097152 | tf_op jit(solution)/shard_map/partial_lags/pallas_call | solution.py:248
  15.8 0.5 collective-permute-start
  16.3 4.3 %partial_lags.5 = (f32[2,264,128]{2,1,0:T(8,128)S(1)}, f32[2,264,128]{2,1,0:T(8,128)S(1)}) custom-call(s32[1]{0:T(128)} %constant.1.clone.1.after_ref, f32[4,8,2,8,2,16,128]{6,5,4,3,2,1,0:T(8,128)} %get-tuple-element.20.waves_ref, bf16[2,2,272,1024]{3,2,1,0:T(8,128)(2,1)S(1)} %get-tuple-element.21.tab_ref), custom_call_target="tpu_custom_call" | custom-call | flops 4000000000 | bytes 2097152 | tf_op jit(solution)/shard_map/partial_lags/pallas_call | solution.py:248
  20.6 0.1 collective-permute-start.1
  20.7 0.0 collective-permute-done
  20.7 3.0 %collective-permute-start.2 = (f32[264,128]{1,0:T(8,128)S(1)}, f32[264,128]{1,0:T(8,128)S(1)}, u32[]{:S(2)}, u32[]{:S(2)}) collective-permute-start(f32[264,128]{1,0:T(8,128)S(1)} %fusion.11), channel_id=1, source_target_pairs={{0,2},{1,3},{2,0},{3,1},{4,6},{5,7},{6,4},{7,5},{8,10},{9,11},{10,... | collective-permute-start | bytes 405512 | tf_op jit(solution)/shard_map/ppermute | solution.py:313
  23.7 4.3 %partial_lags.6 = (f32[2,264,128]{2,1,0:T(8,128)S(1)}, f32[2,264,128]{2,1,0:T(8,128)S(1)}) custom-call(s32[1]{0:T(128)} %constant.1.clone.1.after_ref, f32[4,8,2,8,2,16,128]{6,5,4,3,2,1,0:T(8,128)} %get-tuple-element.20.waves_ref, bf16[2,2,272,1024]{3,2,1,0:T(8,128)(2,1)S(1)} %get-tuple-element.21.tab_ref), custom_call_target="tpu_custom_call" | custom-call | flops 4000000000 | bytes 2097152 | tf_op jit(solution)/shard_map/partial_lags/pallas_call | solution.py:248
  28.0 0.1 collective-permute-start.6
  28.1 0.0 collective-permute-done.1
  28.1 0.0 collective-permute-done.2
  28.1 3.7 %collective-permute-start.3 = (f32[264,128]{1,0:T(8,128)S(1)}, f32[264,128]{1,0:T(8,128)S(1)}, u32[]{:S(2)}, u32[]{:S(2)}) collective-permute-start(f32[264,128]{1,0:T(8,128)S(1)} %fusion.9), channel_id=1, source_target_pairs={{0,12},{4,8},{8,4},{12,0},{1,13},{5,9},{9,5},{13,1},{2,14},{6,10},... | collective-permute-start | bytes 405512 | tf_op jit(solution)/shard_map/ppermute | solution.py:316
  31.8 1.1 %collective-permute-start.4 = (f32[264,128]{1,0:T(8,128)S(1)}, f32[264,128]{1,0:T(8,128)S(1)}, u32[]{:S(2)}, u32[]{:S(2)}) collective-permute-start(f32[264,128]{1,0:T(8,128)S(1)} %fusion.10), channel_id=1, source_target_pairs={{0,2},{1,3},{2,0},{3,1},{4,6},{5,7},{6,4},{7,5},{8,10},{9,11},{10,... | collective-permute-start | bytes 405512 | tf_op jit(solution)/shard_map/ppermute | solution.py:313
  32.9 4.3 %partial_lags.7 = (f32[2,264,128]{2,1,0:T(8,128)S(1)}, f32[2,264,128]{2,1,0:T(8,128)S(1)}) custom-call(s32[1]{0:T(128)} %constant.1.clone.1.after_ref, f32[4,8,2,8,2,16,128]{6,5,4,3,2,1,0:T(8,128)} %get-tuple-element.20.waves_ref, bf16[2,2,272,1024]{3,2,1,0:T(8,128)(2,1)S(1)} %get-tuple-element.21.tab_ref), custom_call_target="tpu_custom_call" | custom-call | flops 4000000000 | bytes 2097152 | tf_op jit(solution)/shard_map/partial_lags/pallas_call | solution.py:248
  37.2 0.1 collective-permute-start.9
  37.3 0.2 collective-permute-done.4
  37.5 0.1 collective-permute-start.5
  37.6 0.0 collective-permute-done.6
  37.6 0.8 %collective-permute-start.7 = (f32[264,128]{1,0:T(8,128)S(1)}, f32[264,128]{1,0:T(8,128)S(1)}, u32[]{:S(2)}, u32[]{:S(2)}) collective-permute-start(f32[264,128]{1,0:T(8,128)S(1)} %fusion.3), channel_id=1, source_target_pairs={{0,2},{1,3},{2,0},{3,1},{4,6},{5,7},{6,4},{7,5},{8,10},{9,11},{10,... | collective-permute-start | bytes 405512 | tf_op jit(solution)/shard_map/ppermute | solution.py:313
  38.4 0.4 collective-permute-done.9
  38.8 1.0 %collective-permute-start.10 = (f32[264,128]{1,0:T(8,128)S(1)}, f32[264,128]{1,0:T(8,128)S(1)}, u32[]{:S(2)}, u32[]{:S(2)}) collective-permute-start(f32[264,128]{1,0:T(8,128)S(1)} %fusion), channel_id=1, source_target_pairs={{0,2},{1,3},{2,0},{3,1},{4,6},{5,7},{6,4},{7,5},{8,10},{9,11},{10,... | collective-permute-start | bytes 405512 | tf_op jit(solution)/shard_map/ppermute | solution.py:313
  39.8 4.3 %collective-permute-done.7 = f32[264,128]{1,0:T(8,128)S(1)} collective-permute-done((f32[264,128]{1,0:T(8,128)S(1)}, f32[264,128]{1,0:T(8,128)S(1)}, u32[]{:S(2)}, u32[]{:S(2)}) %collective-permute-start.7) | collective-permute-done | bytes 135200 | tf_op jit(solution)/shard_map/ppermute | solution.py:313
  44.1 1.0 %collective-permute-start.8 = (f32[264,128]{1,0:T(8,128)S(1)}, f32[264,128]{1,0:T(8,128)S(1)}, u32[]{:S(2)}, u32[]{:S(2)}) collective-permute-start(f32[264,128]{1,0:T(8,128)S(1)} %fusion.5), channel_id=1, source_target_pairs={{0,4},{4,0},{8,12},{12,8},{1,5},{5,1},{9,13},{13,9},{2,6},{6,2},{1... | collective-permute-start | bytes 405512 | tf_op jit(solution)/shard_map/ppermute | solution.py:316
  45.2 1.2 %collective-permute-done.10 = f32[264,128]{1,0:T(8,128)S(1)} collective-permute-done((f32[264,128]{1,0:T(8,128)S(1)}, f32[264,128]{1,0:T(8,128)S(1)}, u32[]{:S(2)}, u32[]{:S(2)}) %collective-permute-start.10) | collective-permute-done | bytes 135200 | tf_op jit(solution)/shard_map/ppermute | solution.py:313
  46.4 0.7 %fusion.2.refs_3_ = f32[264,128]{1,0:T(8,128)} fusion(f32[264,128]{1,0:T(8,128)S(1)} %collective-permute-done.10, f32[2,264,128]{2,1,0:T(8,128)S(1)} %collective-permute-done.9, f32[2,264,128]{2,1,0:T(8,128)S(1)} %get-tuple-element.33), kind=kLoop, calls=%fused_computation.4 | loop fusion | flops 67584 | bytes 540672 | tf_op jit(solution)/shard_map/add | solution.py:313
  47.0 0.0 collective-permute-done.3.refs_0_
  47.0 0.0 collective-permute-done.5.refs_1_
  47.1 2.2 %collective-permute-done.8.refs_2_ = f32[264,128]{1,0:T(8,128)S(1)} collective-permute-done((f32[264,128]{1,0:T(8,128)S(1)}, f32[264,128]{1,0:T(8,128)S(1)}, u32[]{:S(2)}, u32[]{:S(2)}) %collective-permute-start.8) | collective-permute-done | bytes 135200 | tf_op jit(solution)/shard_map/ppermute | solution.py:316
  49.2 0.0 copy-done.1
  49.2 0.7 %copy-done.2 = f32[264,128]{1,0:T(8,128)} copy-done((f32[264,128]{1,0:T(8,128)}, f32[264,128]{1,0:T(8,128)S(1)}, u32[]{:S(2)}) %copy-start.2) | copy-done | bytes 135192
  49.9 2.1 %finish.1 = f32[4,16,513]{2,1,0:T(8,128)} custom-call(f32[264,128]{1,0:T(8,128)} %copy-done, f32[264,128]{1,0:T(8,128)} %copy-done.1, f32[264,128]{1,0:T(8,128)} %copy-done.2, f32[264,128]{1,0:T(8,128)} %fusion.2.refs_3_), custom_call_target="tpu_custom_call" | custom-call | tf_op jit(solution)/shard_map/finish/pallas_call | solution.py:290
  (11 shorter events, 0.1 us)
Async XLA Ops:
  15.8 4.9 %collective-permute-start = (f32[2,264,128]{2,1,0:T(8,128)S(1)}, f32[2,264,128]{2,1,0:T(8,128)S(1)}, u32[]{:S(2)}, u32[]{:S(2)}) collective-permute-start(f32[2,264,128]{2,1,0:T(8,128)S(1)} %get-tuple-element.23), channel_id=1, source_target_pairs={{0,1},{1,0},{2,3},{3,2},{4,5},{5,4},{6,7},{7,6},{8,9},{9,8},{10,11... | collective-permute-start | bytes 811016 | tf_op jit(solution)/shard_map/ppermute | solution.py:310
  20.6 7.5 %collective-permute-start.1 = (f32[2,264,128]{2,1,0:T(8,128)S(1)}, f32[2,264,128]{2,1,0:T(8,128)S(1)}, u32[]{:S(2)}, u32[]{:S(2)}) collective-permute-start(f32[2,264,128]{2,1,0:T(8,128)S(1)} %get-tuple-element.26), channel_id=1, source_target_pairs={{0,1},{1,0},{2,3},{3,2},{4,5},{5,4},{6,7},{7,6},{8,9},{9,8},{10,11... | collective-permute-start | bytes 811016 | tf_op jit(solution)/shard_map/ppermute | solution.py:310
  20.7 7.4 %collective-permute-start.2 = (f32[264,128]{1,0:T(8,128)S(1)}, f32[264,128]{1,0:T(8,128)S(1)}, u32[]{:S(2)}, u32[]{:S(2)}) collective-permute-start(f32[264,128]{1,0:T(8,128)S(1)} %fusion.11), channel_id=1, source_target_pairs={{0,2},{1,3},{2,0},{3,1},{4,6},{5,7},{6,4},{7,5},{8,10},{9,11},{10,... | collective-permute-start | bytes 405512 | tf_op jit(solution)/shard_map/ppermute | solution.py:313
  28.0 9.6 %collective-permute-start.6 = (f32[2,264,128]{2,1,0:T(8,128)S(1)}, f32[2,264,128]{2,1,0:T(8,128)S(1)}, u32[]{:S(2)}, u32[]{:S(2)}) collective-permute-start(f32[2,264,128]{2,1,0:T(8,128)S(1)} %get-tuple-element.31), channel_id=1, source_target_pairs={{0,1},{1,0},{2,3},{3,2},{4,5},{5,4},{6,7},{7,6},{8,9},{9,8},{10,11... | collective-permute-start | bytes 811016 | tf_op jit(solution)/shard_map/ppermute | solution.py:310
  28.1 18.9 %collective-permute-start.3 = (f32[264,128]{1,0:T(8,128)S(1)}, f32[264,128]{1,0:T(8,128)S(1)}, u32[]{:S(2)}, u32[]{:S(2)}) collective-permute-start(f32[264,128]{1,0:T(8,128)S(1)} %fusion.9), channel_id=1, source_target_pairs={{0,12},{4,8},{8,4},{12,0},{1,13},{5,9},{9,5},{13,1},{2,14},{6,10},... | collective-permute-start | bytes 405512 | tf_op jit(solution)/shard_map/ppermute | solution.py:316
  31.8 5.7 %collective-permute-start.4 = (f32[264,128]{1,0:T(8,128)S(1)}, f32[264,128]{1,0:T(8,128)S(1)}, u32[]{:S(2)}, u32[]{:S(2)}) collective-permute-start(f32[264,128]{1,0:T(8,128)S(1)} %fusion.10), channel_id=1, source_target_pairs={{0,2},{1,3},{2,0},{3,1},{4,6},{5,7},{6,4},{7,5},{8,10},{9,11},{10,... | collective-permute-start | bytes 405512 | tf_op jit(solution)/shard_map/ppermute | solution.py:313
  37.2 1.6 %collective-permute-start.9 = (f32[2,264,128]{2,1,0:T(8,128)S(1)}, f32[2,264,128]{2,1,0:T(8,128)S(1)}, u32[]{:S(2)}, u32[]{:S(2)}) collective-permute-start(f32[2,264,128]{2,1,0:T(8,128)S(1)} %get-tuple-element.34), channel_id=1, source_target_pairs={{0,1},{1,0},{2,3},{3,2},{4,5},{5,4},{6,7},{7,6},{8,9},{9,8},{10,11... | collective-permute-start | bytes 811016 | tf_op jit(solution)/shard_map/ppermute | solution.py:310
  37.5 9.5 %collective-permute-start.5 = (f32[264,128]{1,0:T(8,128)S(1)}, f32[264,128]{1,0:T(8,128)S(1)}, u32[]{:S(2)}, u32[]{:S(2)}) collective-permute-start(f32[264,128]{1,0:T(8,128)S(1)} %fusion.7), channel_id=1, source_target_pairs={{0,8},{4,12},{8,0},{12,4},{1,9},{5,13},{9,1},{13,5},{2,10},{6,14},... | collective-permute-start | bytes 405512 | tf_op jit(solution)/shard_map/ppermute | solution.py:316
  37.6 6.5 %collective-permute-start.7 = (f32[264,128]{1,0:T(8,128)S(1)}, f32[264,128]{1,0:T(8,128)S(1)}, u32[]{:S(2)}, u32[]{:S(2)}) collective-permute-start(f32[264,128]{1,0:T(8,128)S(1)} %fusion.3), channel_id=1, source_target_pairs={{0,2},{1,3},{2,0},{3,1},{4,6},{5,7},{6,4},{7,5},{8,10},{9,11},{10,... | collective-permute-start | bytes 405512 | tf_op jit(solution)/shard_map/ppermute | solution.py:313
  38.8 7.5 %collective-permute-start.10 = (f32[264,128]{1,0:T(8,128)S(1)}, f32[264,128]{1,0:T(8,128)S(1)}, u32[]{:S(2)}, u32[]{:S(2)}) collective-permute-start(f32[264,128]{1,0:T(8,128)S(1)} %fusion), channel_id=1, source_target_pairs={{0,2},{1,3},{2,0},{3,1},{4,6},{5,7},{6,4},{7,5},{8,10},{9,11},{10,... | collective-permute-start | bytes 405512 | tf_op jit(solution)/shard_map/ppermute | solution.py:313
  44.1 5.1 %collective-permute-start.8 = (f32[264,128]{1,0:T(8,128)S(1)}, f32[264,128]{1,0:T(8,128)S(1)}, u32[]{:S(2)}, u32[]{:S(2)}) collective-permute-start(f32[264,128]{1,0:T(8,128)S(1)} %fusion.5), channel_id=1, source_target_pairs={{0,4},{4,0},{8,12},{12,8},{1,5},{5,1},{9,13},{13,9},{2,6},{6,2},{1... | collective-permute-start | bytes 405512 | tf_op jit(solution)/shard_map/ppermute | solution.py:316
  47.0 2.2 %copy-start = (f32[264,128]{1,0:T(8,128)}, f32[264,128]{1,0:T(8,128)S(1)}, u32[]{:S(2)}) copy-start(f32[264,128]{1,0:T(8,128)S(1)} %collective-permute-done.3.refs_0_) | copy-start | bytes 405508
  47.1 2.2 %copy-start.1 = (f32[264,128]{1,0:T(8,128)}, f32[264,128]{1,0:T(8,128)S(1)}, u32[]{:S(2)}) copy-start(f32[264,128]{1,0:T(8,128)S(1)} %collective-permute-done.5.refs_1_) | copy-start | bytes 405508
  49.2 0.7 %copy-start.2 = (f32[264,128]{1,0:T(8,128)}, f32[264,128]{1,0:T(8,128)S(1)}, u32[]{:S(2)}) copy-start(f32[264,128]{1,0:T(8,128)S(1)} %collective-permute-done.8.refs_2_) | copy-start | bytes 405508

commit v7 on v6

--- a/solution.py
+++ b/solution.py
@@ -75,9 +75,9 @@
 
     lane = lax.broadcasted_iota(jnp.int32, (8, LANES), 1)
     at, col = lane % BLOCK, lane // BLOCK
-    chip, core = me // 2, me % 2
+    core = me % 2
     blocks_copy.wait()
-    lead = ((at // 8) ^ core) * 4 + (((at // 4) % 2) ^ chip) * 8 + at % 4
+    lead = ((at // 8) ^ core) * 4 + ((at // 4) % 2) * 8 + at % 4
     block = jnp.zeros_like(lane)
     for t in range(tiles):
         for side in range(2):
@@ -211,8 +211,9 @@
                         prod = plane_ref[p, w, 0, row : row + 1, :] * right
                         sums[i][p] = prod if w == 0 else sums[i][p] + prod
             for i in range(4):
-                rows = slice((quad * 4 + i) * BLOCK, (quad * 4 + i + 1) * BLOCK)
                 for part in range(2):
+                    first = ((quad ^ part) * 4 + i) * BLOCK
+                    rows = slice(first, first + BLOCK)
                     value = sums[i][0] - sums[i][1 + part]
                     high = value.astype(jnp.bfloat16)
                     low = value - high.astype(jnp.float32)
@@ -233,11 +234,12 @@
         tab_high, tab_low = tab_ref[part, 0], tab_ref[part, 1]
         totals.append(product(tab_high, high) + product(tab_low, high) + product(tab_high, low))
     middle = LANES // 2
+    chip = lax.axis_index("win") // 2
     low_lanes = lax.broadcasted_iota(jnp.int32, (LAG_ROWS, LANES), 1) < middle
     for core, ref in enumerate((keep_ref, send_ref)):
         even, odd = (total[:LAG_ROWS, core * LANES : (core + 1) * LANES] for total in totals)
-        ref[0] = jnp.where(low_lanes, even, pltpu.roll(odd, middle, 1))
-        ref[1] = jnp.where(low_lanes, pltpu.roll(even, middle, 1), odd)
+        ref[chip] = jnp.where(low_lanes, even, odd)
+        ref[1 - chip] = jnp.where(low_lanes, odd, even)
 
 
 def partial_lags(m, waves, table, after):
@@ -270,7 +272,8 @@
     half = LANES // 2
     other = pltpu.roll(total, half, 1)
     low_lanes = lax.broadcasted_iota(jnp.int32, total.shape, 1) < half
-    both = jnp.where(low_lanes, total - other, total + other)
+    sign = 1.0 - 2.0 * (lax.axis_index("win") // 2).astype(jnp.float32)
+    both = jnp.where(low_lanes, sign * (total - other), total + other)
     rows, trailing = out_ref.shape[0], out_ref.shape[1]
     mirror = LANES - 1 - lax.broadcasted_iota(jnp.int32, (half, LANES), 1)
     for k in range(HALF // LANES):

time: 52.2 us -> 51.8 us (level)
  transfers between devices with their start and end apart: 11 -> 11, of which waited for: 5 -> 5; matrix products, arithmetic and copies ran while one was open for 2% -> 2% of each run, Pallas kernels for 25% -> 24%
where the time goes in v7:
time: 51.8 us; the launch traced here: 51.6 us
  Pallas kernels  29.4 us (57%)
  starting transfers between devices  11.4 us (22%)
  waiting for transfers between devices  8.4 us (16%)
  local copies, waits for them, and re-layouts  1.42 us (3%)
  other arithmetic  0.81 us (2%)
    pallas_call x4, Pallas kernels, partial_lags(): pl.pallas_call(functools.partial(lag_kernel, m), in_specs=[pl.BlockSpec(m...  16.6 us
    pallas_call x1, Pallas kernels, waves_of(): pl.pallas_call(functools.partial(front_kernel, tiles), in_specs=[pl.Block...  10.7 us
    ppermute x4, starting transfers between devices, over_chip(): part[m] = keep[m][0] + came[m][0] + lax.ppermute(away[m], 'win', cross_chip)  5.88 us
    ppermute x4, waiting for transfers between devices, over_chip(): part[m] = keep[m][0] + came[m][0] + lax.ppermute(away[m], 'win', cross_chip)  5.72 us
    ppermute x3, starting transfers between devices, over_tile(): lax.ppermute(part[m], 'tile', [(z, z ^ m) for z in range(tile_count)])  4.77 us
    ppermute x3, waiting for transfers between devices, over_tile(): lax.ppermute(part[m], 'tile', [(z, z ^ m) for z in range(tile_count)])  2.17 us
    pallas_call x1, Pallas kernels, finish(): pl.pallas_call(finish_kernel, out_shape=jax.ShapeDtypeStruct((rows, BLOCK...  2.05 us
    unnamed x7, local copies, waits for them, and re-layouts  1.42 us
  transfers between devices with their start and end apart: 11, of which 5 were waited for; matrix products, arithmetic and copies ran while one was open for 2% of the time, Pallas kernels for 24%

profile of v7, /device:TPU:0, one launch (start us, length us, event | category | flops | bytes accessed | tf_op | source)
XLA Modules:
  0.0 51.6 jit_solution(16260030615111013454)
XLA Ops:
  0.0 0.8 %copy.4.blocks_ref = s32[4,2]{1,0:T(4,128)S(1)} copy(s32[4,2]{0,1:T(2,128)} %param.4) | data formatting | bytes 64 | tf_op args[1]
  0.8 10.7 %waves.1 = (f32[4,8,2,8,2,16,128]{6,5,4,3,2,1,0:T(8,128)}, bf16[2,2,272,1024]{3,2,1,0:T(8,128)(2,1)S(1)}) custom-call(s32[4,2]{1,0:T(4,128)S(1)} %copy.4.blocks_ref, f32[8,1024,512]{2,1,0:T(8,128)} %phases_ref.1, bf16[4,2,2,272,1024]{4,3,2,1,0:T(8,128)(2,1)} %constant.4.clone.tables_ref), custom_call_target="tpu_custom_call" | custom-call | flops 10000000000 | bytes 16777216 | tf_op jit(solution)/shard_map/waves/pallas_call | solution.py:166
  11.5 4.2 %partial_lags.4 = (f32[2,264,128]{2,1,0:T(8,128)S(1)}, f32[2,264,128]{2,1,0:T(8,128)S(1)}) custom-call(s32[1]{0:T(128)} %constant.1.clone.1.after_ref, f32[4,8,2,8,2,16,128]{6,5,4,3,2,1,0:T(8,128)} %get-tuple-element.20.waves_ref, bf16[2,2,272,1024]{3,2,1,0:T(8,128)(2,1)S(1)} %get-tuple-element.21.tab_ref), custom_call_target="tpu_custom_call" | custom-call | flops 4000000000 | bytes 2097152 | tf_op jit(solution)/shard_map/partial_lags/pallas_call | solution.py:250
  15.6 0.5 %collective-permute-start = (f32[2,264,128]{2,1,0:T(8,128)S(1)}, f32[2,264,128]{2,1,0:T(8,128)S(1)}, u32[]{:S(2)}, u32[]{:S(2)}) collective-permute-start(f32[2,264,128]{2,1,0:T(8,128)S(1)} %get-tuple-element.23), channel_id=1, source_target_pairs={{0,1},{1,0},{2,3},{3,2},{4,5},{5,4},{6,7},{7,6},{8,9},{9,8},{10,11... | collective-permute-start | bytes 811016 | tf_op jit(solution)/shard_map/ppermute | solution.py:313
  16.2 4.2 %partial_lags.5 = (f32[2,264,128]{2,1,0:T(8,128)S(1)}, f32[2,264,128]{2,1,0:T(8,128)S(1)}) custom-call(s32[1]{0:T(128)} %constant.1.clone.1.after_ref, f32[4,8,2,8,2,16,128]{6,5,4,3,2,1,0:T(8,128)} %get-tuple-element.20.waves_ref, bf16[2,2,272,1024]{3,2,1,0:T(8,128)(2,1)S(1)} %get-tuple-element.21.tab_ref), custom_call_target="tpu_custom_call" | custom-call | flops 4000000000 | bytes 2097152 | tf_op jit(solution)/shard_map/partial_lags/pallas_call | solution.py:250
  20.3 0.1 collective-permute-start.1
  20.4 0.0 collective-permute-done
  20.5 3.0 %collective-permute-start.2 = (f32[264,128]{1,0:T(8,128)S(1)}, f32[264,128]{1,0:T(8,128)S(1)}, u32[]{:S(2)}, u32[]{:S(2)}) collective-permute-start(f32[264,128]{1,0:T(8,128)S(1)} %fusion.11), channel_id=1, source_target_pairs={{0,2},{1,3},{2,0},{3,1},{4,6},{5,7},{6,4},{7,5},{8,10},{9,11},{10,... | collective-permute-start | bytes 405512 | tf_op jit(solution)/shard_map/ppermute | solution.py:316
  23.5 4.2 %partial_lags.6 = (f32[2,264,128]{2,1,0:T(8,128)S(1)}, f32[2,264,128]{2,1,0:T(8,128)S(1)}) custom-call(s32[1]{0:T(128)} %constant.1.clone.1.after_ref, f32[4,8,2,8,2,16,128]{6,5,4,3,2,1,0:T(8,128)} %get-tuple-element.20.waves_ref, bf16[2,2,272,1024]{3,2,1,0:T(8,128)(2,1)S(1)} %get-tuple-element.21.tab_ref), custom_call_target="tpu_custom_call" | custom-call | flops 4000000000 | bytes 2097152 | tf_op jit(solution)/shard_map/partial_lags/pallas_call | solution.py:250
  27.6 0.1 collective-permute-start.6
  27.7 0.0 collective-permute-done.1
  27.7 0.0 collective-permute-done.2
  27.8 3.7 %collective-permute-start.3 = (f32[264,128]{1,0:T(8,128)S(1)}, f32[264,128]{1,0:T(8,128)S(1)}, u32[]{:S(2)}, u32[]{:S(2)}) collective-permute-start(f32[264,128]{1,0:T(8,128)S(1)} %fusion.9), channel_id=1, source_target_pairs={{0,12},{4,8},{8,4},{12,0},{1,13},{5,9},{9,5},{13,1},{2,14},{6,10},... | collective-permute-start | bytes 405512 | tf_op jit(solution)/shard_map/ppermute | solution.py:319
  31.5 1.2 %collective-permute-start.4 = (f32[264,128]{1,0:T(8,128)S(1)}, f32[264,128]{1,0:T(8,128)S(1)}, u32[]{:S(2)}, u32[]{:S(2)}) collective-permute-start(f32[264,128]{1,0:T(8,128)S(1)} %fusion.10), channel_id=1, source_target_pairs={{0,2},{1,3},{2,0},{3,1},{4,6},{5,7},{6,4},{7,5},{8,10},{9,11},{10,... | collective-permute-start | bytes 405512 | tf_op jit(solution)/shard_map/ppermute | solution.py:316
  32.7 4.2 %partial_lags.7 = (f32[2,264,128]{2,1,0:T(8,128)S(1)}, f32[2,264,128]{2,1,0:T(8,128)S(1)}) custom-call(s32[1]{0:T(128)} %constant.1.clone.1.after_ref, f32[4,8,2,8,2,16,128]{6,5,4,3,2,1,0:T(8,128)} %get-tuple-element.20.waves_ref, bf16[2,2,272,1024]{3,2,1,0:T(8,128)(2,1)S(1)} %get-tuple-element.21.tab_ref), custom_call_target="tpu_custom_call" | custom-call | flops 4000000000 | bytes 2097152 | tf_op jit(solution)/shard_map/partial_lags/pallas_call | solution.py:250
  36.8 0.1 collective-permute-start.9
  36.9 0.2 collective-permute-done.4
  37.2 0.1 collective-permute-start.5
  37.3 0.0 collective-permute-done.6
  37.3 0.7 %collective-permute-start.7 = (f32[264,128]{1,0:T(8,128)S(1)}, f32[264,128]{1,0:T(8,128)S(1)}, u32[]{:S(2)}, u32[]{:S(2)}) collective-permute-start(f32[264,128]{1,0:T(8,128)S(1)} %fusion.3), channel_id=1, source_target_pairs={{0,2},{1,3},{2,0},{3,1},{4,6},{5,7},{6,4},{7,5},{8,10},{9,11},{10,... | collective-permute-start | bytes 405512 | tf_op jit(solution)/shard_map/ppermute | solution.py:316
  38.0 0.5 collective-permute-done.9
  38.5 1.0 %collective-permute-start.10 = (f32[264,128]{1,0:T(8,128)S(1)}, f32[264,128]{1,0:T(8,128)S(1)}, u32[]{:S(2)}, u32[]{:S(2)}) collective-permute-start(f32[264,128]{1,0:T(8,128)S(1)} %fusion), channel_id=1, source_target_pairs={{0,2},{1,3},{2,0},{3,1},{4,6},{5,7},{6,4},{7,5},{8,10},{9,11},{10,... | collective-permute-start | bytes 405512 | tf_op jit(solution)/shard_map/ppermute | solution.py:316
  39.5 4.3 %collective-permute-done.7 = f32[264,128]{1,0:T(8,128)S(1)} collective-permute-done((f32[264,128]{1,0:T(8,128)S(1)}, f32[264,128]{1,0:T(8,128)S(1)}, u32[]{:S(2)}, u32[]{:S(2)}) %collective-permute-start.7) | collective-permute-done | bytes 135200 | tf_op jit(solution)/shard_map/ppermute | solution.py:316
  43.8 1.0 %collective-permute-start.8 = (f32[264,128]{1,0:T(8,128)S(1)}, f32[264,128]{1,0:T(8,128)S(1)}, u32[]{:S(2)}, u32[]{:S(2)}) collective-permute-start(f32[264,128]{1,0:T(8,128)S(1)} %fusion.5), channel_id=1, source_target_pairs={{0,4},{4,0},{8,12},{12,8},{1,5},{5,1},{9,13},{13,9},{2,6},{6,2},{1... | collective-permute-start | bytes 405512 | tf_op jit(solution)/shard_map/ppermute | solution.py:319
  44.8 1.2 %collective-permute-done.10 = f32[264,128]{1,0:T(8,128)S(1)} collective-permute-done((f32[264,128]{1,0:T(8,128)S(1)}, f32[264,128]{1,0:T(8,128)S(1)}, u32[]{:S(2)}, u32[]{:S(2)}) %collective-permute-start.10) | collective-permute-done | bytes 135200 | tf_op jit(solution)/shard_map/ppermute | solution.py:316
  46.0 0.7 %fusion.2.refs_3_ = f32[264,128]{1,0:T(8,128)} fusion(f32[264,128]{1,0:T(8,128)S(1)} %collective-permute-done.10, f32[2,264,128]{2,1,0:T(8,128)S(1)} %collective-permute-done.9, f32[2,264,128]{2,1,0:T(8,128)S(1)} %get-tuple-element.33), kind=kLoop, calls=%fused_computation.4 | loop fusion | flops 67584 | bytes 540672 | tf_op jit(solution)/shard_map/add | solution.py:316
  46.7 0.0 collective-permute-done.3.refs_0_
  46.7 0.0 collective-permute-done.5.refs_1_
  46.7 2.2 %collective-permute-done.8.refs_2_ = f32[264,128]{1,0:T(8,128)S(1)} collective-permute-done((f32[264,128]{1,0:T(8,128)S(1)}, f32[264,128]{1,0:T(8,128)S(1)}, u32[]{:S(2)}, u32[]{:S(2)}) %collective-permute-start.8) | collective-permute-done | bytes 135200 | tf_op jit(solution)/shard_map/ppermute | solution.py:319
  48.9 0.0 copy-done
  48.9 0.7 %copy-done.2 = f32[264,128]{1,0:T(8,128)} copy-done((f32[264,128]{1,0:T(8,128)}, f32[264,128]{1,0:T(8,128)S(1)}, u32[]{:S(2)}) %copy-start.2) | copy-done | bytes 135192
  49.5 2.1 %finish.1 = f32[4,16,513]{2,1,0:T(8,128)} custom-call(f32[264,128]{1,0:T(8,128)} %copy-done, f32[264,128]{1,0:T(8,128)} %copy-done.1, f32[264,128]{1,0:T(8,128)} %copy-done.2, f32[264,128]{1,0:T(8,128)} %fusion.2.refs_3_), custom_call_target="tpu_custom_call" | custom-call | tf_op jit(solution)/shard_map/finish/pallas_call | solution.py:293
  (11 shorter events, 0.1 us)
Async XLA Ops:
  15.6 4.8 %collective-permute-start = (f32[2,264,128]{2,1,0:T(8,128)S(1)}, f32[2,264,128]{2,1,0:T(8,128)S(1)}, u32[]{:S(2)}, u32[]{:S(2)}) collective-permute-start(f32[2,264,128]{2,1,0:T(8,128)S(1)} %get-tuple-element.23), channel_id=1, source_target_pairs={{0,1},{1,0},{2,3},{3,2},{4,5},{5,4},{6,7},{7,6},{8,9},{9,8},{10,11... | collective-permute-start | bytes 811016 | tf_op jit(solution)/shard_map/ppermute | solution.py:313
  20.3 7.4 %collective-permute-start.1 = (f32[2,264,128]{2,1,0:T(8,128)S(1)}, f32[2,264,128]{2,1,0:T(8,128)S(1)}, u32[]{:S(2)}, u32[]{:S(2)}) collective-permute-start(f32[2,264,128]{2,1,0:T(8,128)S(1)} %get-tuple-element.26), channel_id=1, source_target_pairs={{0,1},{1,0},{2,3},{3,2},{4,5},{5,4},{6,7},{7,6},{8,9},{9,8},{10,11... | collective-permute-start | bytes 811016 | tf_op jit(solution)/shard_map/ppermute | solution.py:313
  20.5 7.3 %collective-permute-start.2 = (f32[264,128]{1,0:T(8,128)S(1)}, f32[264,128]{1,0:T(8,128)S(1)}, u32[]{:S(2)}, u32[]{:S(2)}) collective-permute-start(f32[264,128]{1,0:T(8,128)S(1)} %fusion.11), channel_id=1, source_target_pairs={{0,2},{1,3},{2,0},{3,1},{4,6},{5,7},{6,4},{7,5},{8,10},{9,11},{10,... | collective-permute-start | bytes 405512 | tf_op jit(solution)/shard_map/ppermute | solution.py:316
  27.6 9.6 %collective-permute-start.6 = (f32[2,264,128]{2,1,0:T(8,128)S(1)}, f32[2,264,128]{2,1,0:T(8,128)S(1)}, u32[]{:S(2)}, u32[]{:S(2)}) collective-permute-start(f32[2,264,128]{2,1,0:T(8,128)S(1)} %get-tuple-element.31), channel_id=1, source_target_pairs={{0,1},{1,0},{2,3},{3,2},{4,5},{5,4},{6,7},{7,6},{8,9},{9,8},{10,11... | collective-permute-start | bytes 811016 | tf_op jit(solution)/shard_map/ppermute | solution.py:313
  27.8 18.9 %collective-permute-start.3 = (f32[264,128]{1,0:T(8,128)S(1)}, f32[264,128]{1,0:T(8,128)S(1)}, u32[]{:S(2)}, u32[]{:S(2)}) collective-permute-start(f32[264,128]{1,0:T(8,128)S(1)} %fusion.9), channel_id=1, source_target_pairs={{0,12},{4,8},{8,4},{12,0},{1,13},{5,9},{9,5},{13,1},{2,14},{6,10},... | collective-permute-start | bytes 405512 | tf_op jit(solution)/shard_map/ppermute | solution.py:319
  31.5 5.7 %collective-permute-start.4 = (f32[264,128]{1,0:T(8,128)S(1)}, f32[264,128]{1,0:T(8,128)S(1)}, u32[]{:S(2)}, u32[]{:S(2)}) collective-permute-start(f32[264,128]{1,0:T(8,128)S(1)} %fusion.10), channel_id=1, source_target_pairs={{0,2},{1,3},{2,0},{3,1},{4,6},{5,7},{6,4},{7,5},{8,10},{9,11},{10,... | collective-permute-start | bytes 405512 | tf_op jit(solution)/shard_map/ppermute | solution.py:316
  36.8 1.6 %collective-permute-start.9 = (f32[2,264,128]{2,1,0:T(8,128)S(1)}, f32[2,264,128]{2,1,0:T(8,128)S(1)}, u32[]{:S(2)}, u32[]{:S(2)}) collective-permute-start(f32[2,264,128]{2,1,0:T(8,128)S(1)} %get-tuple-element.34), channel_id=1, source_target_pairs={{0,1},{1,0},{2,3},{3,2},{4,5},{5,4},{6,7},{7,6},{8,9},{9,8},{10,11... | collective-permute-start | bytes 811016 | tf_op jit(solution)/shard_map/ppermute | solution.py:313
  37.2 9.5 %collective-permute-start.5 = (f32[264,128]{1,0:T(8,128)S(1)}, f32[264,128]{1,0:T(8,128)S(1)}, u32[]{:S(2)}, u32[]{:S(2)}) collective-permute-start(f32[264,128]{1,0:T(8,128)S(1)} %fusion.7), channel_id=1, source_target_pairs={{0,8},{4,12},{8,0},{12,4},{1,9},{5,13},{9,1},{13,5},{2,10},{6,14},... | collective-permute-start | bytes 405512 | tf_op jit(solution)/shard_map/ppermute | solution.py:319
  37.3 6.5 %collective-permute-start.7 = (f32[264,128]{1,0:T(8,128)S(1)}, f32[264,128]{1,0:T(8,128)S(1)}, u32[]{:S(2)}, u32[]{:S(2)}) collective-permute-start(f32[264,128]{1,0:T(8,128)S(1)} %fusion.3), channel_id=1, source_target_pairs={{0,2},{1,3},{2,0},{3,1},{4,6},{5,7},{6,4},{7,5},{8,10},{9,11},{10,... | collective-permute-start | bytes 405512 | tf_op jit(solution)/shard_map/ppermute | solution.py:316
  38.5 7.5 %collective-permute-start.10 = (f32[264,128]{1,0:T(8,128)S(1)}, f32[264,128]{1,0:T(8,128)S(1)}, u32[]{:S(2)}, u32[]{:S(2)}) collective-permute-start(f32[264,128]{1,0:T(8,128)S(1)} %fusion), channel_id=1, source_target_pairs={{0,2},{1,3},{2,0},{3,1},{4,6},{5,7},{6,4},{7,5},{8,10},{9,11},{10,... | collective-permute-start | bytes 405512 | tf_op jit(solution)/shard_map/ppermute | solution.py:316
  43.8 5.1 %collective-permute-start.8 = (f32[264,128]{1,0:T(8,128)S(1)}, f32[264,128]{1,0:T(8,128)S(1)}, u32[]{:S(2)}, u32[]{:S(2)}) collective-permute-start(f32[264,128]{1,0:T(8,128)S(1)} %fusion.5), channel_id=1, source_target_pairs={{0,4},{4,0},{8,12},{12,8},{1,5},{5,1},{9,13},{13,9},{2,6},{6,2},{1... | collective-permute-start | bytes 405512 | tf_op jit(solution)/shard_map/ppermute | solution.py:319
  46.7 2.2 %copy-start = (f32[264,128]{1,0:T(8,128)}, f32[264,128]{1,0:T(8,128)S(1)}, u32[]{:S(2)}) copy-start(f32[264,128]{1,0:T(8,128)S(1)} %collective-permute-done.3.refs_0_) | copy-start | bytes 405508
  46.7 2.2 %copy-start.1 = (f32[264,128]{1,0:T(8,128)}, f32[264,128]{1,0:T(8,128)S(1)}, u32[]{:S(2)}) copy-start(f32[264,128]{1,0:T(8,128)S(1)} %collective-permute-done.5.refs_1_) | copy-start | bytes 405508
  48.9 0.7 %copy-start.2 = (f32[264,128]{1,0:T(8,128)}, f32[264,128]{1,0:T(8,128)S(1)}, u32[]{:S(2)}) copy-start(f32[264,128]{1,0:T(8,128)S(1)} %collective-permute-done.8.refs_2_) | copy-start | bytes 405508

commit v8 on v7

--- a/solution.py
+++ b/solution.py
@@ -65,7 +65,7 @@
         bins = pl.ds(unit * LANES, LANES)
         return pltpu.make_async_copy(phases_ref.at[:, bins, :], raw_ref.at[:, bins, :], raw_sem.at[unit])
 
-    ahead = min(units, 4)
+    ahead = units
     for unit in range(ahead):
         raw_copy(unit).start()
 
@@ -84,18 +84,17 @@
             here = ((col // 2) ^ place == t) & (col % 2 == side)
             block = jnp.where(here, held_ref[t : t + 1, side : side + 1], block)
     row = jnp.where(col % 2 == 0, lead, at) + (block % per_lane_tile) * BLOCK
-    row = jnp.tile(row, (BLOCK // 8, 1))
-    source = jnp.tile(block // per_lane_tile, (BLOCK // 8, 1))
+    source = block // per_lane_tile
 
     def gather(item, to, piece):
         unit, w = item // windows, item % windows
-        first = pl.multiple_of(unit * LANES + piece * BLOCK, BLOCK)
-        value = None
-        for q in range(channels // LANES):
-            raw = raw_ref[w, pl.ds(first, BLOCK), q * LANES : (q + 1) * LANES]
-            moved = jnp.take_along_axis(raw, row, axis=1)
-            value = moved if value is None else jnp.where(source == q, moved, value)
-        to[piece * BLOCK : (piece + 1) * BLOCK] = value
+        for first in range(piece * BLOCK, (piece + 1) * BLOCK, 8):
+            bins = pl.ds(pl.multiple_of(unit * LANES + first, 8), 8)
+            value = None
+            for q in range(channels // LANES):
+                moved = jnp.take_along_axis(raw_ref[w, bins, q * LANES : (q + 1) * LANES], row, axis=1)
+                value = moved if value is None else jnp.where(source == q, moved, value)
+            to[first : first + 8] = value
 
     def unfold(item, rows_ref, m):
         unit, w = item // windows, item % windows

time: 51.8 us -> 51.8 us (level)
  no operation moved by 1% of the time
where the time goes in v8:
time: 51.8 us; the launch traced here: 51.6 us
  Pallas kernels  29.4 us (57%)
  starting transfers between devices  11.4 us (22%)
  waiting for transfers between devices  8.41 us (16%)
  local copies, waits for them, and re-layouts  1.42 us (3%)
  other arithmetic  0.81 us (2%)
    pallas_call x4, Pallas kernels, partial_lags(): pl.pallas_call(functools.partial(lag_kernel, m), in_specs=[pl.BlockSpec(m...  16.6 us
    pallas_call x1, Pallas kernels, waves_of(): pl.pallas_call(functools.partial(front_kernel, tiles), in_specs=[pl.Block...  10.7 us
    ppermute x4, starting transfers between devices, over_chip(): part[m] = keep[m][0] + came[m][0] + lax.ppermute(away[m], 'win', cross_chip)  5.88 us
    ppermute x4, waiting for transfers between devices, over_chip(): part[m] = keep[m][0] + came[m][0] + lax.ppermute(away[m], 'win', cross_chip)  5.73 us
    ppermute x3, starting transfers between devices, over_tile(): lax.ppermute(part[m], 'tile', [(z, z ^ m) for z in range(tile_count)])  4.76 us
    ppermute x3, waiting for transfers between devices, over_tile(): lax.ppermute(part[m], 'tile', [(z, z ^ m) for z in range(tile_count)])  2.17 us
    pallas_call x1, Pallas kernels, finish(): pl.pallas_call(finish_kernel, out_shape=jax.ShapeDtypeStruct((rows, BLOCK...  2.05 us
    unnamed x7, local copies, waits for them, and re-layouts  1.42 us
  transfers between devices with their start and end apart: 11, of which 5 were waited for; matrix products, arithmetic and copies ran while one was open for 2% of the time, Pallas kernels for 24%

profile of v8, /device:TPU:0, one launch (start us, length us, event | category | flops | bytes accessed | tf_op | source)
XLA Modules:
  0.0 51.6 jit_solution(10309115020408112721)
XLA Ops:
  0.0 0.8 %copy.4.blocks_ref = s32[4,2]{1,0:T(4,128)S(1)} copy(s32[4,2]{0,1:T(2,128)} %param.4) | data formatting | bytes 64 | tf_op args[1]
  0.8 10.7 %waves.1 = (f32[4,8,2,8,2,16,128]{6,5,4,3,2,1,0:T(8,128)}, bf16[2,2,272,1024]{3,2,1,0:T(8,128)(2,1)S(1)}) custom-call(s32[4,2]{1,0:T(4,128)S(1)} %copy.4.blocks_ref, f32[8,1024,512]{2,1,0:T(8,128)} %phases_ref.1, bf16[4,2,2,272,1024]{4,3,2,1,0:T(8,128)(2,1)} %constant.4.clone.tables_ref), custom_call_target="tpu_custom_call" | custom-call | flops 10000000000 | bytes 16777216 | tf_op jit(solution)/shard_map/waves/pallas_call | solution.py:165
  11.5 4.2 %partial_lags.4 = (f32[2,264,128]{2,1,0:T(8,128)S(1)}, f32[2,264,128]{2,1,0:T(8,128)S(1)}) custom-call(s32[1]{0:T(128)} %constant.1.clone.1.after_ref, f32[4,8,2,8,2,16,128]{6,5,4,3,2,1,0:T(8,128)} %get-tuple-element.20.waves_ref, bf16[2,2,272,1024]{3,2,1,0:T(8,128)(2,1)S(1)} %get-tuple-element.21.tab_ref), custom_call_target="tpu_custom_call" | custom-call | flops 4000000000 | bytes 2097152 | tf_op jit(solution)/shard_map/partial_lags/pallas_call | solution.py:249
  15.7 0.5 %collective-permute-start = (f32[2,264,128]{2,1,0:T(8,128)S(1)}, f32[2,264,128]{2,1,0:T(8,128)S(1)}, u32[]{:S(2)}, u32[]{:S(2)}) collective-permute-start(f32[2,264,128]{2,1,0:T(8,128)S(1)} %get-tuple-element.23), channel_id=1, source_target_pairs={{0,1},{1,0},{2,3},{3,2},{4,5},{5,4},{6,7},{7,6},{8,9},{9,8},{10,11... | collective-permute-start | bytes 811016 | tf_op jit(solution)/shard_map/ppermute | solution.py:312
  16.2 4.2 %partial_lags.5 = (f32[2,264,128]{2,1,0:T(8,128)S(1)}, f32[2,264,128]{2,1,0:T(8,128)S(1)}) custom-call(s32[1]{0:T(128)} %constant.1.clone.1.after_ref, f32[4,8,2,8,2,16,128]{6,5,4,3,2,1,0:T(8,128)} %get-tuple-element.20.waves_ref, bf16[2,2,272,1024]{3,2,1,0:T(8,128)(2,1)S(1)} %get-tuple-element.21.tab_ref), custom_call_target="tpu_custom_call" | custom-call | flops 4000000000 | bytes 2097152 | tf_op jit(solution)/shard_map/partial_lags/pallas_call | solution.py:249
  20.4 0.1 collective-permute-start.1
  20.5 0.0 collective-permute-done
  20.5 3.0 %collective-permute-start.2 = (f32[264,128]{1,0:T(8,128)S(1)}, f32[264,128]{1,0:T(8,128)S(1)}, u32[]{:S(2)}, u32[]{:S(2)}) collective-permute-start(f32[264,128]{1,0:T(8,128)S(1)} %fusion.11), channel_id=1, source_target_pairs={{0,2},{1,3},{2,0},{3,1},{4,6},{5,7},{6,4},{7,5},{8,10},{9,11},{10,... | collective-permute-start | bytes 405512 | tf_op jit(solution)/shard_map/ppermute | solution.py:315
  23.5 4.2 %partial_lags.6 = (f32[2,264,128]{2,1,0:T(8,128)S(1)}, f32[2,264,128]{2,1,0:T(8,128)S(1)}) custom-call(s32[1]{0:T(128)} %constant.1.clone.1.after_ref, f32[4,8,2,8,2,16,128]{6,5,4,3,2,1,0:T(8,128)} %get-tuple-element.20.waves_ref, bf16[2,2,272,1024]{3,2,1,0:T(8,128)(2,1)S(1)} %get-tuple-element.21.tab_ref), custom_call_target="tpu_custom_call" | custom-call | flops 4000000000 | bytes 2097152 | tf_op jit(solution)/shard_map/partial_lags/pallas_call | solution.py:249
  27.7 0.1 collective-permute-start.6
  27.7 0.0 collective-permute-done.1
  27.8 0.0 collective-permute-done.2
  27.8 3.7 %collective-permute-start.3 = (f32[264,128]{1,0:T(8,128)S(1)}, f32[264,128]{1,0:T(8,128)S(1)}, u32[]{:S(2)}, u32[]{:S(2)}) collective-permute-start(f32[264,128]{1,0:T(8,128)S(1)} %fusion.9), channel_id=1, source_target_pairs={{0,12},{4,8},{8,4},{12,0},{1,13},{5,9},{9,5},{13,1},{2,14},{6,10},... | collective-permute-start | bytes 405512 | tf_op jit(solution)/shard_map/ppermute | solution.py:318
  31.5 1.2 %collective-permute-start.4 = (f32[264,128]{1,0:T(8,128)S(1)}, f32[264,128]{1,0:T(8,128)S(1)}, u32[]{:S(2)}, u32[]{:S(2)}) collective-permute-start(f32[264,128]{1,0:T(8,128)S(1)} %fusion.10), channel_id=1, source_target_pairs={{0,2},{1,3},{2,0},{3,1},{4,6},{5,7},{6,4},{7,5},{8,10},{9,11},{10,... | collective-permute-start | bytes 405512 | tf_op jit(solution)/shard_map/ppermute | solution.py:315
  32.7 4.2 %partial_lags.7 = (f32[2,264,128]{2,1,0:T(8,128)S(1)}, f32[2,264,128]{2,1,0:T(8,128)S(1)}) custom-call(s32[1]{0:T(128)} %constant.1.clone.1.after_ref, f32[4,8,2,8,2,16,128]{6,5,4,3,2,1,0:T(8,128)} %get-tuple-element.20.waves_ref, bf16[2,2,272,1024]{3,2,1,0:T(8,128)(2,1)S(1)} %get-tuple-element.21.tab_ref), custom_call_target="tpu_custom_call" | custom-call | flops 4000000000 | bytes 2097152 | tf_op jit(solution)/shard_map/partial_lags/pallas_call | solution.py:249
  36.9 0.1 collective-permute-start.9
  37.0 0.2 collective-permute-done.4
  37.2 0.1 collective-permute-start.5
  37.3 0.0 collective-permute-done.6
  37.3 0.7 %collective-permute-start.7 = (f32[264,128]{1,0:T(8,128)S(1)}, f32[264,128]{1,0:T(8,128)S(1)}, u32[]{:S(2)}, u32[]{:S(2)}) collective-permute-start(f32[264,128]{1,0:T(8,128)S(1)} %fusion.3), channel_id=1, source_target_pairs={{0,2},{1,3},{2,0},{3,1},{4,6},{5,7},{6,4},{7,5},{8,10},{9,11},{10,... | collective-permute-start | bytes 405512 | tf_op jit(solution)/shard_map/ppermute | solution.py:315
  38.0 0.5 collective-permute-done.9
  38.5 1.0 %collective-permute-start.10 = (f32[264,128]{1,0:T(8,128)S(1)}, f32[264,128]{1,0:T(8,128)S(1)}, u32[]{:S(2)}, u32[]{:S(2)}) collective-permute-start(f32[264,128]{1,0:T(8,128)S(1)} %fusion), channel_id=1, source_target_pairs={{0,2},{1,3},{2,0},{3,1},{4,6},{5,7},{6,4},{7,5},{8,10},{9,11},{10,... | collective-permute-start | bytes 405512 | tf_op jit(solution)/shard_map/ppermute | solution.py:315
  39.5 4.3 %collective-permute-done.7 = f32[264,128]{1,0:T(8,128)S(1)} collective-permute-done((f32[264,128]{1,0:T(8,128)S(1)}, f32[264,128]{1,0:T(8,128)S(1)}, u32[]{:S(2)}, u32[]{:S(2)}) %collective-permute-start.7) | collective-permute-done | bytes 135200 | tf_op jit(solution)/shard_map/ppermute | solution.py:315
  43.8 1.0 %collective-permute-start.8 = (f32[264,128]{1,0:T(8,128)S(1)}, f32[264,128]{1,0:T(8,128)S(1)}, u32[]{:S(2)}, u32[]{:S(2)}) collective-permute-start(f32[264,128]{1,0:T(8,128)S(1)} %fusion.5), channel_id=1, source_target_pairs={{0,4},{4,0},{8,12},{12,8},{1,5},{5,1},{9,13},{13,9},{2,6},{6,2},{1... | collective-permute-start | bytes 405512 | tf_op jit(solution)/shard_map/ppermute | solution.py:318
  44.9 1.2 %collective-permute-done.10 = f32[264,128]{1,0:T(8,128)S(1)} collective-permute-done((f32[264,128]{1,0:T(8,128)S(1)}, f32[264,128]{1,0:T(8,128)S(1)}, u32[]{:S(2)}, u32[]{:S(2)}) %collective-permute-start.10) | collective-permute-done | bytes 135200 | tf_op jit(solution)/shard_map/ppermute | solution.py:315
  46.1 0.7 %fusion.2.refs_3_ = f32[264,128]{1,0:T(8,128)} fusion(f32[264,128]{1,0:T(8,128)S(1)} %collective-permute-done.10, f32[2,264,128]{2,1,0:T(8,128)S(1)} %collective-permute-done.9, f32[2,264,128]{2,1,0:T(8,128)S(1)} %get-tuple-element.33), kind=kLoop, calls=%fused_computation.4 | loop fusion | flops 67584 | bytes 540672 | tf_op jit(solution)/shard_map/add | solution.py:315
  46.7 0.0 collective-permute-done.3.refs_0_
  46.7 0.0 collective-permute-done.5.refs_1_
  46.7 2.2 %collective-permute-done.8.refs_2_ = f32[264,128]{1,0:T(8,128)S(1)} collective-permute-done((f32[264,128]{1,0:T(8,128)S(1)}, f32[264,128]{1,0:T(8,128)S(1)}, u32[]{:S(2)}, u32[]{:S(2)}) %collective-permute-start.8) | collective-permute-done | bytes 135200 | tf_op jit(solution)/shard_map/ppermute | solution.py:318
  48.9 0.0 copy-done
  48.9 0.7 %copy-done.2 = f32[264,128]{1,0:T(8,128)} copy-done((f32[264,128]{1,0:T(8,128)}, f32[264,128]{1,0:T(8,128)S(1)}, u32[]{:S(2)}) %copy-start.2) | copy-done | bytes 135192
  49.6 2.1 %finish.1 = f32[4,16,513]{2,1,0:T(8,128)} custom-call(f32[264,128]{1,0:T(8,128)} %copy-done, f32[264,128]{1,0:T(8,128)} %copy-done.1, f32[264,128]{1,0:T(8,128)} %copy-done.2, f32[264,128]{1,0:T(8,128)} %fusion.2.refs_3_), custom_call_target="tpu_custom_call" | custom-call | tf_op jit(solution)/shard_map/finish/pallas_call | solution.py:292
  (11 shorter events, 0.1 us)
Async XLA Ops:
  15.7 4.8 %collective-permute-start = (f32[2,264,128]{2,1,0:T(8,128)S(1)}, f32[2,264,128]{2,1,0:T(8,128)S(1)}, u32[]{:S(2)}, u32[]{:S(2)}) collective-permute-start(f32[2,264,128]{2,1,0:T(8,128)S(1)} %get-tuple-element.23), channel_id=1, source_target_pairs={{0,1},{1,0},{2,3},{3,2},{4,5},{5,4},{6,7},{7,6},{8,9},{9,8},{10,11... | collective-permute-start | bytes 811016 | tf_op jit(solution)/shard_map/ppermute | solution.py:312
  20.4 7.4 %collective-permute-start.1 = (f32[2,264,128]{2,1,0:T(8,128)S(1)}, f32[2,264,128]{2,1,0:T(8,128)S(1)}, u32[]{:S(2)}, u32[]{:S(2)}) collective-permute-start(f32[2,264,128]{2,1,0:T(8,128)S(1)} %get-tuple-element.26), channel_id=1, source_target_pairs={{0,1},{1,0},{2,3},{3,2},{4,5},{5,4},{6,7},{7,6},{8,9},{9,8},{10,11... | collective-permute-start | bytes 811016 | tf_op jit(solution)/shard_map/ppermute | solution.py:312
  20.5 7.3 %collective-permute-start.2 = (f32[264,128]{1,0:T(8,128)S(1)}, f32[264,128]{1,0:T(8,128)S(1)}, u32[]{:S(2)}, u32[]{:S(2)}) collective-permute-start(f32[264,128]{1,0:T(8,128)S(1)} %fusion.11), channel_id=1, source_target_pairs={{0,2},{1,3},{2,0},{3,1},{4,6},{5,7},{6,4},{7,5},{8,10},{9,11},{10,... | collective-permute-start | bytes 405512 | tf_op jit(solution)/shard_map/ppermute | solution.py:315
  27.7 9.6 %collective-permute-start.6 = (f32[2,264,128]{2,1,0:T(8,128)S(1)}, f32[2,264,128]{2,1,0:T(8,128)S(1)}, u32[]{:S(2)}, u32[]{:S(2)}) collective-permute-start(f32[2,264,128]{2,1,0:T(8,128)S(1)} %get-tuple-element.31), channel_id=1, source_target_pairs={{0,1},{1,0},{2,3},{3,2},{4,5},{5,4},{6,7},{7,6},{8,9},{9,8},{10,11... | collective-permute-start | bytes 811016 | tf_op jit(solution)/shard_map/ppermute | solution.py:312
  27.8 18.9 %collective-permute-start.3 = (f32[264,128]{1,0:T(8,128)S(1)}, f32[264,128]{1,0:T(8,128)S(1)}, u32[]{:S(2)}, u32[]{:S(2)}) collective-permute-start(f32[264,128]{1,0:T(8,128)S(1)} %fusion.9), channel_id=1, source_target_pairs={{0,12},{4,8},{8,4},{12,0},{1,13},{5,9},{9,5},{13,1},{2,14},{6,10},... | collective-permute-start | bytes 405512 | tf_op jit(solution)/shard_map/ppermute | solution.py:318
  31.5 5.7 %collective-permute-start.4 = (f32[264,128]{1,0:T(8,128)S(1)}, f32[264,128]{1,0:T(8,128)S(1)}, u32[]{:S(2)}, u32[]{:S(2)}) collective-permute-start(f32[264,128]{1,0:T(8,128)S(1)} %fusion.10), channel_id=1, source_target_pairs={{0,2},{1,3},{2,0},{3,1},{4,6},{5,7},{6,4},{7,5},{8,10},{9,11},{10,... | collective-permute-start | bytes 405512 | tf_op jit(solution)/shard_map/ppermute | solution.py:315
  36.9 1.6 %collective-permute-start.9 = (f32[2,264,128]{2,1,0:T(8,128)S(1)}, f32[2,264,128]{2,1,0:T(8,128)S(1)}, u32[]{:S(2)}, u32[]{:S(2)}) collective-permute-start(f32[2,264,128]{2,1,0:T(8,128)S(1)} %get-tuple-element.34), channel_id=1, source_target_pairs={{0,1},{1,0},{2,3},{3,2},{4,5},{5,4},{6,7},{7,6},{8,9},{9,8},{10,11... | collective-permute-start | bytes 811016 | tf_op jit(solution)/shard_map/ppermute | solution.py:312
  37.2 9.5 %collective-permute-start.5 = (f32[264,128]{1,0:T(8,128)S(1)}, f32[264,128]{1,0:T(8,128)S(1)}, u32[]{:S(2)}, u32[]{:S(2)}) collective-permute-start(f32[264,128]{1,0:T(8,128)S(1)} %fusion.7), channel_id=1, source_target_pairs={{0,8},{4,12},{8,0},{12,4},{1,9},{5,13},{9,1},{13,5},{2,10},{6,14},... | collective-permute-start | bytes 405512 | tf_op jit(solution)/shard_map/ppermute | solution.py:318
  37.3 6.5 %collective-permute-start.7 = (f32[264,128]{1,0:T(8,128)S(1)}, f32[264,128]{1,0:T(8,128)S(1)}, u32[]{:S(2)}, u32[]{:S(2)}) collective-permute-start(f32[264,128]{1,0:T(8,128)S(1)} %fusion.3), channel_id=1, source_target_pairs={{0,2},{1,3},{2,0},{3,1},{4,6},{5,7},{6,4},{7,5},{8,10},{9,11},{10,... | collective-permute-start | bytes 405512 | tf_op jit(solution)/shard_map/ppermute | solution.py:315
  38.5 7.5 %collective-permute-start.10 = (f32[264,128]{1,0:T(8,128)S(1)}, f32[264,128]{1,0:T(8,128)S(1)}, u32[]{:S(2)}, u32[]{:S(2)}) collective-permute-start(f32[264,128]{1,0:T(8,128)S(1)} %fusion), channel_id=1, source_target_pairs={{0,2},{1,3},{2,0},{3,1},{4,6},{5,7},{6,4},{7,5},{8,10},{9,11},{10,... | collective-permute-start | bytes 405512 | tf_op jit(solution)/shard_map/ppermute | solution.py:315
  43.8 5.1 %collective-permute-start.8 = (f32[264,128]{1,0:T(8,128)S(1)}, f32[264,128]{1,0:T(8,128)S(1)}, u32[]{:S(2)}, u32[]{:S(2)}) collective-permute-start(f32[264,128]{1,0:T(8,128)S(1)} %fusion.5), channel_id=1, source_target_pairs={{0,4},{4,0},{8,12},{12,8},{1,5},{5,1},{9,13},{13,9},{2,6},{6,2},{1... | collective-permute-start | bytes 405512 | tf_op jit(solution)/shard_map/ppermute | solution.py:318
  46.7 2.2 %copy-start = (f32[264,128]{1,0:T(8,128)}, f32[264,128]{1,0:T(8,128)S(1)}, u32[]{:S(2)}) copy-start(f32[264,128]{1,0:T(8,128)S(1)} %collective-permute-done.3.refs_0_) | copy-start | bytes 405508
  46.7 2.2 %copy-start.1 = (f32[264,128]{1,0:T(8,128)}, f32[264,128]{1,0:T(8,128)S(1)}, u32[]{:S(2)}) copy-start(f32[264,128]{1,0:T(8,128)S(1)} %collective-permute-done.5.refs_1_) | copy-start | bytes 405508
  48.9 0.7 %copy-start.2 = (f32[264,128]{1,0:T(8,128)}, f32[264,128]{1,0:T(8,128)S(1)}, u32[]{:S(2)}) copy-start(f32[264,128]{1,0:T(8,128)S(1)} %collective-permute-done.8.refs_2_) | copy-start | bytes 405508
